TPU v7x, 256 devices: a whole 4x4x8 slice. The times are simulated.
256 devices in a mesh: row: 32 (over y_lo, z, core), col: 8 (over y_hi, x).
Axes of the slice: x: 4, y: 4 (y_hi: 2, y_lo: 2; y = y_hi * 2 + y_lo), z: 8, core: 2. Of those that a mesh axis runs over, the one named last changes fastest.
Arguments:
- coefficients: float32 [1024, 64], P(('row', 'col')), may hold values from -3 to 3
- off_x: int32 [1024], P(('row', 'col')), may hold values from 0 to 31
- off_y: int32 [1024], P(('row', 'col')), may hold values from 0 to 31
- off_z: int32 [1024], P(('row', 'col')), may hold values from 0 to 127
- external: float32 [1024, 256, 128], P('row', 'col'), may hold values from -6 to 6
- pattern: int32 [128, 128], replicated, may hold values from 0 to 1, as said below
- hamiltonian: bfloat16 [8192, 8192], P('row', 'col'), may hold values from -0.125 to 0.125
- density_matrix: bfloat16 [8192, 8192], P('row', 'col'), may hold values from -6 to 6
Outputs:
- density: float32 [1024, 256, 128], P('row', 'col')
- integrals: float32 [1024, 64], P(('row', 'col'))
- product: float32 [8192, 8192], P('row', 'col')
Inputs may be any that keep to these rules, and one draw needn't show every extreme that they name: `pattern`: each tile of 4 x 16 blocks that one device holds (block rows of one index of row, block columns of one index of col) has at most 24 ones, and some tile has exactly 24.
All inputs are finite; a program needn't handle non-finite values.
Results may differ from a plain program's by a relative error of at most 0.00045.
Values may be sent and summed in bfloat16 or wider, within the bound.
No kernel may reach another device: no remote copies, remote signals or barrier semaphores. Data moves between devices by JAX's collectives and lax.ppermute only.
A program may use at most 128 MiB of HBM per device.

v0:
```python
import jax
import jax.numpy as jnp
from jax import lax
from jax.sharding import PartitionSpec as P

BS = 64
BASIS = 8
NCOMP = 64
CUBE = 32


PRECISE = lax.Precision.HIGHEST


def extended_2(value, sides, width):
    for axis, dim in sides:
        size, length = (lax.axis_size(axis), value.shape[dim])
        up = [(i, (i + 1) % size) for i in range(size)]
        down = [(j, i) for i, j in up]
        last = lax.slice_in_dim(value, length - width, length, axis=dim)
        first = lax.slice_in_dim(value, 0, width, axis=dim)
        before = lax.ppermute(last, axis, up)
        after = lax.ppermute(first, axis, down)
        value = jnp.concatenate([before, value, after], axis=dim)
    return value


def hermite(distance):
    scaled = (distance.astype(jnp.float32) + 0.5 - CUBE / 2.0) * (6.0 / CUBE)
    gaussian = jnp.exp(-0.5 * scaled * scaled)
    return jnp.stack(
        [
            gaussian,
            scaled * gaussian,
            scaled * scaled * gaussian,
            scaled * scaled * scaled * gaussian,
        ],
        axis=1,
    )


def factor(distance):
    inside = (distance >= 0) & (distance < CUBE)
    values = hermite(jnp.clip(distance, 0, CUBE - 1))
    return jnp.where(inside[:, None, :], values, 0.0)


def frames(start_x, start_y, start_z, cells_x, cells_y, cells_z):
    index_x = jnp.arange(cells_x, dtype=jnp.int32)
    index_y = jnp.arange(cells_y, dtype=jnp.int32)
    index_z = jnp.arange(cells_z, dtype=jnp.int32)
    factor_x = factor(index_x[None, :] - start_x[:, None])
    factor_y = factor(index_y[None, :] - start_y[:, None])
    factor_z = factor(jnp.mod(index_z[None, :] - start_z[:, None] + CUBE // 2, cells_z))
    return (factor_x, factor_y, factor_z)


def collocate(coef_rows, factor_x, factor_y, factor_z):
    coef_cube = coef_rows.reshape(-1, 4, 4, 4)
    section_one = jnp.einsum("aijk,aie->ajke", coef_cube, factor_x, precision=PRECISE)
    section_two = jnp.einsum("ajke,ajf->akef", section_one, factor_y, precision=PRECISE)
    return jnp.einsum("akef,akz->efz", section_two, factor_z, precision=PRECISE)


def integrate(field, factor_x, factor_y, factor_z):
    section_one = jnp.einsum("efz,akz->akef", field, factor_z, precision=PRECISE)
    section_two = jnp.einsum("akef,ajf->ajke", section_one, factor_y, precision=PRECISE)
    result = jnp.einsum("ajke,aie->aijk", section_two, factor_x, precision=PRECISE)
    return result.reshape(-1, NCOMP) * (6.0 / CUBE) ** 3


def fold_rim(extended, axis, length):
    half_cube = CUBE // 2
    core_part = lax.slice_in_dim(extended, 2 * half_cube, 2 * half_cube + length, axis=axis)
    below = lax.slice_in_dim(extended, 0, half_cube, axis=axis)
    above = lax.slice_in_dim(extended, length + 3 * half_cube, length + 4 * half_cube, axis=axis)
    widths_low = [(0, 0)] * 3
    widths_low[axis] = (0, length - half_cube)
    widths_high = [(0, 0)] * 3
    widths_high[axis] = (length - half_cube, 0)
    return core_part + jnp.pad(below, widths_low) + jnp.pad(above, widths_high)


def apply_mask(matrix, own_tile):
    tile_rows, tile_cols = matrix.shape
    shaped = matrix.reshape(tile_rows // BS, BS, tile_cols // BS, BS)
    return (shaped * own_tile.astype(matrix.dtype)[:, None, :, None]).reshape(tile_rows, tile_cols)


def on_device(coefficients, off_x, off_y, off_z, external, pattern, hamiltonian, density_matrix):
    wide_x, wide_y, z_cells = external.shape
    half_cube = CUBE // 2
    factor_x, factor_y, factor_z = frames(
        off_x, off_y, off_z, wide_x + CUBE, wide_y + CUBE, z_cells
    )
    spread = collocate(coefficients, factor_x, factor_y, factor_z)
    extended = extended_2(spread, (("row", 0), ("col", 1)), half_cube)
    density = fold_rim(fold_rim(extended, 0, wide_x), 1, wide_y)
    potential = external + jnp.tanh(density)
    framed = extended_2(potential.astype(jnp.bfloat16), (("row", 0), ("col", 1)), half_cube).astype(
        potential.dtype
    )
    integrals = integrate(framed, factor_x, factor_y, factor_z)
    row_id = lax.axis_index("row")
    col_id = lax.axis_index("col")
    tile_rows, tile_cols = hamiltonian.shape
    block_rows = tile_rows // BS
    block_cols = tile_cols // BS
    own_tile = lax.dynamic_slice(
        pattern, (row_id * block_rows, col_id * block_cols), (block_rows, block_cols)
    )
    h_masked = apply_mask(hamiltonian, own_tile)
    p_masked = apply_mask(density_matrix, own_tile)
    row_panel = lax.all_gather(h_masked, "col", axis=1, tiled=True)
    diagonal = lax.all_gather(integrals, "col", axis=0, tiled=True)
    product = jnp.dot(
        row_panel,
        lax.all_gather(p_masked, "row", axis=0, tiled=True),
        preferred_element_type=jnp.float32,
    )
    local_term = jnp.einsum(
        "anm,amj->anj",
        diagonal.reshape(-1, BASIS, BASIS),
        p_masked.astype(jnp.float32).reshape(-1, BASIS, tile_cols),
        precision=PRECISE,
    )
    product = product + local_term.reshape(tile_rows, tile_cols)
    return (density, integrals, product)


def solution(mesh):
    return jax.shard_map(
        on_device,
        mesh=mesh,
        in_specs=(
            P(("row", "col"), None),
            P(("row", "col")),
            P(("row", "col")),
            P(("row", "col")),
            P("row", "col", None),
            P(),
            P("row", "col"),
            P("row", "col"),
        ),
        out_specs=(P("row", "col", None), P(("row", "col"), None), P("row", "col")),
        check_vma=False,
    )
```

profile of v0, /device:TPU:1, one launch (start us, length us, event | category | flops | bytes accessed | tf_op | source)
XLA Modules:
  0.0 232.0 jit_solution(9263994134841237533)
XLA Ops:
  7.2 0.0 all-gather.4.cloned.1.call-start
  7.2 0.8 dynamic-slice_convert_fusion
  8.1 0.2 mul.445
  8.3 0.7 mul.446
  9.0 0.0 copy-done
  9.0 0.0 copy-done.1
  9.0 0.0 copy-start.3
  9.0 0.0 copy-start.5
  9.0 0.0 copy-start.6
  9.1 0.0 copy-start.7
  9.1 1.1 fusion.59
  10.2 0.0 all-gather.4.cloned.1.call-update
  10.2 0.0 all-gather.6.cloned.1.call-start
  10.2 0.7 all-gather.6.cloned.1.call-update
  10.9 0.1 reshape.475
  11.1 0.2 copy.21
  11.3 0.0 copy-done.5
  11.3 0.1 fusion.49
  11.3 0.1 fusion.50
  11.4 0.0 copy-done.7
  11.4 0.1 compare_and_fusion
  11.5 0.1 multiply_exponential_fusion.2
  11.6 0.1 multiply_exponential_fusion.1
  11.7 0.1 multiply_exponential_fusion
  11.8 0.2 fusion.29
  12.0 1.0 fusion.23
  13.0 3.5 %convolution_bitcast_fusion = f32[64,64,128]{2,1,0:T(8,128)S(1)} fusion(f32[4,4,64,64]{3,2,1,0:T(8,128)S(1)} %fusion.23, f32[4,1,128]{2,1,0:T(1,128)S(1)} %get-tuple-element.17, f32[4,1,128]{2,1,0:T(1,128)S(1)} %get-tuple-element.16, f32[4,1,128]{2,1,0:T(1,128)S(1)} %get-tuple-element.18, f32[4,1,128]{2,1,0:T(1,128)S(1)} %get-tuple-element.15, ...), kind=kOutput, calls=%fused_computation.1 | convolution fusion | flops 100671488 | bytes 2368000 | tf_op jit(solution)/shard_map/akef,akz->efz/dot_general | solution.py:62
  16.5 0.1 fusion.58
  16.6 3.3 %collective-permute-start.1 = (f32[16,64,128]{2,1,0:T(8,128)S(1)}, f32[16,64,128]{2,1,0:T(8,128)S(1)}, u32[]{:S(2)}, u32[]{:S(2)}) collective-permute-start(f32[16,64,128]{2,1,0:T(8,128)S(1)} %get-tuple-element.8), channel_id=1, source_target_pairs={{8,0},{16,8},{24,16},{32,24},{40,32},{48,40},{56,48},{64,56},{72,6... | collective-permute-start | bytes 1572872 | tf_op jit(solution)/shard_map/ppermute | solution.py:23
  19.9 0.0 collective-permute-start
  19.9 6.6 %collective-permute-done.1 = f32[16,64,128]{2,1,0:T(8,128)S(1)} collective-permute-done((f32[16,64,128]{2,1,0:T(8,128)S(1)}, f32[16,64,128]{2,1,0:T(8,128)S(1)}, u32[]{:S(2)}, u32[]{:S(2)}) %collective-permute-start.1) | collective-permute-done | bytes 524320 | tf_op jit(solution)/shard_map/ppermute | solution.py:23
  26.6 0.0 collective-permute-done
  26.6 0.1 pad_maximum_fusion.3
  26.7 5.2 %collective-permute-start.3 = (f32[96,16,128]{2,1,0:T(8,128)S(1)}, f32[96,16,128]{2,1,0:T(8,128)S(1)}, u32[]{:S(2)}, u32[]{:S(2)}) collective-permute-start(f32[96,16,128]{2,1,0:T(8,128)S(1)} %get-tuple-element.6), channel_id=1, source_target_pairs={{1,0},{2,1},{3,2},{4,3},{5,4},{6,5},{7,6},{0,7},{9,8},{10,9},{11,1... | collective-permute-start | bytes 2359304 | tf_op jit(solution)/shard_map/ppermute | solution.py:23
  31.9 0.0 collective-permute-start.2
  31.9 15.6 %collective-permute-done.3 = f32[96,16,128]{2,1,0:T(8,128)S(1)} collective-permute-done((f32[96,16,128]{2,1,0:T(8,128)S(1)}, f32[96,16,128]{2,1,0:T(8,128)S(1)}, u32[]{:S(2)}, u32[]{:S(2)}) %collective-permute-start.3) | collective-permute-done | bytes 786464 | tf_op jit(solution)/shard_map/ppermute | solution.py:23
  47.5 0.0 collective-permute-done.2
  47.5 1.7 pad_maximum_fusion
  49.2 0.0 copy-start.2
  49.3 0.3 fusion
  49.6 0.7 copy-done.2
  50.3 1.0 add_convert_fusion
  51.3 12.1 %collective-permute-start.5 = (bf16[16,32,128]{2,1,0:T(8,128)(2,1)S(1)}, bf16[16,32,128]{2,1,0:T(8,128)(2,1)S(1)}, u32[]{:S(2)}, u32[]{:S(2)}) collective-permute-start(bf16[16,32,128]{2,1,0:T(8,128)(2,1)S(1)} %get-tuple-element.14), channel_id=1, source_target_pairs={{8,0},{16,8},{24,16},{32,24},{40,32},{48,40},{56,48},{64,56},{72,6... | collective-permute-start | bytes 393224 | tf_op jit(solution)/shard_map/ppermute | solution.py:23
  63.4 2.2 collective-permute-start.4
  65.6 2.4 %collective-permute-done.5 = bf16[16,32,128]{2,1,0:T(8,128)(2,1)S(1)} collective-permute-done((bf16[16,32,128]{2,1,0:T(8,128)(2,1)S(1)}, bf16[16,32,128]{2,1,0:T(8,128)(2,1)S(1)}, u32[]{:S(2)}, u32[]{:S(2)}) %collective-permute-start.5) | collective-permute-done | bytes 131104 | tf_op jit(solution)/shard_map/ppermute | solution.py:23
  68.0 2.3 collective-permute-done.4
  70.3 0.1 pad_maximum_fusion.4
  70.4 1.5 collective-permute-start.7
  71.9 0.0 collective-permute-start.6
  71.9 0.1 mul.449
  72.0 0.1 mul.450
  72.2 9.1 %collective-permute-done.7 = bf16[64,16,128]{2,1,0:T(8,128)(2,1)S(1)} collective-permute-done((bf16[64,16,128]{2,1,0:T(8,128)(2,1)S(1)}, bf16[64,16,128]{2,1,0:T(8,128)(2,1)S(1)}, u32[]{:S(2)}, u32[]{:S(2)}) %collective-permute-start.7) | collective-permute-done | bytes 262176 | tf_op jit(solution)/shard_map/ppermute | solution.py:23
  81.3 2.6 %collective-permute-done.6 = bf16[64,16,128]{2,1,0:T(8,128)(2,1)S(1)} collective-permute-done((bf16[64,16,128]{2,1,0:T(8,128)(2,1)S(1)}, bf16[64,16,128]{2,1,0:T(8,128)(2,1)S(1)}, u32[]{:S(2)}, u32[]{:S(2)}) %collective-permute-start.6) | collective-permute-done | bytes 262176 | tf_op jit(solution)/shard_map/ppermute | solution.py:22
  83.9 2.5 %fusion.7 = f32[4,4,64,64]{3,1,2,0:T(4,128)S(1)} fusion(bf16[64,16,128]{2,1,0:T(8,128)(2,1)S(1)} %collective-permute-done.7, bf16[16,32,128]{2,1,0:T(8,128)(2,1)S(1)} %collective-permute-done.5, bf16[32,32,128]{2,1,0:T(8,128)(2,1)S(1)} %get-tuple-element.3, bf16[16,32,128]{2,1,0:T(8,128)(2,1)S(1)} %collective-permute-done.4, ...), kind=kOutput, calls=%fused_computation.17 | convolution fusion | flops 105914368 | bytes 1319424 | tf_op jit(solution)/shard_map/efz,akz->akef/dot_general | solution.py:66
  86.4 1.3 fusion.18
  87.8 1.0 convolution_multiply_fusion
  88.8 0.7 mul.442
  89.5 0.1 reshape.479
  89.6 25.9 %all-gather = f32[8,4,64]{2,1,0:T(4,128)S(1)} all-gather(f32[1,4,64]{2,1,0:T(4,128)S(1)} %reshape.479), channel_id=1, replica_groups=mesh['row'=32,'col'=8] {'col'}, dimensions={0}, use_global_device_ids=true | all-gather | bytes 9216 | tf_op jit(solution)/shard_map/all_gather | solution.py:115
  115.5 0.1 reshape.476
  115.6 0.6 convolution_bitcast_fusion.1
  116.2 0.0 all-gather.4.cloned.1.call-done
  116.2 96.4 %all-gather.6.cloned.1.call-done = bf16[8192,1024]{1,0:T(8,128)(2,1)} async-done(((bf16[256,1024]{1,0:T(8,128)(2,1)}), bf16[8192,1024]{1,0:T(8,128)(2,1)}) %all-gather.6.cloned.1.call-update) | async-done | bytes 16777232 | tf_op jit(solution)/shard_map/all_gather | solution.py:118
  212.6 12.5 %convolution_add_fusion = f32[256,1024]{1,0:T(8,128)} fusion(f32[256,1024]{1,0:T(8,128)S(1)} %convolution_bitcast_fusion.1, bf16[256,8192]{1,0:T(8,128)(2,1)} %all-gather.4.cloned.1.call-done, bf16[8192,1024]{1,0:T(8,128)(2,1)} %all-gather.6.cloned.1.call-done), kind=kOutput, calls=%fused_computation.13 | convolution fusion | flops 4295229440 | bytes 23068672 | tf_op jit(solution)/shard_map/dot_general | solution.py:116
  (13 shorter events, 0.1 us)
Async XLA Ops:
  7.2 1.8 copy-start
  7.2 1.8 copy-start.1
  7.2 109.0 %all-gather.4.cloned.1.call-start = ((), (), s32[]{:S(2)}) async-start(), calls=%async_computation | async-start | bytes 4718592 | tf_op jit(solution)/shard_map/all_gather | solution.py:114
  9.0 1.9 copy-start.3
  9.0 2.2 copy-start.5
  9.0 2.3 copy-start.6
  9.1 2.4 %copy-start.7 = (s32[4]{0:T(128)S(1)}, s32[4]{0:T(128)}, u32[]{:S(2)}) copy-start(s32[4]{0:T(128)} %param.11) | copy-start | bytes 52
  10.2 202.4 %all-gather.6.cloned.1.call-start = ((), (), s32[]{:S(2)}) async-start(), calls=%async_computation.1 | async-start | bytes 17301504 | tf_op jit(solution)/shard_map/all_gather | solution.py:118
  16.6 10.0 %collective-permute-start.1 = (f32[16,64,128]{2,1,0:T(8,128)S(1)}, f32[16,64,128]{2,1,0:T(8,128)S(1)}, u32[]{:S(2)}, u32[]{:S(2)}) collective-permute-start(f32[16,64,128]{2,1,0:T(8,128)S(1)} %get-tuple-element.8), channel_id=1, source_target_pairs={{8,0},{16,8},{24,16},{32,24},{40,32},{48,40},{56,48},{64,56},{72,6... | collective-permute-start | bytes 1572872 | tf_op jit(solution)/shard_map/ppermute | solution.py:23
  19.9 6.7 %collective-permute-start = (f32[16,64,128]{2,1,0:T(8,128)S(1)}, f32[16,64,128]{2,1,0:T(8,128)S(1)}, u32[]{:S(2)}, u32[]{:S(2)}) collective-permute-start(f32[16,64,128]{2,1,0:T(8,128)S(1)} %get-tuple-element.7), channel_id=1, source_target_pairs={{0,8},{8,16},{16,24},{24,32},{32,40},{40,48},{48,56},{56,64},{64,7... | collective-permute-start | bytes 1572872 | tf_op jit(solution)/shard_map/ppermute | solution.py:22
  26.7 20.8 %collective-permute-start.3 = (f32[96,16,128]{2,1,0:T(8,128)S(1)}, f32[96,16,128]{2,1,0:T(8,128)S(1)}, u32[]{:S(2)}, u32[]{:S(2)}) collective-permute-start(f32[96,16,128]{2,1,0:T(8,128)S(1)} %get-tuple-element.6), channel_id=1, source_target_pairs={{1,0},{2,1},{3,2},{4,3},{5,4},{6,5},{7,6},{0,7},{9,8},{10,9},{11,1... | collective-permute-start | bytes 2359304 | tf_op jit(solution)/shard_map/ppermute | solution.py:23
  31.9 17.3 %copy-start.4 = (pred[32]{0:T(512)(128)(4,1)S(1)}, pred[32]{0:T(512)(128)(4,1)}, u32[]{:S(2)}) copy-start(pred[32]{0:T(512)(128)(4,1)} %constant.59.clone.1) | copy-start | bytes 100
  31.9 15.6 %collective-permute-start.2 = (f32[96,16,128]{2,1,0:T(8,128)S(1)}, f32[96,16,128]{2,1,0:T(8,128)S(1)}, u32[]{:S(2)}, u32[]{:S(2)}) collective-permute-start(f32[96,16,128]{2,1,0:T(8,128)S(1)} %get-tuple-element.5), channel_id=1, source_target_pairs={{0,1},{1,2},{2,3},{3,4},{4,5},{5,6},{6,7},{7,0},{8,9},{9,10},{10,1... | collective-permute-start | bytes 2359304 | tf_op jit(solution)/shard_map/ppermute | solution.py:22
  49.2 1.0 copy-start.2
  51.3 16.6 %collective-permute-start.5 = (bf16[16,32,128]{2,1,0:T(8,128)(2,1)S(1)}, bf16[16,32,128]{2,1,0:T(8,128)(2,1)S(1)}, u32[]{:S(2)}, u32[]{:S(2)}) collective-permute-start(bf16[16,32,128]{2,1,0:T(8,128)(2,1)S(1)} %get-tuple-element.14), channel_id=1, source_target_pairs={{8,0},{16,8},{24,16},{32,24},{40,32},{48,40},{56,48},{64,56},{72,6... | collective-permute-start | bytes 393224 | tf_op jit(solution)/shard_map/ppermute | solution.py:23
  63.4 6.9 %collective-permute-start.4 = (bf16[16,32,128]{2,1,0:T(8,128)(2,1)S(1)}, bf16[16,32,128]{2,1,0:T(8,128)(2,1)S(1)}, u32[]{:S(2)}, u32[]{:S(2)}) collective-permute-start(bf16[16,32,128]{2,1,0:T(8,128)(2,1)S(1)} %get-tuple-element.13), channel_id=1, source_target_pairs={{0,8},{8,16},{16,24},{24,32},{32,40},{40,48},{48,56},{56,64},{64,7... | collective-permute-start | bytes 393224 | tf_op jit(solution)/shard_map/ppermute | solution.py:22
  70.4 10.9 %collective-permute-start.7 = (bf16[64,16,128]{2,1,0:T(8,128)(2,1)S(1)}, bf16[64,16,128]{2,1,0:T(8,128)(2,1)S(1)}, u32[]{:S(2)}, u32[]{:S(2)}) collective-permute-start(bf16[64,16,128]{2,1,0:T(8,128)(2,1)S(1)} %get-tuple-element.12), channel_id=1, source_target_pairs={{1,0},{2,1},{3,2},{4,3},{5,4},{6,5},{7,6},{0,7},{9,8},{10,9},{11,1... | collective-permute-start | bytes 786440 | tf_op jit(solution)/shard_map/ppermute | solution.py:23
  71.9 12.0 %collective-permute-start.6 = (bf16[64,16,128]{2,1,0:T(8,128)(2,1)S(1)}, bf16[64,16,128]{2,1,0:T(8,128)(2,1)S(1)}, u32[]{:S(2)}, u32[]{:S(2)}) collective-permute-start(bf16[64,16,128]{2,1,0:T(8,128)(2,1)S(1)} %get-tuple-element.11), channel_id=1, source_target_pairs={{0,1},{1,2},{2,3},{3,4},{4,5},{5,6},{6,7},{7,0},{8,9},{9,10},{10,1... | collective-permute-start | bytes 786440 | tf_op jit(solution)/shard_map/ppermute | solution.py:22
Sparse Core Ops, SparseCore 0:
  10.7 102.9 all-gather.3
  116.1 96.4 all-gather.5
where the time goes:
time: 232 us
  waiting for transfers between devices  136 us (59%)
  blocking collectives  25.9 us (11%)
  starting transfers between devices  24.4 us (11%)
  matrix products  22.6 us (10%)
  between operations  14.3 us (6%)
  other arithmetic  5.64 us (2%)
  local copies, waits for them, and re-layouts  3.28 us (1%)
    all_gather x1, waiting for transfers between devices, on_device(): lax.all_gather(p_masked, 'row', axis=0, tiled=True)  96.4 us
    ppermute x4, waiting for transfers between devices, extended_2(): after = lax.ppermute(first, axis, down)  33.8 us
    all_gather x1, blocking collectives, on_device(): diagonal = lax.all_gather(integrals, 'col', axis=0, tiled=True)  25.9 us
    ppermute x4, starting transfers between devices, extended_2(): after = lax.ppermute(first, axis, down)  22.1 us
    dot_general x1, matrix products, on_device(): jnp.dot(row_panel, lax.all_gather(p_masked, 'row', axis=0, tiled=True), p...  12.5 us
    ppermute x4, waiting for transfers between devices, extended_2(): before = lax.ppermute(last, axis, up)  4.91 us
  transfers between devices with their start and end apart: 10, of which 7 were waited for; matrix products, arithmetic and copies ran while one was open for 7% of the time, Pallas kernels for 0%

commit v1 on v0

v1 whole, which is shorter than its diff:
```python
import functools

import jax
import jax.numpy as jnp
from jax import lax
from jax.experimental import pallas as pl
from jax.experimental.pallas import tpu as pltpu
from jax.sharding import PartitionSpec as P

BS = 64
CUBE = 32
SLOTS = 24
PACK = SLOTS // 2 * BS
F32 = jnp.float32
BF16 = jnp.bfloat16
PRECISE = lax.Precision.HIGHEST
SCALE = 6.0 / CUBE


def swap_halves(block):
    return jnp.concatenate([block[:, BS:], block[:, :BS]], axis=1)


def pack_kernel(pattern_ref, h_ref, p_ref, hp_ref, pp_ref, rows, places, sem):
    row, col = lax.axis_index("row"), lax.axis_index("col")
    copy = pltpu.make_async_copy(
        pattern_ref.at[pl.ds(pl.multiple_of(row // 2 * 8, 8), 8), :], rows, sem
    )
    copy.start()
    copy.wait()
    places[SLOTS] = 0

    def clear(i, _):
        places[i] = 0
        return 0

    lax.fori_loop(0, SLOTS, clear, 0)

    def scan(block, count):
        places[count] = block
        flag = rows[row % 2 * 4 + block // 16, col * 16 + block % 16]
        return count + jnp.where(flag != 0, 1, 0)

    lax.fori_loop(0, 64, scan, 0)
    left = lax.broadcasted_iota(jnp.int32, (BS, 2 * BS), 1) < BS
    for source, target in ((p_ref, pp_ref), (h_ref, hp_ref)):
        for pair in range(SLOTS // 2):
            halves = []
            for half in range(2):
                place = places[2 * pair + half]
                r, c = place // 16, place % 16
                block = source[
                    pl.ds(pl.multiple_of(r * BS, BS), BS),
                    pl.ds(pl.multiple_of(c // 2 * 128, 128), 128),
                ]
                halves.append(jnp.where(c % 2 == half, block, swap_halves(block)))
            target[pl.ds(pair * BS, BS), :] = jnp.where(left, halves[0], halves[1])


def pack(pattern, hamiltonian, density_matrix):
    packed = jax.ShapeDtypeStruct((PACK, 128), BF16)
    vmem = pl.BlockSpec(memory_space=pltpu.VMEM)
    return pl.pallas_call(
        pack_kernel,
        out_shape=(packed, packed),
        in_specs=[pl.BlockSpec(memory_space=pl.ANY), vmem, vmem],
        out_specs=(vmem, vmem),
        scratch_shapes=[
            pltpu.SMEM((8, 128), jnp.int32),
            pltpu.SMEM((SLOTS + 8,), jnp.int32),
            pltpu.SemaphoreType.DMA,
        ],
        compiler_params=pltpu.CompilerParams(vmem_limit_bytes=8 * 2**20),
        cost_estimate=pl.CostEstimate(flops=0, bytes_accessed=4 * 2**20, transcendentals=0),
    )(pattern, hamiltonian, density_matrix)


def block_offsets(tiles):
    flags = (tiles != 0).astype(F32)
    earlier = (
        lax.broadcasted_iota(jnp.int32, (64, 64), 0) < lax.broadcasted_iota(jnp.int32, (64, 64), 1)
    ).astype(F32)
    slot = jnp.dot(flags, earlier, precision=PRECISE).astype(jnp.int32)
    parity = lax.broadcasted_iota(jnp.int32, slot.shape, 1) % 2
    at = slot // 2 * BS + jnp.where(slot % 2 == parity, 0, PACK)
    return jnp.where(flags > 0, at, 2 * PACK)


def tile_tables(pattern):
    row, col = lax.axis_index("row"), lax.axis_index("col")
    mine = lax.dynamic_slice(pattern, (0, col * 16), (128, 16)).reshape(32, 64)
    across = lax.dynamic_slice(pattern, (row * 4, 0), (4, 128))
    across = across.reshape(4, 8, 16).transpose(1, 0, 2).reshape(8, 64)
    table = block_offsets(jnp.concatenate([mine, across], axis=0))
    return table[:32], table[32:]


def spread_tile(packed, table_ref, tile, both, store):
    both[0:PACK, :] = packed
    both[PACK : 2 * PACK, :] = swap_halves(packed)
    left = lax.broadcasted_iota(jnp.int32, (BS, 2 * BS), 1) < BS
    for r in range(4):
        for c in range(8):
            at0 = pl.multiple_of(table_ref[tile, r * 16 + 2 * c], BS)
            at1 = pl.multiple_of(table_ref[tile, r * 16 + 2 * c + 1], BS)
            block = jnp.where(left, both[pl.ds(at0, BS), :], both[pl.ds(at1, BS), :])
            store(r, c, block)


def spread_kernel(order, count, table_ref, *refs):
    parts, out_ref, both = refs[:count], refs[count], refs[count + 1]
    col = lax.axis_index("col")
    y, x = col // 4, col % 4
    both[2 * PACK :, :] = jnp.zeros((BS, 128), BF16)
    for part, dx in order:

        def one(j, _, part=part, dx=dx):
            if callable(dx):
                turn = dx(lax.axis_index("row") % 2)
            else:
                turn = dx
            source = (y + j) % 2 * 4 + (x + turn) % 4
            packed = parts[part][pl.ds(pl.multiple_of(j * PACK, PACK), PACK), :]

            def store(r, c, block):
                out_ref[
                    source * 4 + c // 2, r * BS : (r + 1) * BS, c % 2 * 128 : c % 2 * 128 + 128
                ] = block

            spread_tile(packed, table_ref, source, both, store)
            return 0

        lax.fori_loop(0, 2, one, 0)


def spread_hamiltonian(table, parts, order):
    vmem = pl.BlockSpec(memory_space=pltpu.VMEM)
    return pl.pallas_call(
        functools.partial(spread_kernel, order, len(parts)),
        out_shape=jax.ShapeDtypeStruct((32, 256, 256), BF16),
        in_specs=[pl.BlockSpec(memory_space=pltpu.SMEM)] + [vmem] * len(parts),
        out_specs=vmem,
        scratch_shapes=[pltpu.VMEM((2 * PACK + BS, 128), BF16)],
        compiler_params=pltpu.CompilerParams(vmem_limit_bytes=16 * 2**20),
        cost_estimate=pl.CostEstimate(flops=0, bytes_accessed=12 * 2**20, transcendentals=0),
    )(table, *parts)


def split3(value):
    high = value.astype(BF16)
    rest = value - high.astype(F32)
    middle = rest.astype(BF16)
    return high, middle, (rest - middle.astype(F32)).astype(BF16)


def accumulate_kernel(groups, start, local, table_ref, h_ref, *refs):
    refs = list(refs)
    before = None if start else refs.pop(0)
    atoms = refs.pop(0) if local else None
    parts = [refs.pop(0) for _ in groups]
    out_ref, both, dense, wide = refs
    row = lax.axis_index("row")
    y, z, core = row // 16, row // 2 % 8, row % 2
    direction = 1 - 2 * core
    both[2 * PACK :, :] = jnp.zeros((BS, 128), BF16)
    first = True
    for at in range(0, len(groups), 2):
        pair = groups[at : at + 2]
        for g, (steps, flip) in enumerate(pair):
            part = parts[at + g]

            def one(j, _, part=part, steps=steps, flip=flip, g=g):
                tile = ((y + j) % 2 * 8 + (z + steps * direction + 8) % 8) * 2 + (core + flip) % 2
                packed = part[pl.ds(pl.multiple_of(j * PACK, PACK), PACK), :]
                base = pl.multiple_of((2 * g + j) * 256, 256)

                def store(r, c, block):
                    dense[pl.ds(base + r * BS, BS), c * 128 : c * 128 + 128] = block

                spread_tile(packed, table_ref, tile, both, store)
                wide[:, pl.ds(base, 256)] = h_ref[tile]
                return 0

            lax.fori_loop(0, 2, one, 0)
        depth = len(pair) * 512
        if local and at == 0:
            values = atoms[...]
            lane_atom = lax.broadcasted_iota(jnp.int32, (256, 128), 1) // 4
            row_atom = lax.broadcasted_iota(jnp.int32, (256, 128), 0) // 8
            tall = [
                jnp.where(
                    lane_atom == row_atom,
                    jnp.concatenate([values[8 * b : 8 * b + 8, :]] * 32, axis=0),
                    0.0,
                )
                for b in range(2)
            ]
            q = lax.broadcasted_iota(jnp.int32, (256, 256), 0)
            m = lax.broadcasted_iota(jnp.int32, (256, 256), 1)
            place = q % 128 // 4 * 8 + q // 128 * 4 + q % 4
            chosen = jnp.where(place == m, 1.0, 0.0).astype(BF16)
            terms = [
                jnp.dot(t, chosen, preferred_element_type=F32).astype(BF16)
                for t in split3(jnp.concatenate(tall, axis=1))
            ]
        for n in range(4):
            lanes = slice(n * 256, n * 256 + 256)
            total = jnp.dot(
                wide[:, :depth], dense[:depth, lanes], preferred_element_type=F32
            )
            if local and at == 0:
                for term in terms:
                    total += jnp.dot(term, dense[0:256, lanes], preferred_element_type=F32)
            if first:
                if before is not None:
                    total += before[:, lanes]
                out_ref[:, lanes] = total
            else:
                out_ref[:, lanes] += total
        first = False


def accumulate(table, h_dense, before, parts, groups, atoms=None):
    vmem = pl.BlockSpec(memory_space=pltpu.VMEM)
    operands = [table, h_dense]
    if before is not None:
        operands.append(before)
    if atoms is not None:
        operands.append(atoms)
    operands += parts
    depth = 512 * min(2, len(groups))
    return pl.pallas_call(
        functools.partial(accumulate_kernel, groups, before is None, atoms is not None),
        out_shape=jax.ShapeDtypeStruct((256, 1024), F32),
        in_specs=[pl.BlockSpec(memory_space=pltpu.SMEM)] + [vmem] * (len(operands) - 1),
        out_specs=vmem,
        scratch_shapes=[
            pltpu.VMEM((2 * PACK + BS, 128), BF16),
            pltpu.VMEM((depth, 1024), BF16),
            pltpu.VMEM((256, depth), BF16),
        ],
        compiler_params=pltpu.CompilerParams(vmem_limit_bytes=24 * 2**20),
        cost_estimate=pl.CostEstimate(
            flops=2 * 256 * 512 * 1024 * len(groups), bytes_accessed=8 * 2**20, transcendentals=0
        ),
    )(*operands)


def hermite(distance):
    scaled = (distance + (0.5 - CUBE / 2.0)) * SCALE
    inside = (distance >= 0) & (distance < CUBE)
    gaussian = jnp.where(inside, jnp.exp(-0.5 * scaled * scaled), 0.0)
    return gaussian, scaled


def powers(distance):
    gaussian, scaled = hermite(distance)
    first = scaled * gaussian
    second = scaled * first
    return gaussian, first, second, scaled * second


ROWS = [(a, 2 * bh + bl) for bl in range(2) for a in range(4) for bh in range(2)]


def grid_kernel(info_ref, external_ref, density_ref, share_ref, gx_ref, gy_ref, gz_ref, u_ref, s_ref):
    lanes = 256
    cell = lax.broadcasted_iota(jnp.int32, (CUBE, lanes), 0).astype(F32)
    off_x, off_y, off_z = (info_ref[16 + k : 17 + k, :] for k in range(3))
    for n, value in enumerate(powers(cell - off_x + CUBE // 2)):
        gx_ref[n] = value
    for n, value in enumerate(powers(cell - off_y + CUBE // 2)):
        gy_ref[n] = value
    deep = lax.broadcasted_iota(jnp.int32, (128, lanes), 0).astype(F32)
    away = deep - off_z + CUBE // 2
    away = jnp.where(away < 0, away + 128.0, away)
    away = jnp.where(away >= 128, away - 128.0, away)
    kinds = powers(away)
    e = lax.broadcasted_iota(jnp.int32, (128, lanes), 1) % 4
    gz_ref[...] = jnp.where(e == 0, kinds[0], jnp.where(e == 1, kinds[1], jnp.where(e == 2, kinds[2], kinds[3])))
    for b in range(4):
        total = None
        for a in range(4):
            at = ROWS.index((a, b))
            term = info_ref[at : at + 1, :] * gx_ref[a]
            total = term if total is None else total + term
        u_ref[b] = total
    s_ref[...] = jnp.zeros_like(s_ref)
    gz = gz_ref[...]
    chunk = 8

    def step(i, _):
        planes = []
        x0 = pl.multiple_of(i * chunk, chunk)
        rows_u = [u_ref[b, pl.ds(x0, chunk), :] for b in range(4)]
        rows_g = [gx_ref[a, pl.ds(x0, chunk), :] for a in range(4)]
        for x in range(chunk):
            plane = None
            for b in range(4):
                term = rows_u[b][x : x + 1, :] * gy_ref[b]
                plane = term if plane is None else plane + term
            planes.append(plane)
        spread = jnp.concatenate(planes, axis=0)
        density = lax.dot_general(
            spread, gz, (((1,), (1,)), ((), ())), precision=PRECISE, preferred_element_type=F32
        )
        density = density.reshape(chunk, CUBE, 128)
        density_ref[pl.ds(x0, chunk)] = density
        potential = external_ref[pl.ds(x0, chunk)] + jnp.tanh(density)
        along = jnp.dot(
            potential.reshape(chunk * CUBE, 128), gz, precision=PRECISE, preferred_element_type=F32
        )
        for a in range(4):
            total = None
            for x in range(chunk):
                term = along[x * CUBE : (x + 1) * CUBE, :] * rows_g[a][x : x + 1, :]
                total = term if total is None else total + term
            s_ref[a] += total
        return 0

    lax.fori_loop(0, CUBE // chunk, step, 0)
    for at, (a, b) in enumerate(ROWS):
        share_ref[at : at + 1, :] = (
            jnp.sum(s_ref[a] * gy_ref[b], axis=0, keepdims=True) * SCALE**3
        )


def grid_part(info, external):
    vmem = pl.BlockSpec(memory_space=pltpu.VMEM)
    return pl.pallas_call(
        grid_kernel,
        out_shape=(
            jax.ShapeDtypeStruct(external.shape, F32),
            jax.ShapeDtypeStruct((16, 256), F32),
        ),
        in_specs=[vmem, vmem],
        out_specs=(vmem, vmem),
        scratch_shapes=[
            pltpu.VMEM((4, CUBE, 256), F32),
            pltpu.VMEM((4, CUBE, 256), F32),
            pltpu.VMEM((128, 256), F32),
            pltpu.VMEM((4, CUBE, 256), F32),
            pltpu.VMEM((4, CUBE, 256), F32),
        ],
        compiler_params=pltpu.CompilerParams(vmem_limit_bytes=16 * 2**20),
        cost_estimate=pl.CostEstimate(
            flops=2 * 2 * 6 * 1024 * 256 * 128, bytes_accessed=2 * 2**20, transcendentals=2**18
        ),
    )(info, external)


def collect_kernel(near_ref, next_ref, last_ref, far_ref, atoms_ref, mine_ref):
    col = lax.axis_index("col")
    y, x = col // 4, col % 4
    total = jnp.zeros((16, 128), F32)
    for ref, dx in ((near_ref, 0), (next_ref, 1), (last_ref, 3), (far_ref, 2)):
        for j in range(2):
            source = (y + j) % 2 * 4 + (x + dx) % 4
            total += pltpu.roll(ref[16 * j : 16 * j + 16, :], (source + 7) % 8 * 16, 1)
    atoms_ref[...] = total
    mine_ref[...] = pltpu.roll(total, (8 - col) % 8 * 16, 1)


def collect(parts):
    vmem = pl.BlockSpec(memory_space=pltpu.VMEM)
    out = jax.ShapeDtypeStruct((16, 128), F32)
    return pl.pallas_call(
        collect_kernel,
        out_shape=(out, out),
        in_specs=[vmem] * 4,
        out_specs=(vmem, vmem),
        compiler_params=pltpu.CompilerParams(vmem_limit_bytes=2 * 2**20),
        cost_estimate=pl.CostEstimate(flops=0, bytes_accessed=2**17, transcendentals=0),
    )(*parts)


def row_of(y, z, core):
    return (y % 2 * 8 + z % 8) * 2 + core % 2


SITES = [(y, z, core) for y in range(2) for z in range(8) for core in range(2)]
ACROSS_Y = [(row_of(*s), row_of(s[0] + 1, s[1], s[2])) for s in SITES]
ACROSS_CORES = [(row_of(*s), row_of(s[0], s[1], s[2] + 1)) for s in SITES]
ALONG_Z = [(row_of(*s), row_of(s[0], s[1] + 1 - 2 * s[2], s[2])) for s in SITES]
COLS = [(y, x) for y in range(2) for x in range(4)]


def col_pairs(dy, dx):
    return [(y * 4 + x, (y + dy) % 2 * 4 + (x + dx) % 4) for y, x in COLS]


def ring(axis, size, step):
    return [(i, (i + step) % size) for i in range(size)]


def from_neighbours(last, first, axis, size):
    before = lax.ppermute(last, axis, ring(axis, size, 1))
    after = lax.ppermute(first, axis, ring(axis, size, -1))
    return before, after


def shifted(info, line, amount):
    return info.at[line].add(amount)


def on_device(coefficients, off_x, off_y, off_z, external, pattern, hamiltonian, density_matrix):
    core = lax.axis_index("row") % 2
    hp, pp = pack(pattern, hamiltonian, density_matrix)
    table_p, table_h = tile_tables(pattern)

    coef = coefficients.reshape(4, 4, 2, 2, 4).transpose(3, 1, 2, 0, 4).reshape(16, 16)
    offs = jnp.stack([off_x, off_y, off_z]).astype(F32)
    offs = jnp.broadcast_to(offs[:, :, None], (3, 4, 4)).reshape(3, 16)
    info = jnp.concatenate([coef, offs, jnp.zeros((5, 16), F32)], axis=0)
    before, after = from_neighbours(info, info, "col", 8)
    info = jnp.concatenate([shifted(before, 17, -32.0), info, shifted(after, 17, 32.0)], axis=1)
    before, after = from_neighbours(info, info, "row", 32)
    info = jnp.concatenate(
        [shifted(before, 16, -32.0), info, shifted(after, 16, 32.0), jnp.zeros((24, 112), F32)], axis=1
    )
    density, share = grid_part(info, external)
    before, after = from_neighbours(share[:, 96:144], share[:, 0:48], "row", 32)
    share = share[:, 48:96] + before + after
    share = jnp.concatenate([share, jnp.zeros((16, 80), F32)], axis=1)
    other = lax.ppermute(share, "col", col_pairs(1, 0))
    share = jnp.concatenate([share, other], axis=0)
    shares = [share] + [lax.ppermute(share, "col", col_pairs(0, d)) for d in (3, 1, 2)]
    atoms, mine = collect(shares)
    integrals = (
        mine[:, :16].reshape(2, 4, 2, 4, 4).transpose(3, 1, 2, 0, 4).reshape(4, 64)
    )

    hy = lax.ppermute(hp, "col", col_pairs(1, 0))
    h0 = jnp.concatenate([hp, hy], axis=0)
    h_next = lax.ppermute(h0, "col", col_pairs(0, 3))
    h_last = lax.ppermute(h0, "col", col_pairs(0, 1))
    h_far = lax.ppermute(h0, "col", col_pairs(0, 2))
    h_dense = spread_hamiltonian(
        table_h, [h0, h_next, h_last, h_far], ((0, 0), (1, 1), (2, 3), (3, 2))
    )

    py = lax.ppermute(pp, "row", ACROSS_Y)
    m = jnp.concatenate([pp, py], axis=0)
    mc = lax.ppermute(m, "row", ACROSS_CORES)
    own = [m, mc]
    product = None
    chain, chain_c = m, mc
    for s in (1, 2, 3):
        chain = lax.ppermute(chain, "row", ALONG_Z)
        chain_c = lax.ppermute(chain_c, "row", ALONG_Z)
        other = lax.ppermute(chain, "row", ACROSS_CORES)
        other_c = lax.ppermute(chain_c, "row", ACROSS_CORES)
        product = accumulate(
            table_p,
            h_dense,
            product,
            [chain, chain_c, other, other_c],
            ((-s, 0), (-s, 1), (s, 1), (s, 0)),
        )
    chain = lax.ppermute(chain, "row", ALONG_Z)
    other = lax.ppermute(chain, "row", ACROSS_CORES)
    product = accumulate(table_p, h_dense, product, own, ((0, 0), (0, 1)), atoms)
    product = accumulate(table_p, h_dense, product, [chain, other], ((4, 0), (4, 1)))
    return (density, integrals, product)


def solution(mesh):
    return jax.shard_map(
        on_device,
        mesh=mesh,
        in_specs=(
            P(("row", "col"), None),
            P(("row", "col")),
            P(("row", "col")),
            P(("row", "col")),
            P("row", "col", None),
            P(),
            P("row", "col"),
            P("row", "col"),
        ),
        out_specs=(P("row", "col", None), P(("row", "col"), None), P("row", "col")),
        check_vma=False,
    )
```

time: 232 us -> 125 us (0.54)
  waiting for transfers between devices: 136 us -> 20.7 us
  Pallas kernels: 0 us -> 32.2 us
  blocking collectives: 25.9 us -> 0 us
  matrix products: 22.6 us -> 0.95 us
  starting transfers between devices: 24.4 us -> 45.1 us
  local copies, waits for them, and re-layouts: 3.28 us -> 23.2 us
  between operations: 14.3 us -> 0.91 us
  other arithmetic: 5.64 us -> 0.89 us
    all_gather x2 -> x0, waiting for transfers between devices: 96.4 us -> none  [the longest x1 96.4 us: on_device(): lax.all_gather(p_masked, 'row', axis=0, tiled=True)]
    pallas_call x0 -> x9, Pallas kernels: none -> 32.2 us  [the longest x5 21.9 us: accumulate(): pl.pallas_call(functools.partial(accumulate_kernel, groups, before is Non...]
    all_gather x1 -> x0, blocking collectives: 25.9 us -> none  [on_device(): diagonal = lax.all_gather(integrals, 'col', axis=0, tiled=True)]
    dot_general x7 -> x1, matrix products: 22.4 us -> 0.95 us  [block_offsets(): slot = jnp.dot(flags, earlier, precision=PRECISE).astype(jnp.int32)]
    ppermute x8 -> x30, starting transfers between devices: 24.3 us -> 45.1 us  [the longest x4 11.6 us: on_device(): chain = lax.ppermute(chain, 'row', ALONG_Z)]
    ppermute x8 -> x30, waiting for transfers between devices: 38.7 us -> 20.7 us  [the longest x3 8.69 us: on_device(): lax.ppermute(share, 'col', col_pairs(0, d))]
    unnamed x17 -> x38, local copies, waits for them, and re-layouts: 0.85 us -> 11.1 us
    reshape x3 -> x9, local copies, waits for them, and re-layouts: 0.4 us -> 6.65 us  [the longest x2 2.82 us: on_device(): mine[:, :16].reshape(2, 4, 2, 4, 4).transpose(3, 1, 2, 0, 4).reshape(4, 64)]
  transfers between devices with their start and end apart: 10 -> 30, of which waited for: 7 -> 8; matrix products, arithmetic and copies ran while one was open for 7% -> 10% of each run, Pallas kernels for 0% -> 23%
where the time goes in v1:
time: 125 us; the launch traced here: 124 us
  starting transfers between devices  45.1 us (36%)
  Pallas kernels  32.2 us (26%)
  local copies, waits for them, and re-layouts  23.2 us (19%)
  waiting for transfers between devices  20.7 us (17%)
    pallas_call x5, Pallas kernels, accumulate(): pl.pallas_call(functools.partial(accumulate_kernel, groups, before is Non...  21.9 us
    ppermute x4, starting transfers between devices, on_device(): chain = lax.ppermute(chain, 'row', ALONG_Z)  11.6 us
    unnamed x38, local copies, waits for them, and re-layouts  11.1 us
    ppermute x3, waiting for transfers between devices, on_device(): lax.ppermute(share, 'col', col_pairs(0, d))  8.69 us
    ppermute x4, starting transfers between devices, on_device(): other = lax.ppermute(chain, 'row', ACROSS_CORES)  6.97 us
    ppermute x3, starting transfers between devices, from_neighbours(): after = lax.ppermute(first, axis, ring(axis, size, -1))  6.31 us
    ppermute x3, starting transfers between devices, on_device(): chain_c = lax.ppermute(chain_c, 'row', ALONG_Z)  5.11 us
    pallas_call x1, Pallas kernels, grid_part(): pl.pallas_call(grid_kernel, out_shape=(jax.ShapeDtypeStruct(external.shap...  4.79 us
  transfers between devices with their start and end apart: 30, of which 8 were waited for; matrix products, arithmetic and copies ran while one was open for 10% of the time, Pallas kernels for 23%

profile of v1, /device:TPU:1, one launch (start us, length us, event | category | flops | bytes accessed | tf_op | source)
XLA Modules:
  0.0 123.9 jit_solution(12506559403717404476)
XLA Ops:
  0.6 0.8 reshape.134
  1.5 0.7 add_convert_fusion
  2.4 2.1 %collective-permute-start = (f32[24,16]{1,0:T(8,128)S(1)}, f32[24,16]{1,0:T(8,128)S(1)}, u32[]{:S(2)}, u32[]{:S(2)}) collective-permute-start(f32[24,16]{1,0:T(8,128)S(1)} %pad_maximum_fusion.1), channel_id=1, source_target_pairs={{0,1},{1,2},{2,3},{3,4},{4,5},{5,6},{6,7},{7,0},{8,9},{9,10},{10,1... | collective-permute-start | bytes 4616 | tf_op jit(solution)/shard_map/ppermute | solution.py:397
  4.5 4.0 %collective-permute-start.1 = (f32[24,16]{1,0:T(8,128)S(1)}, f32[24,16]{1,0:T(8,128)S(1)}, u32[]{:S(2)}, u32[]{:S(2)}) collective-permute-start(f32[24,16]{1,0:T(8,128)S(1)} %pad_maximum_fusion.1), channel_id=1, source_target_pairs={{0,7},{1,0},{2,1},{3,2},{4,3},{5,4},{6,5},{7,6},{8,15},{9,8},{10,9... | collective-permute-start | bytes 4616 | tf_op jit(solution)/shard_map/ppermute | solution.py:398
  8.5 1.0 copy-done
  9.6 1.0 copy-done.1
  10.6 0.8 copy-done.4
  11.4 2.5 %shard_map.105 = (bf16[768,128]{1,0:T(8,128)(2,1)S(1)}, bf16[768,128]{1,0:T(8,128)(2,1)S(1)}) custom-call(s32[128,128]{1,0:T(8,128)S(1)} %copy-done.4, bf16[256,1024]{1,0:T(8,128)(2,1)S(1)} %copy-done, bf16[256,1024]{1,0:T(8,128)(2,1)S(1)} %copy-done.1), custom_call_target="tpu_custom_call" | custom-call | bytes 4194304 | tf_op jit(solution)/shard_map/pallas_call | solution.py:63
  13.9 2.9 %collective-permute-start.10 = (bf16[768,128]{1,0:T(8,128)(2,1)S(1)}, bf16[768,128]{1,0:T(8,128)(2,1)S(1)}, u32[]{:S(2)}, u32[]{:S(2)}) collective-permute-start(bf16[768,128]{1,0:T(8,128)(2,1)S(1)} %get-tuple-element.60), channel_id=1, source_target_pairs={{0,4},{1,5},{2,6},{3,7},{4,0},{5,1},{6,2},{7,3},{8,12},{9,13},{10,... | collective-permute-start | bytes 589832 | tf_op jit(solution)/shard_map/ppermute | solution.py:433
  17.4 1.8 %collective-permute-start.3 = (f32[24,48]{1,0:T(8,128)S(1)}, f32[24,48]{1,0:T(8,128)S(1)}, u32[]{:S(2)}, u32[]{:S(2)}) collective-permute-start(f32[24,48]{1,0:T(8,128)S(1)} %pad_maximum_fusion.2), channel_id=1, source_target_pairs={{0,248},{8,0},{16,8},{24,16},{32,24},{40,32},{48,40},{56,48},{64,5... | collective-permute-start | bytes 13832 | tf_op jit(solution)/shard_map/ppermute | solution.py:398
  19.3 1.6 %collective-permute-start.2 = (f32[24,48]{1,0:T(8,128)S(1)}, f32[24,48]{1,0:T(8,128)S(1)}, u32[]{:S(2)}, u32[]{:S(2)}) collective-permute-start(f32[24,48]{1,0:T(8,128)S(1)} %pad_maximum_fusion.2), channel_id=1, source_target_pairs={{0,8},{8,16},{16,24},{24,32},{32,40},{40,48},{48,56},{56,64},{64,7... | collective-permute-start | bytes 13832 | tf_op jit(solution)/shard_map/ppermute | solution.py:397
  20.9 4.2 %collective-permute-done.14 = bf16[768,128]{1,0:T(8,128)(2,1)S(1)} collective-permute-done((bf16[768,128]{1,0:T(8,128)(2,1)S(1)}, bf16[768,128]{1,0:T(8,128)(2,1)S(1)}, u32[]{:S(2)}, u32[]{:S(2)}) %collective-permute-start.14) | collective-permute-done | bytes 196640 | tf_op jit(solution)/shard_map/ppermute | solution.py:442
  25.1 2.2 %collective-permute-start.16 = (bf16[1536,128]{1,0:T(8,128)(2,1)S(1)}, bf16[1536,128]{1,0:T(8,128)(2,1)S(1)}, u32[]{:S(2)}, u32[]{:S(2)}) collective-permute-start(bf16[1536,128]{1,0:T(8,128)(2,1)S(1)} %constant_dynamic-update-slice_fusion.2.refs_2_), channel_id=1, source_target_pairs={{0,8},{8,0},{16,24},{24,16},{32,40},{40,32},{48,56},{56,48},{64,72... | collective-permute-start | bytes 1179656 | tf_op jit(solution)/shard_map/ppermute | solution.py:444
  27.4 5.7 %collective-permute-start.15 = (bf16[1536,128]{1,0:T(8,128)(2,1)S(1)}, bf16[1536,128]{1,0:T(8,128)(2,1)S(1)}, u32[]{:S(2)}, u32[]{:S(2)}) collective-permute-start(bf16[1536,128]{1,0:T(8,128)(2,1)S(1)} %constant_dynamic-update-slice_fusion.2.refs_2_), channel_id=1, source_target_pairs={{0,16},{8,120},{16,32},{24,8},{32,48},{40,24},{48,64},{56,40},{64,... | collective-permute-start | bytes 1179656 | tf_op jit(solution)/shard_map/ppermute | solution.py:449
  33.3 1.2 collective-permute-start.17
  34.4 3.4 %collective-permute-done.15.refs_0_ = bf16[1536,128]{1,0:T(8,128)(2,1)S(1)} collective-permute-done((bf16[1536,128]{1,0:T(8,128)(2,1)S(1)}, bf16[1536,128]{1,0:T(8,128)(2,1)S(1)}, u32[]{:S(2)}, u32[]{:S(2)}) %collective-permute-start.15) | collective-permute-done | bytes 393248 | tf_op jit(solution)/shard_map/ppermute | solution.py:449
  37.8 3.1 %collective-permute-start.20 = (bf16[1536,128]{1,0:T(8,128)(2,1)S(1)}, bf16[1536,128]{1,0:T(8,128)(2,1)}, u32[]{:S(2)}, u32[]{:S(2)}) collective-permute-start(bf16[1536,128]{1,0:T(8,128)(2,1)S(1)} %collective-permute-done.15.refs_0_), channel_id=1, source_target_pairs={{0,16},{8,120},{16,32},{24,8},{32,48},{40,24},{48,64},{56,40},{64,... | collective-permute-start | bytes 1179656 | tf_op jit(solution)/shard_map/ppermute | solution.py:449
  40.9 1.0 copy-done.17
  42.0 4.8 %shard_map.103 = (f32[32,32,128]{2,1,0:T(8,128)}, f32[16,256]{1,0:T(8,128)S(1)}) custom-call(f32[24,256]{1,0:T(8,128)S(1)} %concatenate.39.info_ref, f32[32,32,128]{2,1,0:T(8,128)S(1)} %copy-done.17), custom_call_target="tpu_custom_call" | custom-call | flops 805306368 | bytes 2097152 | tf_op jit(solution)/shard_map/pallas_call | solution.py:330
  47.5 0.5 collective-permute-done.4
  48.0 0.9 collective-permute-start.12
  48.9 1.1 collective-permute-start.21
  50.1 1.0 collective-permute-start.24
  51.1 1.6 %collective-permute-start.6 = (f32[16,128]{1,0:T(8,128)S(1)}, f32[16,128]{1,0:T(8,128)S(1)}, u32[]{:S(2)}, u32[]{:S(2)}) collective-permute-start(f32[16,128]{1,0:T(8,128)S(1)} %concatenate.40), channel_id=1, source_target_pairs={{0,4},{1,5},{2,6},{3,7},{4,0},{5,1},{6,2},{7,3},{8,12},{9,13},{10,... | collective-permute-start | bytes 24584 | tf_op jit(solution)/shard_map/ppermute | solution.py:425
  52.7 2.4 %collective-permute-done.6 = f32[16,128]{1,0:T(8,128)S(1)} collective-permute-done((f32[16,128]{1,0:T(8,128)S(1)}, f32[16,128]{1,0:T(8,128)S(1)}, u32[]{:S(2)}, u32[]{:S(2)}) %collective-permute-start.6) | collective-permute-done | bytes 8224 | tf_op jit(solution)/shard_map/ppermute | solution.py:425
  55.2 1.9 %collective-permute-start.7 = (f32[32,128]{1,0:T(8,128)S(1)}, f32[32,128]{1,0:T(8,128)S(1)}, u32[]{:S(2)}, u32[]{:S(2)}) collective-permute-start(f32[32,128]{1,0:T(8,128)S(1)} %pad_maximum_fusion.near_ref), channel_id=1, source_target_pairs={{0,3},{1,0},{2,1},{3,2},{4,7},{5,4},{6,5},{7,6},{8,11},{9,8},{10,9... | collective-permute-start | bytes 49160 | tf_op jit(solution)/shard_map/ppermute | solution.py:427
  57.0 1.3 %collective-permute-done.7.next_ref = f32[32,128]{1,0:T(8,128)S(1)} collective-permute-done((f32[32,128]{1,0:T(8,128)S(1)}, f32[32,128]{1,0:T(8,128)S(1)}, u32[]{:S(2)}, u32[]{:S(2)}) %collective-permute-start.7) | collective-permute-done | bytes 16416 | tf_op jit(solution)/shard_map/ppermute | solution.py:427
  58.4 0.6 copy-done.8
  59.0 4.4 %collective-permute-done.8.last_ref = f32[32,128]{1,0:T(8,128)S(1)} collective-permute-done((f32[32,128]{1,0:T(8,128)S(1)}, f32[32,128]{1,0:T(8,128)S(1)}, u32[]{:S(2)}, u32[]{:S(2)}) %collective-permute-start.8) | collective-permute-done | bytes 16416 | tf_op jit(solution)/shard_map/ppermute | solution.py:427
  63.4 0.6 copy-done.10
  64.0 0.5 collective-permute-start.9
  64.5 0.6 copy-done.5
  65.1 3.0 %collective-permute-done.9.far_ref = f32[32,128]{1,0:T(8,128)S(1)} collective-permute-done((f32[32,128]{1,0:T(8,128)S(1)}, f32[32,128]{1,0:T(8,128)S(1)}, u32[]{:S(2)}, u32[]{:S(2)}) %collective-permute-start.9) | collective-permute-done | bytes 16416 | tf_op jit(solution)/shard_map/ppermute | solution.py:427
  68.1 0.6 copy-done.12
  69.2 4.9 %collective-permute-start.18 = (bf16[1536,128]{1,0:T(8,128)(2,1)S(1)}, bf16[1536,128]{1,0:T(8,128)(2,1)}, u32[]{:S(2)}, u32[]{:S(2)}) collective-permute-start(bf16[1536,128]{1,0:T(8,128)(2,1)S(1)} %collective-permute-done.15.refs_0_), channel_id=1, source_target_pairs={{0,8},{8,0},{16,24},{24,16},{32,40},{40,32},{48,56},{56,48},{64,72... | collective-permute-start | bytes 1179656 | tf_op jit(solution)/shard_map/ppermute | solution.py:451
  74.2 2.8 %collective-permute-start.25 = (bf16[1536,128]{1,0:T(8,128)(2,1)}, bf16[1536,128]{1,0:T(8,128)(2,1)}, u32[]{:S(2)}, u32[]{:S(2)}) collective-permute-start(bf16[1536,128]{1,0:T(8,128)(2,1)} %collective-permute-done.21.refs_2_), channel_id=1, source_target_pairs={{0,16},{8,120},{16,32},{24,8},{32,48},{40,24},{48,64},{56,40},{64,... | collective-permute-start | bytes 1179656 | tf_op jit(solution)/shard_map/ppermute | solution.py:450
  77.0 1.8 %collective-permute-start.28 = (bf16[1536,128]{1,0:T(8,128)(2,1)}, bf16[1536,128]{1,0:T(8,128)(2,1)S(1)}, u32[]{:S(2)}, u32[]{:S(2)}) collective-permute-start(bf16[1536,128]{1,0:T(8,128)(2,1)} %collective-permute-done.24.refs_1_), channel_id=1, source_target_pairs={{0,16},{8,120},{16,32},{24,8},{32,48},{40,24},{48,64},{56,40},{64,... | collective-permute-start | bytes 1179656 | tf_op jit(solution)/shard_map/ppermute | solution.py:460
  78.8 1.6 %constant_dynamic-slice_fusion.1 = s32[128,16]{1,0:T(8,128)} fusion(s32[128,128]{1,0:T(8,128)} %pattern_ref.1, s32[]{:T(128)S(6)} %select_n.30), kind=kLoop, calls=%fused_computation.35 | loop fusion | bytes 16388 | tf_op jit(solution)/shard_map/dynamic_slice | solution.py:91
  80.3 1.5 %reshape.139 = s32[32,64]{1,0:T(8,128)} reshape(s32[128,16]{1,0:T(8,128)} %constant_dynamic-slice_fusion.1) | data formatting | bytes 16384 | tf_op jit(solution)/shard_map/reshape | solution.py:91
  81.9 0.7 constant_dynamic-slice_fusion
  82.5 0.7 reshape.140
  83.2 0.7 copy.15
  84.0 0.7 reshape.141
  84.6 0.9 collective-permute-start.22
  86.2 1.4 %collective-permute-done.28.refs_1_ = bf16[1536,128]{1,0:T(8,128)(2,1)S(1)} collective-permute-done((bf16[1536,128]{1,0:T(8,128)(2,1)}, bf16[1536,128]{1,0:T(8,128)(2,1)S(1)}, u32[]{:S(2)}, u32[]{:S(2)}) %collective-permute-start.28) | collective-permute-done | bytes 393248 | tf_op jit(solution)/shard_map/ppermute | solution.py:460
  87.6 0.7 collective-permute-start.29
  88.3 0.9 fusion.2
  89.3 0.6 slice.101.table_ref
  89.9 0.7 copy-done.6
  90.6 0.7 copy-done.9
  91.3 0.7 copy-done.11
  92.0 0.7 copy-done.13
  92.9 0.6 copy-done.14
  93.5 0.6 copy-done.15
  94.1 1.4 %reshape.137 = f32[2,4,2,4,4]{4,3,2,1,0:T(4,128)} reshape(f32[16,16]{1,0:T(8,128)} %bitcast.9) | data formatting | bytes 2048 | tf_op jit(solution)/shard_map/reshape | solution.py:430
  95.5 1.4 %copy.14 = f32[4,4,2,2,4]{4,3,2,1,0:T(2,128)} copy(f32[4,4,2,2,4]{4,0,2,1,3:T(4,128)} %bitcast.11) | data formatting | bytes 2048 | tf_op jit(solution)/shard_map/transpose | solution.py:430
  96.9 1.4 %reshape.138 = f32[4,64]{1,0:T(4,128)} reshape(f32[4,4,2,2,4]{4,3,2,1,0:T(2,128)} %copy.14) | data formatting | bytes 2048 | tf_op jit(solution)/shard_map/reshape | solution.py:430
  98.3 0.7 copy-done.7
  99.0 2.9 %shard_map.106.h_ref = bf16[32,256,256]{2,1,0:T(8,128)(2,1)S(1)} custom-call(s32[8,64]{1,0:T(8,128)S(1)} %copy-done.7, bf16[1536,128]{1,0:T(8,128)(2,1)S(1)} %constant_dynamic-update-slice_fusion.refs_0_, bf16[1536,128]{1,0:T(8,128)(2,1)S(1)} %collective-permute-done.11.refs_1_, bf16[1536,128]{1,0:T(8,128)(2,1)S(1)} %collective-permute-done.12.refs_2_, ...), custom_call_target="tpu_custom_call" | custom-call | bytes 12582912 | tf_op jit(solution)/shard_map/pallas_call | solution.py:138
  101.9 4.8 %shard_map.107.refs_0_ = f32[256,1024]{1,0:T(8,128)S(1)} custom-call(s32[32,64]{1,0:T(8,128)S(1)} %slice.100.table_ref, bf16[32,256,256]{2,1,0:T(8,128)(2,1)S(1)} %shard_map.106.h_ref, bf16[1536,128]{1,0:T(8,128)(2,1)S(1)} %collective-permute-done.15.refs_0_, bf16[1536,128]{1,0:T(8,128)(2,1)S(1)} %copy-done.3, ...), custom_call_target="tpu_custom_call" | custom-call | flops 1073741824 | bytes 8388608 | tf_op jit(solution)/shard_map/pallas_call | solution.py:232
  106.7 5.1 %shard_map.108.refs_0_ = f32[256,1024]{1,0:T(8,128)S(1)} custom-call(s32[32,64]{1,0:T(8,128)S(1)} %slice.100.table_ref, bf16[32,256,256]{2,1,0:T(8,128)(2,1)S(1)} %shard_map.106.h_ref, f32[256,1024]{1,0:T(8,128)S(1)} %shard_map.107.refs_0_, bf16[1536,128]{1,0:T(8,128)(2,1)} %collective-permute-done.20.refs_1_, ...), custom_call_target="tpu_custom_call" | custom-call | flops 1073741824 | bytes 8388608 | tf_op jit(solution)/shard_map/pallas_call | solution.py:232
  111.8 5.1 %shard_map.109.refs_0_ = f32[256,1024]{1,0:T(8,128)S(1)} custom-call(s32[32,64]{1,0:T(8,128)S(1)} %slice.100.table_ref, bf16[32,256,256]{2,1,0:T(8,128)(2,1)S(1)} %shard_map.106.h_ref, f32[256,1024]{1,0:T(8,128)S(1)} %shard_map.108.refs_0_, bf16[1536,128]{1,0:T(8,128)(2,1)} %collective-permute-done.24.refs_1_, ...), custom_call_target="tpu_custom_call" | custom-call | flops 1073741824 | bytes 8388608 | tf_op jit(solution)/shard_map/pallas_call | solution.py:232
  116.9 3.3 %shard_map.110.refs_0_ = f32[256,1024]{1,0:T(8,128)S(1)} custom-call(s32[32,64]{1,0:T(8,128)S(1)} %slice.100.table_ref, bf16[32,256,256]{2,1,0:T(8,128)(2,1)S(1)} %shard_map.106.h_ref, f32[256,1024]{1,0:T(8,128)S(1)} %shard_map.109.refs_0_, f32[16,128]{1,0:T(8,128)S(1)} %copy-done.16, bf16[1536,128]{1,0:T(8,128)(2,1)S(1)} %constant_dynamic-update-slice_fusion.2.refs_2_, ...), custom_call_target="tpu_custom_call" | custom-call | flops 536870912 | bytes 8388608 | tf_op jit(solution)/shard_map/pallas_call | solution.py:232
  120.2 3.7 %shard_map.111 = f32[256,1024]{1,0:T(8,128)} custom-call(s32[32,64]{1,0:T(8,128)S(1)} %slice.100.table_ref, bf16[32,256,256]{2,1,0:T(8,128)(2,1)S(1)} %shard_map.106.h_ref, f32[256,1024]{1,0:T(8,128)S(1)} %shard_map.110.refs_0_, bf16[1536,128]{1,0:T(8,128)(2,1)S(1)} %collective-permute-done.28.refs_1_, bf16[1536,128]{1,0:T(8,128)(2,1)S(1)} %collective-permute-done.29.refs_2_), custom_call_target="tpu_custom_call" | custom-call | flops 536870912 | bytes 8388608 | tf_op jit(solution)/shard_map/pallas_call | solution.py:232
  (82 shorter events, 3.3 us)
Async XLA Ops:
  2.4 14.8 %collective-permute-start = (f32[24,16]{1,0:T(8,128)S(1)}, f32[24,16]{1,0:T(8,128)S(1)}, u32[]{:S(2)}, u32[]{:S(2)}) collective-permute-start(f32[24,16]{1,0:T(8,128)S(1)} %pad_maximum_fusion.1), channel_id=1, source_target_pairs={{0,1},{1,2},{2,3},{3,4},{4,5},{5,6},{6,7},{7,0},{8,9},{9,10},{10,1... | collective-permute-start | bytes 4616 | tf_op jit(solution)/shard_map/ppermute | solution.py:397
  4.5 12.7 %collective-permute-start.1 = (f32[24,16]{1,0:T(8,128)S(1)}, f32[24,16]{1,0:T(8,128)S(1)}, u32[]{:S(2)}, u32[]{:S(2)}) collective-permute-start(f32[24,16]{1,0:T(8,128)S(1)} %pad_maximum_fusion.1), channel_id=1, source_target_pairs={{0,7},{1,0},{2,1},{3,2},{4,3},{5,4},{6,5},{7,6},{8,15},{9,8},{10,9... | collective-permute-start | bytes 4616 | tf_op jit(solution)/shard_map/ppermute | solution.py:398
  8.5 1.0 copy-start
  9.6 1.0 copy-start.1
  10.6 0.8 copy-start.4
  13.9 33.4 %collective-permute-start.10 = (bf16[768,128]{1,0:T(8,128)(2,1)S(1)}, bf16[768,128]{1,0:T(8,128)(2,1)S(1)}, u32[]{:S(2)}, u32[]{:S(2)}) collective-permute-start(bf16[768,128]{1,0:T(8,128)(2,1)S(1)} %get-tuple-element.60), channel_id=1, source_target_pairs={{0,4},{1,5},{2,6},{3,7},{4,0},{5,1},{6,2},{7,3},{8,12},{9,13},{10,... | collective-permute-start | bytes 589832 | tf_op jit(solution)/shard_map/ppermute | solution.py:433
  16.8 8.3 %collective-permute-start.14 = (bf16[768,128]{1,0:T(8,128)(2,1)S(1)}, bf16[768,128]{1,0:T(8,128)(2,1)S(1)}, u32[]{:S(2)}, u32[]{:S(2)}) collective-permute-start(bf16[768,128]{1,0:T(8,128)(2,1)S(1)} %get-tuple-element.61), channel_id=1, source_target_pairs={{0,128},{8,136},{16,144},{24,152},{32,160},{40,168},{48,176},{56,1... | collective-permute-start | bytes 589832 | tf_op jit(solution)/shard_map/ppermute | solution.py:442
  17.4 15.7 %collective-permute-start.3 = (f32[24,48]{1,0:T(8,128)S(1)}, f32[24,48]{1,0:T(8,128)S(1)}, u32[]{:S(2)}, u32[]{:S(2)}) collective-permute-start(f32[24,48]{1,0:T(8,128)S(1)} %pad_maximum_fusion.2), channel_id=1, source_target_pairs={{0,248},{8,0},{16,8},{24,16},{32,24},{40,32},{48,40},{56,48},{64,5... | collective-permute-start | bytes 13832 | tf_op jit(solution)/shard_map/ppermute | solution.py:398
  19.3 13.9 %collective-permute-start.2 = (f32[24,48]{1,0:T(8,128)S(1)}, f32[24,48]{1,0:T(8,128)S(1)}, u32[]{:S(2)}, u32[]{:S(2)}) collective-permute-start(f32[24,48]{1,0:T(8,128)S(1)} %pad_maximum_fusion.2), channel_id=1, source_target_pairs={{0,8},{8,16},{16,24},{24,32},{32,40},{40,48},{48,56},{56,64},{64,7... | collective-permute-start | bytes 13832 | tf_op jit(solution)/shard_map/ppermute | solution.py:397
  25.1 8.1 %collective-permute-start.16 = (bf16[1536,128]{1,0:T(8,128)(2,1)S(1)}, bf16[1536,128]{1,0:T(8,128)(2,1)S(1)}, u32[]{:S(2)}, u32[]{:S(2)}) collective-permute-start(bf16[1536,128]{1,0:T(8,128)(2,1)S(1)} %constant_dynamic-update-slice_fusion.2.refs_2_), channel_id=1, source_target_pairs={{0,8},{8,0},{16,24},{24,16},{32,40},{40,32},{48,56},{56,48},{64,72... | collective-permute-start | bytes 1179656 | tf_op jit(solution)/shard_map/ppermute | solution.py:444
  27.4 10.4 %collective-permute-start.15 = (bf16[1536,128]{1,0:T(8,128)(2,1)S(1)}, bf16[1536,128]{1,0:T(8,128)(2,1)S(1)}, u32[]{:S(2)}, u32[]{:S(2)}) collective-permute-start(bf16[1536,128]{1,0:T(8,128)(2,1)S(1)} %constant_dynamic-update-slice_fusion.2.refs_2_), channel_id=1, source_target_pairs={{0,16},{8,120},{16,32},{24,8},{32,48},{40,24},{48,64},{56,40},{64,... | collective-permute-start | bytes 1179656 | tf_op jit(solution)/shard_map/ppermute | solution.py:449
  33.3 15.6 %collective-permute-start.17 = (bf16[1536,128]{1,0:T(8,128)(2,1)S(1)}, bf16[1536,128]{1,0:T(8,128)(2,1)S(1)}, u32[]{:S(2)}, u32[]{:S(2)}) collective-permute-start(bf16[1536,128]{1,0:T(8,128)(2,1)S(1)} %collective-permute-done.16.refs_3_), channel_id=1, source_target_pairs={{0,16},{8,120},{16,32},{24,8},{32,48},{40,24},{48,64},{56,40},{64,... | collective-permute-start | bytes 1179656 | tf_op jit(solution)/shard_map/ppermute | solution.py:450
  37.8 12.3 %collective-permute-start.20 = (bf16[1536,128]{1,0:T(8,128)(2,1)S(1)}, bf16[1536,128]{1,0:T(8,128)(2,1)}, u32[]{:S(2)}, u32[]{:S(2)}) collective-permute-start(bf16[1536,128]{1,0:T(8,128)(2,1)S(1)} %collective-permute-done.15.refs_0_), channel_id=1, source_target_pairs={{0,16},{8,120},{16,32},{24,8},{32,48},{40,24},{48,64},{56,40},{64,... | collective-permute-start | bytes 1179656 | tf_op jit(solution)/shard_map/ppermute | solution.py:449
  40.9 1.0 copy-start.17
  46.8 1.2 collective-permute-start.4
  46.8 4.2 %collective-permute-start.5 = (f32[16,48]{1,0:T(8,128)S(1)}, f32[16,48]{1,0:T(8,128)S(1)}, u32[]{:S(2)}, u32[]{:S(2)}) collective-permute-start(f32[16,48]{1,0:T(8,128)S(1)} %get-tuple-element.64), channel_id=1, source_target_pairs={{0,248},{8,0},{16,8},{24,16},{32,24},{40,32},{48,40},{56,48},{64,5... | collective-permute-start | bytes 9224 | tf_op jit(solution)/shard_map/ppermute | solution.py:398
  47.4 21.8 %collective-permute-start.11 = (bf16[1536,128]{1,0:T(8,128)(2,1)S(1)}, bf16[1536,128]{1,0:T(8,128)(2,1)S(1)}, u32[]{:S(2)}, u32[]{:S(2)}) collective-permute-start(bf16[1536,128]{1,0:T(8,128)(2,1)S(1)} %constant_dynamic-update-slice_fusion.refs_0_), channel_id=1, source_target_pairs={{0,3},{1,0},{2,1},{3,2},{4,7},{5,4},{6,5},{7,6},{8,11},{9,8},{10,9... | collective-permute-start | bytes 1179656 | tf_op jit(solution)/shard_map/ppermute | solution.py:435
  48.0 26.1 %collective-permute-start.12 = (bf16[1536,128]{1,0:T(8,128)(2,1)S(1)}, bf16[1536,128]{1,0:T(8,128)(2,1)S(1)}, u32[]{:S(2)}, u32[]{:S(2)}) collective-permute-start(bf16[1536,128]{1,0:T(8,128)(2,1)S(1)} %constant_dynamic-update-slice_fusion.refs_0_), channel_id=1, source_target_pairs={{0,1},{1,2},{2,3},{3,0},{4,5},{5,6},{6,7},{7,4},{8,9},{9,10},{10,1... | collective-permute-start | bytes 1179656 | tf_op jit(solution)/shard_map/ppermute | solution.py:436
  48.9 37.3 %copy-start.2 = (bf16[1536,128]{1,0:T(8,128)(2,1)}, bf16[1536,128]{1,0:T(8,128)(2,1)S(1)}, u32[]{:S(2)}) copy-start(bf16[1536,128]{1,0:T(8,128)(2,1)S(1)} %collective-permute-done.17.refs_1_) | copy-start | bytes 1179652
  48.9 25.2 %collective-permute-start.21 = (bf16[1536,128]{1,0:T(8,128)(2,1)S(1)}, bf16[1536,128]{1,0:T(8,128)(2,1)}, u32[]{:S(2)}, u32[]{:S(2)}) collective-permute-start(bf16[1536,128]{1,0:T(8,128)(2,1)S(1)} %collective-permute-done.17.refs_1_), channel_id=1, source_target_pairs={{0,16},{8,120},{16,32},{24,8},{32,48},{40,24},{48,64},{56,40},{64,... | collective-permute-start | bytes 1179656 | tf_op jit(solution)/shard_map/ppermute | solution.py:450
  50.1 26.9 %collective-permute-start.24 = (bf16[1536,128]{1,0:T(8,128)(2,1)}, bf16[1536,128]{1,0:T(8,128)(2,1)}, u32[]{:S(2)}, u32[]{:S(2)}) collective-permute-start(bf16[1536,128]{1,0:T(8,128)(2,1)} %collective-permute-done.20.refs_1_), channel_id=1, source_target_pairs={{0,16},{8,120},{16,32},{24,8},{32,48},{40,24},{48,64},{56,40},{64,... | collective-permute-start | bytes 1179656 | tf_op jit(solution)/shard_map/ppermute | solution.py:449
  51.1 4.0 %collective-permute-start.6 = (f32[16,128]{1,0:T(8,128)S(1)}, f32[16,128]{1,0:T(8,128)S(1)}, u32[]{:S(2)}, u32[]{:S(2)}) collective-permute-start(f32[16,128]{1,0:T(8,128)S(1)} %concatenate.40), channel_id=1, source_target_pairs={{0,4},{1,5},{2,6},{3,7},{4,0},{5,1},{6,2},{7,3},{8,12},{9,13},{10,... | collective-permute-start | bytes 24584 | tf_op jit(solution)/shard_map/ppermute | solution.py:425
  55.2 3.2 %collective-permute-start.7 = (f32[32,128]{1,0:T(8,128)S(1)}, f32[32,128]{1,0:T(8,128)S(1)}, u32[]{:S(2)}, u32[]{:S(2)}) collective-permute-start(f32[32,128]{1,0:T(8,128)S(1)} %pad_maximum_fusion.near_ref), channel_id=1, source_target_pairs={{0,3},{1,0},{2,1},{3,2},{4,7},{5,4},{6,5},{7,6},{8,11},{9,8},{10,9... | collective-permute-start | bytes 49160 | tf_op jit(solution)/shard_map/ppermute | solution.py:427
  58.4 0.6 copy-start.8
  59.0 4.4 %collective-permute-start.8 = (f32[32,128]{1,0:T(8,128)S(1)}, f32[32,128]{1,0:T(8,128)S(1)}, u32[]{:S(2)}, u32[]{:S(2)}) collective-permute-start(f32[32,128]{1,0:T(8,128)S(1)} %pad_maximum_fusion.near_ref), channel_id=1, source_target_pairs={{0,1},{1,2},{2,3},{3,0},{4,5},{5,6},{6,7},{7,4},{8,9},{9,10},{10,1... | collective-permute-start | bytes 49160 | tf_op jit(solution)/shard_map/ppermute | solution.py:427
  63.4 0.6 copy-start.10
  64.0 4.1 %collective-permute-start.9 = (f32[32,128]{1,0:T(8,128)S(1)}, f32[32,128]{1,0:T(8,128)S(1)}, u32[]{:S(2)}, u32[]{:S(2)}) collective-permute-start(f32[32,128]{1,0:T(8,128)S(1)} %pad_maximum_fusion.near_ref), channel_id=1, source_target_pairs={{0,2},{1,3},{2,0},{3,1},{4,6},{5,7},{6,4},{7,5},{8,10},{9,11},{10,... | collective-permute-start | bytes 49160 | tf_op jit(solution)/shard_map/ppermute | solution.py:427
  64.5 0.6 copy-start.5
  68.1 0.6 copy-start.12
  68.7 16.0 %collective-permute-start.13 = (bf16[1536,128]{1,0:T(8,128)(2,1)S(1)}, bf16[1536,128]{1,0:T(8,128)(2,1)S(1)}, u32[]{:S(2)}, u32[]{:S(2)}) collective-permute-start(bf16[1536,128]{1,0:T(8,128)(2,1)S(1)} %constant_dynamic-update-slice_fusion.refs_0_), channel_id=1, source_target_pairs={{0,2},{1,3},{2,0},{3,1},{4,6},{5,7},{6,4},{7,5},{8,10},{9,11},{10,... | collective-permute-start | bytes 1179656 | tf_op jit(solution)/shard_map/ppermute | solution.py:437
  69.2 16.4 %collective-permute-start.18 = (bf16[1536,128]{1,0:T(8,128)(2,1)S(1)}, bf16[1536,128]{1,0:T(8,128)(2,1)}, u32[]{:S(2)}, u32[]{:S(2)}) collective-permute-start(bf16[1536,128]{1,0:T(8,128)(2,1)S(1)} %collective-permute-done.15.refs_0_), channel_id=1, source_target_pairs={{0,8},{8,0},{16,24},{24,16},{32,40},{40,32},{48,56},{56,48},{64,72... | collective-permute-start | bytes 1179656 | tf_op jit(solution)/shard_map/ppermute | solution.py:451
  74.1 11.6 %collective-permute-start.19 = (bf16[1536,128]{1,0:T(8,128)(2,1)S(1)}, bf16[1536,128]{1,0:T(8,128)(2,1)}, u32[]{:S(2)}, u32[]{:S(2)}) collective-permute-start(bf16[1536,128]{1,0:T(8,128)(2,1)S(1)} %collective-permute-done.17.refs_1_), channel_id=1, source_target_pairs={{0,8},{8,0},{16,24},{24,16},{32,40},{40,32},{48,56},{56,48},{64,72... | collective-permute-start | bytes 1179656 | tf_op jit(solution)/shard_map/ppermute | solution.py:452
  74.2 11.9 %collective-permute-start.25 = (bf16[1536,128]{1,0:T(8,128)(2,1)}, bf16[1536,128]{1,0:T(8,128)(2,1)}, u32[]{:S(2)}, u32[]{:S(2)}) collective-permute-start(bf16[1536,128]{1,0:T(8,128)(2,1)} %collective-permute-done.21.refs_2_), channel_id=1, source_target_pairs={{0,16},{8,120},{16,32},{24,8},{32,48},{40,24},{48,64},{56,40},{64,... | collective-permute-start | bytes 1179656 | tf_op jit(solution)/shard_map/ppermute | solution.py:450
  77.0 10.6 %collective-permute-start.28 = (bf16[1536,128]{1,0:T(8,128)(2,1)}, bf16[1536,128]{1,0:T(8,128)(2,1)S(1)}, u32[]{:S(2)}, u32[]{:S(2)}) collective-permute-start(bf16[1536,128]{1,0:T(8,128)(2,1)} %collective-permute-done.24.refs_1_), channel_id=1, source_target_pairs={{0,16},{8,120},{16,32},{24,8},{32,48},{40,24},{48,64},{56,40},{64,... | collective-permute-start | bytes 1179656 | tf_op jit(solution)/shard_map/ppermute | solution.py:460
  84.6 22.1 %collective-permute-start.22 = (bf16[1536,128]{1,0:T(8,128)(2,1)}, bf16[1536,128]{1,0:T(8,128)(2,1)}, u32[]{:S(2)}, u32[]{:S(2)}) collective-permute-start(bf16[1536,128]{1,0:T(8,128)(2,1)} %collective-permute-done.20.refs_1_), channel_id=1, source_target_pairs={{0,8},{8,0},{16,24},{24,16},{32,40},{40,32},{48,56},{56,48},{64,72... | collective-permute-start | bytes 1179656 | tf_op jit(solution)/shard_map/ppermute | solution.py:451
  85.6 21.1 %collective-permute-start.23 = (bf16[1536,128]{1,0:T(8,128)(2,1)}, bf16[1536,128]{1,0:T(8,128)(2,1)}, u32[]{:S(2)}, u32[]{:S(2)}) collective-permute-start(bf16[1536,128]{1,0:T(8,128)(2,1)} %collective-permute-done.21.refs_2_), channel_id=1, source_target_pairs={{0,8},{8,0},{16,24},{24,16},{32,40},{40,32},{48,56},{56,48},{64,72... | collective-permute-start | bytes 1179656 | tf_op jit(solution)/shard_map/ppermute | solution.py:452
  85.7 26.1 %collective-permute-start.26 = (bf16[1536,128]{1,0:T(8,128)(2,1)}, bf16[1536,128]{1,0:T(8,128)(2,1)}, u32[]{:S(2)}, u32[]{:S(2)}) collective-permute-start(bf16[1536,128]{1,0:T(8,128)(2,1)} %collective-permute-done.24.refs_1_), channel_id=1, source_target_pairs={{0,8},{8,0},{16,24},{24,16},{32,40},{40,32},{48,56},{56,48},{64,72... | collective-permute-start | bytes 1179656 | tf_op jit(solution)/shard_map/ppermute | solution.py:451
  86.1 25.7 %collective-permute-start.27 = (bf16[1536,128]{1,0:T(8,128)(2,1)}, bf16[1536,128]{1,0:T(8,128)(2,1)}, u32[]{:S(2)}, u32[]{:S(2)}) collective-permute-start(bf16[1536,128]{1,0:T(8,128)(2,1)} %collective-permute-done.25.refs_2_), channel_id=1, source_target_pairs={{0,8},{8,0},{16,24},{24,16},{32,40},{40,32},{48,56},{56,48},{64,72... | collective-permute-start | bytes 1179656 | tf_op jit(solution)/shard_map/ppermute | solution.py:452
  87.6 32.6 %collective-permute-start.29 = (bf16[1536,128]{1,0:T(8,128)(2,1)S(1)}, bf16[1536,128]{1,0:T(8,128)(2,1)S(1)}, u32[]{:S(2)}, u32[]{:S(2)}) collective-permute-start(bf16[1536,128]{1,0:T(8,128)(2,1)S(1)} %collective-permute-done.28.refs_1_), channel_id=1, source_target_pairs={{0,8},{8,0},{16,24},{24,16},{32,40},{40,32},{48,56},{56,48},{64,72... | collective-permute-start | bytes 1179656 | tf_op jit(solution)/shard_map/ppermute | solution.py:461
  89.9 0.7 copy-start.6
  90.6 0.7 copy-start.9
  91.3 0.7 copy-start.11
  92.0 0.7 copy-start.13
  92.9 0.6 copy-start.14
  93.5 0.6 copy-start.15
  98.3 0.7 copy-start.7
  99.0 2.9 %copy-start.3 = (bf16[1536,128]{1,0:T(8,128)(2,1)S(1)}, bf16[1536,128]{1,0:T(8,128)(2,1)}, u32[]{:S(2)}) copy-start(bf16[1536,128]{1,0:T(8,128)(2,1)} %copy-done.2) | copy-start | bytes 1179652
  111.8 5.1 %copy-start.16 = (f32[16,128]{1,0:T(8,128)S(1)}, f32[16,128]{1,0:T(8,128)}, u32[]{:S(2)}) copy-start(f32[16,128]{1,0:T(8,128)} %copy-done.15) | copy-start | bytes 24580

commit v2 on v1

v2 whole, which is shorter than its diff:
```python
import functools

import jax
import jax.numpy as jnp
from jax import lax
from jax.experimental import pallas as pl
from jax.experimental.pallas import tpu as pltpu
from jax.sharding import PartitionSpec as P

BS = 64
CUBE = 32
SLOTS = 24
PACK = SLOTS // 2 * BS
F32 = jnp.float32
BF16 = jnp.bfloat16
PRECISE = lax.Precision.HIGHEST
SCALE = 6.0 / CUBE


def swap_halves(block):
    return jnp.concatenate([block[:, BS:], block[:, :BS]], axis=1)


def atom_rows(coef_ref, offset_refs, info_ref, wide):
    rho = lax.broadcasted_iota(jnp.int32, (16, 64), 0)
    lane = lax.broadcasted_iota(jnp.int32, (16, 64), 1)
    match = lane // 4 == rho % 8 // 2 * 4 + rho % 2 * 2 + rho // 8
    for i in range(4):
        wide[:, 64 * i : 64 * i + 64] = jnp.where(match, coef_ref[i : i + 1, :], 0.0)
    m = lax.broadcasted_iota(jnp.int32, (256, 128), 0)
    target = lax.broadcasted_iota(jnp.int32, (256, 128), 1)
    move = jnp.where((target // 4 == m // 64) & (target % 4 == m % 4), 1.0, 0.0)
    total = jnp.dot(wide[...], move, precision=PRECISE, preferred_element_type=F32)
    info_ref[0:16, :] = total[:, :16]
    atom = lax.broadcasted_iota(jnp.int32, (8, 16), 1) // 4
    line = lax.broadcasted_iota(jnp.int32, (8, 16), 0)
    lower = jnp.zeros((8, 16), F32)
    for k, ref in enumerate(offset_refs):
        for i in range(4):
            lower = jnp.where((line == k) & (atom == i), ref[i].astype(F32), lower)
    info_ref[16:24, :] = lower


def pack_kernel(
    pattern_hbm, h_hbm, p_hbm, coef_hbm, x_hbm, y_hbm, z_hbm, hp_ref, pp_ref, info_ref,
    rows, places, h_ref, p_ref, coef_ref, x_ref, y_ref, z_ref, wide, sems,
):
    row, col = lax.axis_index("row"), lax.axis_index("col")
    copies = [
        pltpu.make_async_copy(
            pattern_hbm.at[pl.ds(pl.multiple_of(row // 2 * 8, 8), 8), :], rows, sems.at[0]
        ),
        pltpu.make_async_copy(p_hbm, p_ref, sems.at[1]),
        pltpu.make_async_copy(h_hbm, h_ref, sems.at[2]),
        pltpu.make_async_copy(coef_hbm, coef_ref, sems.at[3]),
        pltpu.make_async_copy(x_hbm, x_ref, sems.at[4]),
        pltpu.make_async_copy(y_hbm, y_ref, sems.at[5]),
        pltpu.make_async_copy(z_hbm, z_ref, sems.at[6]),
    ]
    for copy in copies:
        copy.start()

    def clear(i, _):
        places[i] = 0
        return 0

    lax.fori_loop(0, SLOTS + 1, clear, 0)
    copies[0].wait()
    count = jnp.int32(0)
    for block in range(64):
        places[count] = block
        flag = rows[row % 2 * 4 + block // 16, col * 16 + block % 16]
        count = count + jnp.where(flag != 0, 1, 0)
    left = lax.broadcasted_iota(jnp.int32, (BS, 2 * BS), 1) < BS
    for copy, source, target in ((copies[1], p_ref, pp_ref), (copies[2], h_ref, hp_ref)):
        copy.wait()
        for pair in range(SLOTS // 2):
            halves = []
            for half in range(2):
                place = places[2 * pair + half]
                r, c = place // 16, place % 16
                block = source[
                    pl.ds(pl.multiple_of(r * BS, BS), BS),
                    pl.ds(pl.multiple_of(c // 2 * 128, 128), 128),
                ]
                halves.append(jnp.where(c % 2 == half, block, swap_halves(block)))
            target[pl.ds(pair * BS, BS), :] = jnp.where(left, halves[0], halves[1])
    for copy in copies[3:]:
        copy.wait()
    atom_rows(coef_ref, (x_ref, y_ref, z_ref), info_ref, wide)


def pack(*operands):
    packed = jax.ShapeDtypeStruct((PACK, 128), BF16)
    vmem = pl.BlockSpec(memory_space=pltpu.VMEM)
    return pl.pallas_call(
        pack_kernel,
        out_shape=(packed, packed, jax.ShapeDtypeStruct((24, 16), F32)),
        in_specs=[pl.BlockSpec(memory_space=pltpu.HBM)] * 7,
        out_specs=(vmem, vmem, vmem),
        scratch_shapes=[
            pltpu.SMEM((8, 128), jnp.int32),
            pltpu.SMEM((SLOTS + 8,), jnp.int32),
            pltpu.VMEM((256, 1024), BF16),
            pltpu.VMEM((256, 1024), BF16),
            pltpu.VMEM((4, 64), F32),
            pltpu.SMEM((4,), jnp.int32),
            pltpu.SMEM((4,), jnp.int32),
            pltpu.SMEM((4,), jnp.int32),
            pltpu.VMEM((16, 256), F32),
            pltpu.SemaphoreType.DMA((7,)),
        ],
        compiler_params=pltpu.CompilerParams(vmem_limit_bytes=58 * 2**20),
        cost_estimate=pl.CostEstimate(flops=0, bytes_accessed=6 * 2**20, transcendentals=0),
    )(*operands)


def offsets_of(slot, flags):
    slot = slot.astype(jnp.int32)
    parity = lax.broadcasted_iota(jnp.int32, slot.shape, 1) % 2
    at = slot // 2 * BS + jnp.where(slot % 2 == parity, 0, PACK)
    return jnp.where(flags > 0, at, 2 * PACK)


def table_kernel(pattern_ref, _, p_ref, h_ref, held):
    row, col = lax.axis_index("row"), lax.axis_index("col")
    r = lax.broadcasted_iota(jnp.int32, (128, 128), 0)
    m = lax.broadcasted_iota(jnp.int32, (128, 128), 1)

    def product(a, b):
        return jnp.dot(a.astype(BF16), b.astype(BF16), preferred_element_type=F32)

    def ones(where):
        return jnp.where(where, 1.0, 0.0)

    flags = ones(pattern_ref[...] != 0)
    mine = jnp.where(m < 16, pltpu.roll(flags, (8 - col) % 8 * 16, 1), 0.0)
    above = ones((r // 4 == m // 4) & (m < r))
    slot = product(mine, ones((r < m) & (m < 16)))
    slot += product(above, product(mine, ones(r < 16)))
    held[...] = offsets_of(slot, mine)
    total = jnp.zeros((32, 128), jnp.int32)
    lane = lax.broadcasted_iota(jnp.int32, (32, 128), 1)
    for b in range(4):
        part = jnp.where(lane < 16, held[pl.ds(b, 32, stride=4), :], 0)
        total += pltpu.roll(part, 16 * b, 1) if b else part
    p_ref[...] = total[:, :64]

    two = ones(pattern_ref[pl.ds(pl.multiple_of(row // 2 * 8, 8), 8), :] != 0)
    two = jnp.where(row % 2 == 0, two, pltpu.roll(two, 4, 0))
    four = jnp.where(lax.broadcasted_iota(jnp.int32, (8, 128), 0) < 4, two, 0.0)
    before = product(four, ones((r // 16 == m // 16) & (r < m)))
    whole = product(four, ones(r // 16 == m // 16))
    up = lax.broadcasted_iota(jnp.int32, (8, 8), 1) < lax.broadcasted_iota(jnp.int32, (8, 8), 0)
    before += jnp.dot(ones(up), whole, precision=PRECISE, preferred_element_type=F32)
    h_ref[...] = offsets_of(before, four)


def tile_tables(pattern, after):
    vmem = pl.BlockSpec(memory_space=pltpu.VMEM)
    return pl.pallas_call(
        table_kernel,
        out_shape=(
            jax.ShapeDtypeStruct((32, 64), jnp.int32),
            jax.ShapeDtypeStruct((8, 128), jnp.int32),
        ),
        in_specs=[vmem, pl.BlockSpec(memory_space=pl.ANY)],
        out_specs=(vmem, vmem),
        scratch_shapes=[pltpu.VMEM((128, 128), jnp.int32)],
        compiler_params=pltpu.CompilerParams(vmem_limit_bytes=4 * 2**20),
        cost_estimate=pl.CostEstimate(flops=0, bytes_accessed=2**21, transcendentals=0),
    )(pattern, after)


def spread_tile(packed, offset, both, store):
    both[0:PACK, :] = packed
    both[PACK : 2 * PACK, :] = swap_halves(packed)
    left = lax.broadcasted_iota(jnp.int32, (BS, 2 * BS), 1) < BS
    for r in range(4):
        for c in range(8):
            at0 = pl.multiple_of(offset(r, 2 * c), BS)
            at1 = pl.multiple_of(offset(r, 2 * c + 1), BS)
            block = jnp.where(left, both[pl.ds(at0, BS), :], both[pl.ds(at1, BS), :])
            store(r, c, block)


def spread_kernel(table_ref, near_ref, next_ref, last_ref, far_ref, out_ref, both):
    col = lax.axis_index("col")
    y, x = col // 4, col % 4
    both[2 * PACK :, :] = jnp.zeros((BS, 128), BF16)
    for part, dx in ((near_ref, 0), (next_ref, 1), (last_ref, 3), (far_ref, 2)):

        def one(j, _, part=part, dx=dx):
            source = (y + j) % 2 * 4 + (x + dx) % 4
            packed = part[pl.ds(pl.multiple_of(j * PACK, PACK), PACK), :]

            def store(r, c, block):
                out_ref[
                    source * 4 + c // 2, r * BS : (r + 1) * BS, c % 2 * 128 : c % 2 * 128 + 128
                ] = block

            spread_tile(packed, lambda r, c: table_ref[r, source * 16 + c], both, store)
            return 0

        lax.fori_loop(0, 2, one, 0)


def spread_hamiltonian(table, parts):
    vmem = pl.BlockSpec(memory_space=pltpu.VMEM)
    return pl.pallas_call(
        spread_kernel,
        out_shape=jax.ShapeDtypeStruct((32, 256, 256), BF16),
        in_specs=[pl.BlockSpec(memory_space=pltpu.SMEM)] + [vmem] * len(parts),
        out_specs=vmem,
        scratch_shapes=[pltpu.VMEM((2 * PACK + BS, 128), BF16)],
        compiler_params=pltpu.CompilerParams(vmem_limit_bytes=4 * 2**20),
        cost_estimate=pl.CostEstimate(flops=0, bytes_accessed=8 * 2**20, transcendentals=0),
    )(table, *parts)


def split3(value):
    high = value.astype(BF16)
    rest = value - high.astype(F32)
    middle = rest.astype(BF16)
    return high, middle, (rest - middle.astype(F32)).astype(BF16)


def accumulate_kernel(groups, start, local, after, table_ref, h_ref, *refs):
    refs = list(refs)
    before = None if start else refs.pop(0)
    atoms, mine = (refs.pop(0), refs.pop(0)) if local else (None, None)
    parts = [refs.pop(0) for _ in groups]
    if after:
        refs.pop(0)
    out_ref, token_ref, both, dense, wide, table, sem = refs[:7]
    token_ref[...] = jnp.zeros_like(token_ref)
    copy = pltpu.make_async_copy(table_ref, table, sem)
    copy.start()
    row = lax.axis_index("row")
    y, z, core = row // 16, row // 2 % 8, row % 2
    direction = 1 - 2 * core
    both[2 * PACK :, :] = jnp.zeros((BS, 128), BF16)
    tiles = []
    for steps, flip in groups:
        for j in range(2):
            tiles.append(((y + j) % 2 * 8 + (z + steps * direction + 8) % 8) * 2 + (core + flip) % 2)
    for at, tile in enumerate(tiles):
        wide[:, at * 256 : at * 256 + 256] = h_ref[tile]
    copy.wait()
    for g, part in enumerate(parts):

        def one(j, _, part=part, g=g):
            tile = jnp.where(j == 0, tiles[2 * g], tiles[2 * g + 1])
            packed = part[pl.ds(pl.multiple_of(j * PACK, PACK), PACK), :]
            base = pl.multiple_of((2 * g + j) * 256, 256)

            def store(r, c, block):
                dense[pl.ds(base + r * BS, BS), c * 128 : c * 128 + 128] = block

            spread_tile(packed, lambda r, c: table[tile, r * 16 + c], both, store)
            return 0

        lax.fori_loop(0, 2, one, 0)
    if local:
        own, held = refs[7], refs[8]

        def store(r, c, block):
            own[r * BS : r * BS + BS, c * 128 : c * 128 + 128] = block

        spread_tile(mine[0:PACK, :], lambda r, c: table[row, r * 16 + c], both, store)
        values = atoms[...]
        lane_atom = lax.broadcasted_iota(jnp.int32, (256, 128), 1) // 4
        row_atom = lax.broadcasted_iota(jnp.int32, (256, 128), 0) // 8
        tall = [
            jnp.where(
                lane_atom == row_atom,
                jnp.concatenate([values[8 * b : 8 * b + 8, :]] * 32, axis=0),
                0.0,
            )
            for b in range(2)
        ]
        q = lax.broadcasted_iota(jnp.int32, (256, 256), 0)
        m = lax.broadcasted_iota(jnp.int32, (256, 256), 1)
        place = q % 128 // 4 * 8 + q // 128 * 4 + q % 4
        chosen = jnp.where(place == m, 1.0, 0.0).astype(BF16)
        for k, t in enumerate(split3(jnp.concatenate(tall, axis=1))):
            held[k] = jnp.dot(t, chosen, preferred_element_type=F32).astype(BF16)

    def column(n, _):
        lanes = pl.ds(pl.multiple_of(n * 256, 256), 256)
        total = jnp.dot(wide[...], dense[:, lanes], preferred_element_type=F32)
        if local:
            for k in range(3):
                total += jnp.dot(held[k], own[:, lanes], preferred_element_type=F32)
        if before is not None:
            total += before[:, lanes]
        out_ref[:, lanes] = total
        return 0

    lax.fori_loop(0, 4, column, 0)


def accumulate(table, h_dense, before, parts, groups, local=(), after=None):
    vmem = pl.BlockSpec(memory_space=pltpu.VMEM)
    operands = [h_dense]
    if before is not None:
        operands.append(before)
    operands += list(local) + parts
    specs = [pl.BlockSpec(memory_space=pl.ANY)] + [vmem] * len(operands)
    if after is not None:
        operands.append(after)
        specs.append(pl.BlockSpec(memory_space=pl.ANY))
    depth = 512 * len(groups)
    scratch = [
        pltpu.VMEM((2 * PACK + BS, 128), BF16),
        pltpu.VMEM((depth, 1024), BF16),
        pltpu.VMEM((256, depth), BF16),
        pltpu.SMEM((32, 64), jnp.int32),
        pltpu.SemaphoreType.DMA,
    ]
    if local:
        scratch += [pltpu.VMEM((256, 1024), BF16), pltpu.VMEM((3, 256, 256), BF16)]
    return pl.pallas_call(
        functools.partial(accumulate_kernel, groups, before is None, bool(local), after is not None),
        out_shape=(jax.ShapeDtypeStruct((256, 1024), F32), jax.ShapeDtypeStruct((8, 128), F32)),
        in_specs=specs,
        out_specs=(vmem, vmem),
        scratch_shapes=scratch,
        compiler_params=pltpu.CompilerParams(vmem_limit_bytes=12 * 2**20),
        cost_estimate=pl.CostEstimate(
            flops=4 * 256 * 512 * 1024 * len(groups), bytes_accessed=4 * 2**20 * len(groups), transcendentals=0
        ),
    )(table, *operands)


def tie(buffer, token):
    anywhere = pl.BlockSpec(memory_space=pl.ANY)

    def kernel(buffer_ref, token_ref, out_ref):
        pass

    return pl.pallas_call(
        kernel,
        out_shape=jax.ShapeDtypeStruct(buffer.shape, buffer.dtype),
        in_specs=[anywhere, anywhere],
        out_specs=anywhere,
        input_output_aliases={0: 0},
        compiler_params=pltpu.CompilerParams(vmem_limit_bytes=2**20),
        cost_estimate=pl.CostEstimate(flops=0, bytes_accessed=0, transcendentals=0),
    )(buffer, token)


def hermite(distance):
    scaled = (distance + (0.5 - CUBE / 2.0)) * SCALE
    inside = (distance >= 0) & (distance < CUBE)
    gaussian = jnp.where(inside, jnp.exp(-0.5 * scaled * scaled), 0.0)
    return gaussian, scaled


def powers(distance):
    gaussian, scaled = hermite(distance)
    first = scaled * gaussian
    second = scaled * first
    return gaussian, first, second, scaled * second


ROWS = [(a, 2 * bh + bl) for bl in range(2) for a in range(4) for bh in range(2)]


def grid_kernel(info_ref, external_hbm, density_ref, share_ref, gx_ref, gy_ref, gz_ref, u_ref, s_ref, external_ref, sem):
    lanes = 256
    copy = pltpu.make_async_copy(external_hbm, external_ref, sem)
    copy.start()
    cell = lax.broadcasted_iota(jnp.int32, (CUBE, lanes), 0).astype(F32)
    place = lax.broadcasted_iota(jnp.int32, (1, lanes), 1)
    off_x = info_ref[16:17, :] + CUBE * (place // 48 - 1).astype(F32)
    off_y = info_ref[17:18, :] + CUBE * (place % 48 // 16 - 1).astype(F32)
    off_z = info_ref[18:19, :]
    for n, value in enumerate(powers(cell - off_x + CUBE // 2)):
        gx_ref[n] = value
    for n, value in enumerate(powers(cell - off_y + CUBE // 2)):
        gy_ref[n] = value
    deep = lax.broadcasted_iota(jnp.int32, (128, lanes), 0).astype(F32)
    away = deep - off_z + CUBE // 2
    away = jnp.where(away < 0, away + 128.0, away)
    away = jnp.where(away >= 128, away - 128.0, away)
    kinds = powers(away)
    e = lax.broadcasted_iota(jnp.int32, (128, lanes), 1) % 4
    gz_ref[...] = jnp.where(e == 0, kinds[0], jnp.where(e == 1, kinds[1], jnp.where(e == 2, kinds[2], kinds[3])))
    for b in range(4):
        total = None
        for a in range(4):
            at = ROWS.index((a, b))
            term = info_ref[at : at + 1, :] * gx_ref[a]
            total = term if total is None else total + term
        u_ref[b] = total
    s_ref[...] = jnp.zeros_like(s_ref)
    gz = gz_ref[...]
    chunk = 8
    copy.wait()

    def step(i, _):
        planes = []
        x0 = pl.multiple_of(i * chunk, chunk)
        rows_u = [u_ref[b, pl.ds(x0, chunk), :] for b in range(4)]
        rows_g = [gx_ref[a, pl.ds(x0, chunk), :] for a in range(4)]
        for x in range(chunk):
            plane = None
            for b in range(4):
                term = rows_u[b][x : x + 1, :] * gy_ref[b]
                plane = term if plane is None else plane + term
            planes.append(plane)
        spread = jnp.concatenate(planes, axis=0)
        density = lax.dot_general(
            spread, gz, (((1,), (1,)), ((), ())), precision=PRECISE, preferred_element_type=F32
        )
        density = density.reshape(chunk, CUBE, 128)
        density_ref[pl.ds(x0, chunk)] = density
        potential = external_ref[pl.ds(x0, chunk)] + jnp.tanh(density)
        along = jnp.dot(
            potential.reshape(chunk * CUBE, 128), gz, precision=PRECISE, preferred_element_type=F32
        )
        for a in range(4):
            total = None
            for x in range(chunk):
                term = along[x * CUBE : (x + 1) * CUBE, :] * rows_g[a][x : x + 1, :]
                total = term if total is None else total + term
            s_ref[a] += total
        return 0

    lax.fori_loop(0, CUBE // chunk, step, 0)
    for at, (a, b) in enumerate(ROWS):
        share_ref[at : at + 1, :] = (
            jnp.sum(s_ref[a] * gy_ref[b], axis=0, keepdims=True) * SCALE**3
        )


def grid_part(info, external):
    vmem = pl.BlockSpec(memory_space=pltpu.VMEM)
    return pl.pallas_call(
        grid_kernel,
        out_shape=(
            jax.ShapeDtypeStruct(external.shape, F32),
            jax.ShapeDtypeStruct((16, 256), F32),
        ),
        in_specs=[vmem, pl.BlockSpec(memory_space=pltpu.HBM)],
        out_specs=(vmem, vmem),
        scratch_shapes=[
            pltpu.VMEM((4, CUBE, 256), F32),
            pltpu.VMEM((4, CUBE, 256), F32),
            pltpu.VMEM((128, 256), F32),
            pltpu.VMEM((4, CUBE, 256), F32),
            pltpu.VMEM((4, CUBE, 256), F32),
            pltpu.VMEM(external.shape, F32),
            pltpu.SemaphoreType.DMA,
        ],
        compiler_params=pltpu.CompilerParams(vmem_limit_bytes=12 * 2**20),
        cost_estimate=pl.CostEstimate(
            flops=2 * 2 * 6 * 1024 * 256 * 128, bytes_accessed=2 * 2**20, transcendentals=2**18
        ),
    )(info, external)


def collect_kernel(near_ref, next_ref, last_ref, far_ref, atoms_ref, mine_ref):
    col = lax.axis_index("col")
    y, x = col // 4, col % 4
    total = jnp.zeros((16, 128), F32)
    for ref, dx in ((near_ref, 0), (next_ref, 1), (last_ref, 3), (far_ref, 2)):
        for j in range(2):
            source = (y + j) % 2 * 4 + (x + dx) % 4
            total += pltpu.roll(ref[16 * j : 16 * j + 16, :], (source + 7) % 8 * 16, 1)
    atoms_ref[...] = total
    mine = pltpu.roll(total, (8 - col) % 8 * 16, 1)
    lane = lax.broadcasted_iota(jnp.int32, (16, 128), 1)
    l = lax.broadcasted_iota(jnp.int32, (128, 64), 0)
    m = lax.broadcasted_iota(jnp.int32, (128, 64), 1)
    move = jnp.where(l % 4 == m % 4, 1.0, 0.0)
    rho = lax.broadcasted_iota(jnp.int32, (16, 64), 0)
    match = lax.broadcasted_iota(jnp.int32, (16, 64), 1) // 4 == rho % 8 // 2 * 4 + rho % 2 * 2 + rho // 8
    for i in range(4):
        value = jnp.dot(
            jnp.where(lane // 4 == i, mine, 0.0), move, precision=PRECISE, preferred_element_type=F32
        )
        mine_ref[i : i + 1, :] = jnp.sum(jnp.where(match, value, 0.0), axis=0, keepdims=True)


def collect(parts):
    vmem = pl.BlockSpec(memory_space=pltpu.VMEM)
    return pl.pallas_call(
        collect_kernel,
        out_shape=(jax.ShapeDtypeStruct((16, 128), F32), jax.ShapeDtypeStruct((4, 64), F32)),
        in_specs=[vmem] * 4,
        out_specs=(vmem, vmem),
        compiler_params=pltpu.CompilerParams(vmem_limit_bytes=2 * 2**20),
        cost_estimate=pl.CostEstimate(flops=0, bytes_accessed=2**17, transcendentals=0),
    )(*parts)


def row_of(y, z, core):
    return (y % 2 * 8 + z % 8) * 2 + core % 2


SITES = [(y, z, core) for y in range(2) for z in range(8) for core in range(2)]
ACROSS_Y = [(row_of(*s), row_of(s[0] + 1, s[1], s[2])) for s in SITES]
ACROSS_CORES = [(row_of(*s), row_of(s[0], s[1], s[2] + 1)) for s in SITES]
ALONG_Z = [(row_of(*s), row_of(s[0], s[1] + 1 - 2 * s[2], s[2])) for s in SITES]
COLS = [(y, x) for y in range(2) for x in range(4)]


def col_pairs(dy, dx):
    return [(y * 4 + x, (y + dy) % 2 * 4 + (x + dx) % 4) for y, x in COLS]


ALONG_X = [
    (r * 8 + y * 4 + x, r * 8 + y * 4 + (x + 1 - 2 * (r % 2)) % 4) for r in range(32) for y, x in COLS
]


def ring(axis, size, step):
    return [(i, (i + step) % size) for i in range(size)]


def from_neighbours(last, first, axis, size):
    before = lax.ppermute(last, axis, ring(axis, size, 1))
    after = lax.ppermute(first, axis, ring(axis, size, -1))
    return before, after


def on_device(coefficients, off_x, off_y, off_z, external, pattern, hamiltonian, density_matrix):
    core = lax.axis_index("row") % 2
    hp, pp, info = pack(
        pattern, hamiltonian, density_matrix, coefficients, off_x, off_y, off_z
    )
    table_p, table_h = tile_tables(pattern, info)

    before, after = from_neighbours(info, info, "col", 8)
    info = jnp.concatenate([before, info, after], axis=1)
    before, after = from_neighbours(info, info, "row", 32)
    info = jnp.concatenate([before, info, after, jnp.zeros((24, 112), F32)], axis=1)
    density, share9 = grid_part(info, external)
    share = share9
    before, after = from_neighbours(share[:, 96:144], share[:, 0:48], "row", 32)
    share = share[:, 48:96] + before + after
    share = jnp.concatenate([share, jnp.zeros((16, 80), F32)], axis=1)
    other = lax.ppermute(share, "col", col_pairs(1, 0))
    share = jnp.concatenate([share, other], axis=0)
    shares = [share] + [lax.ppermute(share, "col", col_pairs(0, d)) for d in (3, 1, 2)]
    atoms, integrals = collect(shares)

    hy = lax.ppermute(hp, "col", col_pairs(1, 0))
    h0 = jnp.concatenate([hp, hy], axis=0)
    h_next = lax.ppermute(h0, "col", col_pairs(0, 3))
    h_last = lax.ppermute(h0, "col", col_pairs(0, 1))
    h_far = lax.ppermute(jnp.where(core == 0, h_last, h_next), ("row", "col"), ALONG_X)
    h_dense = spread_hamiltonian(table_h, [h0, h_next, h_last, h_far])

    py = lax.ppermute(pp, "row", ACROSS_Y)
    m = jnp.concatenate([pp, py], axis=0)
    mc = lax.ppermute(m, "row", ACROSS_CORES)

    def step(chain):
        chain = lax.ppermute(chain, "row", ALONG_Z)
        return chain, lax.ppermute(chain, "row", ACROSS_CORES)

    def groups(s):
        return ((-s, 0), (-s, 1), (s, 1), (s, 0))

    m1, x1 = step(m)
    c1, xc1 = step(mc)
    m2, x2 = step(m1)
    c2 = lax.ppermute(c1, "row", ALONG_Z)
    product, done = accumulate(
        table_p,
        h_dense,
        None,
        [m, mc, m1, c1, x1, xc1],
        ((0, 0), (0, 1)) + groups(1),
        after=share9,
    )
    c2 = tie(c2, done)
    xc2 = lax.ppermute(c2, "row", ACROSS_CORES)
    c3, xc3 = step(c2)
    m3 = lax.ppermute(m2, "row", ALONG_Z)
    product, done = accumulate(
        table_p, h_dense, product, [m2, c2, x2, xc2], groups(2), after=share
    )
    m3 = tie(m3, done)
    x3 = lax.ppermute(m3, "row", ACROSS_CORES)
    m4, x4 = step(m3)
    product, _ = accumulate(
        table_p, h_dense, product, [m3, c3, x3, xc3], groups(3), local=(atoms, pp)
    )
    product, _ = accumulate(table_p, h_dense, product, [m4, x4], ((4, 0), (4, 1)))
    return (density, integrals, product)


def solution(mesh):
    return jax.shard_map(
        on_device,
        mesh=mesh,
        in_specs=(
            P(("row", "col"), None),
            P(("row", "col")),
            P(("row", "col")),
            P(("row", "col")),
            P("row", "col", None),
            P(),
            P("row", "col"),
            P("row", "col"),
        ),
        out_specs=(P("row", "col", None), P(("row", "col"), None), P("row", "col")),
        check_vma=False,
    )
```

time: 125 us -> 127 us (1.016)
  local copies, waits for them, and re-layouts: 23.2 us -> 5.39 us
  waiting for transfers between devices: 20.7 us -> 33.7 us
  starting transfers between devices: 45.1 us -> 48.7 us
  Pallas kernels: 32.2 us -> 35 us
    unnamed x38 -> x10, local copies, waits for them, and re-layouts: 11.1 us -> 4.47 us
    reshape x9 -> x0, local copies, waits for them, and re-layouts: 6.65 us -> none  [the longest x2 2.82 us: on_device(): mine[:, :16].reshape(2, 4, 2, 4, 4).transpose(3, 1, 2, 0, 4).reshape(4, 64)]
    ppermute x3, waiting for transfers between devices: 0.01 us -> 5.61 us  [from_neighbours(): after = lax.ppermute(first, axis, ring(axis, size, -1))]
    ppermute x3, waiting for transfers between devices: 0.54 us -> 5.95 us  [from_neighbours(): before = lax.ppermute(last, axis, ring(axis, size, 1))]
    ppermute x3, waiting for transfers between devices: 8.69 us -> 3.55 us  [on_device(): lax.ppermute(share, 'col', col_pairs(0, d))]
    ppermute x1, waiting for transfers between devices: 0.01 us -> 3.69 us  [on_device(): h_last = lax.ppermute(h0, 'col', col_pairs(0, 1))]
    ppermute x3, starting transfers between devices: 6.31 us -> 3.23 us  [from_neighbours(): after = lax.ppermute(first, axis, ring(axis, size, -1))]
    ppermute x1, waiting for transfers between devices: 4.24 us -> 6.84 us  [on_device(): py = lax.ppermute(pp, 'row', ACROSS_Y)]
  transfers between devices with their start and end apart: 30 -> 30, of which waited for: 8 -> 14; matrix products, arithmetic and copies ran while one was open for 10% -> 4% of each run, Pallas kernels for 23% -> 22%
where the time goes in v2:
time: 127 us; the launch traced here: 125 us
  starting transfers between devices  48.7 us (38%)
  Pallas kernels  35 us (28%)
  waiting for transfers between devices  33.7 us (27%)
  local copies, waits for them, and re-layouts  5.39 us (4%)
  other arithmetic  1.65 us (1%)
    pallas_call x4, Pallas kernels, accumulate(): pl.pallas_call(functools.partial(accumulate_kernel, groups, before is Non...  22.7 us
    ppermute x5, starting transfers between devices, step(): chain = lax.ppermute(chain, 'row', ALONG_Z)  14.5 us
    ppermute x1, waiting for transfers between devices, on_device(): py = lax.ppermute(pp, 'row', ACROSS_Y)  6.84 us
    ppermute x1, starting transfers between devices, on_device(): c2 = lax.ppermute(c1, 'row', ALONG_Z)  6.18 us
    ppermute x3, waiting for transfers between devices, from_neighbours(): before = lax.ppermute(last, axis, ring(axis, size, 1))  5.95 us
    ppermute x5, waiting for transfers between devices, step(): chain = lax.ppermute(chain, 'row', ALONG_Z)  5.81 us
    ppermute x3, waiting for transfers between devices, from_neighbours(): after = lax.ppermute(first, axis, ring(axis, size, -1))  5.61 us
    ppermute x3, starting transfers between devices, from_neighbours(): before = lax.ppermute(last, axis, ring(axis, size, 1))  5.44 us
  transfers between devices with their start and end apart: 30, of which 14 were waited for; matrix products, arithmetic and copies ran while one was open for 4% of the time, Pallas kernels for 22%

profile of v2, /device:TPU:1, one launch (start us, length us, event | category | flops | bytes accessed | tf_op | source)
XLA Modules:
  0.0 125.4 jit_solution(3978682244564636851)
XLA Ops:
  0.6 2.7 %shard_map.103 = (bf16[768,128]{1,0:T(8,128)(2,1)}, bf16[768,128]{1,0:T(8,128)(2,1)}, f32[24,16]{1,0:T(8,128)}) custom-call(s32[128,128]{1,0:T(8,128)} %pattern_ref.1, bf16[256,1024]{1,0:T(8,128)(2,1)} %h_hbm.1, bf16[256,1024]{1,0:T(8,128)(2,1)} %p_hbm.1, f32[4,64]{1,0:T(4,128)} %coef_hbm.1, s32[4]{0:T(128)} %x_hbm.1, s32[4]{0:T(128)} %y_hbm.1, s32[4]{0:T(128)} %z_hbm.1), custom_call_target="tpu_custom_call" | custom-call | bytes 6291456 | tf_op jit(solution)/shard_map/pallas_call | solution.py:96
  3.4 3.8 %collective-permute-start.10 = (bf16[768,128]{1,0:T(8,128)(2,1)}, bf16[768,128]{1,0:T(8,128)(2,1)S(1)}, u32[]{:S(2)}, u32[]{:S(2)}) collective-permute-start(bf16[768,128]{1,0:T(8,128)(2,1)} %get-tuple-element.24), channel_id=1, source_target_pairs={{0,4},{1,5},{2,6},{3,7},{4,0},{5,1},{6,2},{7,3},{8,12},{9,13},{10,... | collective-permute-start | bytes 589832 | tf_op jit(solution)/shard_map/ppermute | solution.py:550
  7.2 0.4 collective-permute-start.14
  7.6 0.9 constant_dynamic-update-slice_fusion.1
  8.5 0.9 constant_dynamic-update-slice_fusion.3
  9.5 6.8 %collective-permute-done.14 = bf16[768,128]{1,0:T(8,128)(2,1)S(1)} collective-permute-done((bf16[768,128]{1,0:T(8,128)(2,1)}, bf16[768,128]{1,0:T(8,128)(2,1)S(1)}, u32[]{:S(2)}, u32[]{:S(2)}) %collective-permute-start.14) | collective-permute-done | bytes 196640 | tf_op jit(solution)/shard_map/ppermute | solution.py:557
  16.3 1.6 %collective-permute-start.15 = (bf16[1536,128]{1,0:T(8,128)(2,1)S(1)}, bf16[1536,128]{1,0:T(8,128)(2,1)S(1)}, u32[]{:S(2)}, u32[]{:S(2)}) collective-permute-start(bf16[1536,128]{1,0:T(8,128)(2,1)S(1)} %constant_dynamic-update-slice_fusion.2.refs_0_), channel_id=1, source_target_pairs={{0,8},{8,0},{16,24},{24,16},{32,40},{40,32},{48,56},{56,48},{64,72... | collective-permute-start | bytes 1179656 | tf_op jit(solution)/shard_map/ppermute | solution.py:559
  18.0 5.6 %collective-permute-start.16 = (bf16[1536,128]{1,0:T(8,128)(2,1)S(1)}, bf16[1536,128]{1,0:T(8,128)(2,1)}, u32[]{:S(2)}, u32[]{:S(2)}) collective-permute-start(bf16[1536,128]{1,0:T(8,128)(2,1)S(1)} %constant_dynamic-update-slice_fusion.2.refs_0_), channel_id=1, source_target_pairs={{0,16},{8,120},{16,32},{24,8},{32,48},{40,24},{48,64},{56,40},{64,... | collective-permute-start | bytes 1179656 | tf_op jit(solution)/shard_map/ppermute | solution.py:562
  23.6 0.0 collective-permute-done.10
  23.6 2.6 %collective-permute-start.11 = (bf16[1536,128]{1,0:T(8,128)(2,1)S(1)}, bf16[1536,128]{1,0:T(8,128)(2,1)S(1)}, u32[]{:S(2)}, u32[]{:S(2)}) collective-permute-start(bf16[1536,128]{1,0:T(8,128)(2,1)S(1)} %constant_dynamic-update-slice_fusion.near_ref), channel_id=1, source_target_pairs={{0,3},{1,0},{2,1},{3,2},{4,7},{5,4},{6,5},{7,6},{8,11},{9,8},{10,9... | collective-permute-start | bytes 1179656 | tf_op jit(solution)/shard_map/ppermute | solution.py:552
  26.1 0.0 collective-permute-start.12
  26.1 0.0 collective-permute-done.15.refs_1_
  26.1 0.7 collective-permute-start.17
  26.9 1.4 %collective-permute-done.16.refs_2_ = bf16[1536,128]{1,0:T(8,128)(2,1)} collective-permute-done((bf16[1536,128]{1,0:T(8,128)(2,1)S(1)}, bf16[1536,128]{1,0:T(8,128)(2,1)}, u32[]{:S(2)}, u32[]{:S(2)}) %collective-permute-start.16) | collective-permute-done | bytes 393248 | tf_op jit(solution)/shard_map/ppermute | solution.py:562
  28.3 3.4 %collective-permute-start.20 = (bf16[1536,128]{1,0:T(8,128)(2,1)}, bf16[1536,128]{1,0:T(8,128)(2,1)S(1)}, u32[]{:S(2)}, u32[]{:S(2)}) collective-permute-start(bf16[1536,128]{1,0:T(8,128)(2,1)} %collective-permute-done.16.refs_2_), channel_id=1, source_target_pairs={{0,16},{8,120},{16,32},{24,8},{32,48},{40,24},{48,64},{56,40},{64,... | collective-permute-start | bytes 1179656 | tf_op jit(solution)/shard_map/ppermute | solution.py:562
  31.7 0.3 collective-permute-done.11.next_ref
  32.0 3.7 %collective-permute-done.12.last_ref = bf16[1536,128]{1,0:T(8,128)(2,1)S(1)} collective-permute-done((bf16[1536,128]{1,0:T(8,128)(2,1)S(1)}, bf16[1536,128]{1,0:T(8,128)(2,1)S(1)}, u32[]{:S(2)}, u32[]{:S(2)}) %collective-permute-start.12) | collective-permute-done | bytes 393248 | tf_op jit(solution)/shard_map/ppermute | solution.py:553
  35.7 0.8 broadcast_select_fusion
  36.5 0.0 collective-permute-done.17.refs_3_
  36.5 0.5 collective-permute-start.19
  37.0 1.5 %collective-permute-start = (f32[24,16]{1,0:T(8,128)}, f32[24,16]{1,0:T(8,128)S(1)}, u32[]{:S(2)}, u32[]{:S(2)}) collective-permute-start(f32[24,16]{1,0:T(8,128)} %get-tuple-element.18._), channel_id=1, source_target_pairs={{0,1},{1,2},{2,3},{3,4},{4,5},{5,6},{6,7},{7,0},{8,9},{9,10},{10,1... | collective-permute-start | bytes 4616 | tf_op jit(solution)/shard_map/ppermute | solution.py:524
  38.4 5.1 %collective-permute-done = f32[24,16]{1,0:T(8,128)S(1)} collective-permute-done((f32[24,16]{1,0:T(8,128)}, f32[24,16]{1,0:T(8,128)S(1)}, u32[]{:S(2)}, u32[]{:S(2)}) %collective-permute-start) | collective-permute-done | bytes 1568 | tf_op jit(solution)/shard_map/ppermute | solution.py:524
  43.5 0.0 collective-permute-start.1
  43.5 2.8 %collective-permute-done.1 = f32[24,16]{1,0:T(8,128)S(1)} collective-permute-done((f32[24,16]{1,0:T(8,128)}, f32[24,16]{1,0:T(8,128)S(1)}, u32[]{:S(2)}, u32[]{:S(2)}) %collective-permute-start.1) | collective-permute-done | bytes 1568 | tf_op jit(solution)/shard_map/ppermute | solution.py:525
  46.3 0.8 pad_maximum_fusion.1
  47.1 4.0 %collective-permute-start.2 = (f32[24,48]{1,0:T(8,128)S(1)}, f32[24,48]{1,0:T(8,128)S(1)}, u32[]{:S(2)}, u32[]{:S(2)}) collective-permute-start(f32[24,48]{1,0:T(8,128)S(1)} %pad_maximum_fusion.1), channel_id=1, source_target_pairs={{0,8},{8,16},{16,24},{24,32},{32,40},{40,48},{48,56},{56,64},{64,7... | collective-permute-start | bytes 13832 | tf_op jit(solution)/shard_map/ppermute | solution.py:524
  51.1 0.8 collective-permute-done.2
  51.9 2.7 %collective-permute-start.3 = (f32[24,48]{1,0:T(8,128)S(1)}, f32[24,48]{1,0:T(8,128)S(1)}, u32[]{:S(2)}, u32[]{:S(2)}) collective-permute-start(f32[24,48]{1,0:T(8,128)S(1)} %pad_maximum_fusion.1), channel_id=1, source_target_pairs={{0,248},{8,0},{16,8},{24,16},{32,24},{40,32},{48,40},{56,48},{64,5... | collective-permute-start | bytes 13832 | tf_op jit(solution)/shard_map/ppermute | solution.py:525
  54.6 0.9 collective-permute-done.3
  55.6 6.2 %collective-permute-start.21 = (bf16[1536,128]{1,0:T(8,128)(2,1)}, bf16[1536,128]{1,0:T(8,128)(2,1)S(1)}, u32[]{:S(2)}, u32[]{:S(2)}) collective-permute-start(bf16[1536,128]{1,0:T(8,128)(2,1)} %collective-permute-done.17.refs_3_), channel_id=1, source_target_pairs={{0,16},{8,120},{16,32},{24,8},{32,48},{40,24},{48,64},{56,40},{64,... | collective-permute-start | bytes 1179656 | tf_op jit(solution)/shard_map/ppermute | solution.py:571
  61.8 0.8 copy-done
  62.6 0.7 copy-done.2
  63.3 0.5 shard_map.106
  63.8 0.8 concatenate.20.info_ref
  64.6 0.0 copy-start.3
  64.6 1.0 copy-done.3
  65.6 4.8 %shard_map.104 = (f32[32,32,128]{2,1,0:T(8,128)}, f32[16,256]{1,0:T(8,128)S(1)}) custom-call(f32[24,256]{1,0:T(8,128)S(1)} %concatenate.20.info_ref, f32[32,32,128]{2,1,0:T(8,128)S(1)} %copy-done.3), custom_call_target="tpu_custom_call" | custom-call | flops 805306368 | bytes 2097152 | tf_op jit(solution)/shard_map/pallas_call | solution.py:440
  70.5 0.0 collective-permute-done.20.refs_1_
  70.5 0.1 collective-permute-start.22
  70.6 3.1 %shard_map.107.h_ref = bf16[32,256,256]{2,1,0:T(8,128)(2,1)S(1)} custom-call(s32[8,128]{1,0:T(8,128)S(1)} %get-tuple-element.23.table_ref, bf16[1536,128]{1,0:T(8,128)(2,1)S(1)} %constant_dynamic-update-slice_fusion.near_ref, bf16[1536,128]{1,0:T(8,128)(2,1)S(1)} %collective-permute-done.11.next_ref, bf16[1536,128]{1,0:T(8,128)(2,1)S(1)} %collective-permute-done.12.last_ref, ...), custom_call_target="tpu_custom_call" | custom-call | bytes 8388608 | tf_op jit(solution)/shard_map/pallas_call | solution.py:210
  73.7 7.9 %shard_map.108 = (f32[256,1024]{1,0:T(8,128)S(1)}, f32[8,128]{1,0:T(8,128)S(1)}) custom-call(s32[32,64]{1,0:T(8,128)S(1)} %get-tuple-element.22.table_ref, bf16[32,256,256]{2,1,0:T(8,128)(2,1)S(1)} %shard_map.107.h_ref, bf16[1536,128]{1,0:T(8,128)(2,1)S(1)} %constant_dynamic-update-slice_fusion.2.refs_0_, ...), custom_call_target="tpu_custom_call" | custom-call | flops 3221225472 | bytes 25165824 | tf_op jit(solution)/shard_map/pallas_call | solution.py:323
  81.7 0.6 collective-permute-start.23
  82.3 0.1 fusion
  82.3 0.5 collective-permute-start.5
  82.8 0.8 collective-permute-start.24
  83.6 1.9 %collective-permute-done.5 = f32[16,48]{1,0:T(8,128)S(1)} collective-permute-done((f32[16,48]{1,0:T(8,128)S(1)}, f32[16,48]{1,0:T(8,128)S(1)}, u32[]{:S(2)}, u32[]{:S(2)}) %collective-permute-start.5) | collective-permute-done | bytes 3104 | tf_op jit(solution)/shard_map/ppermute | solution.py:525
  85.5 0.1 add_add_fusion
  85.6 2.1 %collective-permute-start.6 = (f32[16,128]{1,0:T(8,128)S(1)}, f32[16,128]{1,0:T(8,128)S(1)}, u32[]{:S(2)}, u32[]{:S(2)}) collective-permute-start(f32[16,128]{1,0:T(8,128)S(1)} %concatenate.21), channel_id=1, source_target_pairs={{0,4},{1,5},{2,6},{3,7},{4,0},{5,1},{6,2},{7,3},{8,12},{9,13},{10,... | collective-permute-start | bytes 24584 | tf_op jit(solution)/shard_map/ppermute | solution.py:545
  87.7 1.9 %collective-permute-done.6 = f32[16,128]{1,0:T(8,128)S(1)} collective-permute-done((f32[16,128]{1,0:T(8,128)S(1)}, f32[16,128]{1,0:T(8,128)S(1)}, u32[]{:S(2)}, u32[]{:S(2)}) %collective-permute-start.6) | collective-permute-done | bytes 8224 | tf_op jit(solution)/shard_map/ppermute | solution.py:545
  89.6 4.4 %collective-permute-start.25 = (bf16[1536,128]{1,0:T(8,128)(2,1)S(1)}, bf16[1536,128]{1,0:T(8,128)(2,1)S(1)}, u32[]{:S(2)}, u32[]{:S(2)}) collective-permute-start(bf16[1536,128]{1,0:T(8,128)(2,1)S(1)} %shard_map.109.refs_2_), channel_id=1, source_target_pairs={{0,16},{8,120},{16,32},{24,8},{32,48},{40,24},{48,64},{56,40},{64,... | collective-permute-start | bytes 1179656 | tf_op jit(solution)/shard_map/ppermute | solution.py:562
  94.1 4.9 %shard_map.110 = (f32[256,1024]{1,0:T(8,128)S(1)}, f32[8,128]{1,0:T(8,128)S(1)}) custom-call(s32[32,64]{1,0:T(8,128)S(1)} %get-tuple-element.22.table_ref, bf16[32,256,256]{2,1,0:T(8,128)(2,1)S(1)} %shard_map.107.h_ref, f32[256,1024]{1,0:T(8,128)S(1)} %get-tuple-element.26.refs_0_, bf16[1536,128]{1,0:T(8,128)(2,1)S(1)} %collective-permute-done.20.refs_1_, ...), custom_call_target="tpu_custom_call" | custom-call | flops 2147483648 | bytes 16777216 | tf_op jit(solution)/shard_map/pallas_call | solution.py:323
  99.0 0.3 collective-permute-start.28
  99.4 0.1 collective-permute-start.26
  99.5 2.4 %collective-permute-start.27 = (bf16[1536,128]{1,0:T(8,128)(2,1)S(1)}, bf16[1536,128]{1,0:T(8,128)(2,1)S(1)}, u32[]{:S(2)}, u32[]{:S(2)}) collective-permute-start(bf16[1536,128]{1,0:T(8,128)(2,1)S(1)} %collective-permute-done.25.refs_4_), channel_id=1, source_target_pairs={{0,8},{8,0},{16,24},{24,16},{32,40},{40,32},{48,56},{56,48},{64,72... | collective-permute-start | bytes 1179656 | tf_op jit(solution)/shard_map/ppermute | solution.py:563
  101.9 4.4 %collective-permute-done.28.refs_1_ = bf16[1536,128]{1,0:T(8,128)(2,1)S(1)} collective-permute-done((bf16[1536,128]{1,0:T(8,128)(2,1)S(1)}, bf16[1536,128]{1,0:T(8,128)(2,1)S(1)}, u32[]{:S(2)}, u32[]{:S(2)}) %collective-permute-start.28) | collective-permute-done | bytes 393248 | tf_op jit(solution)/shard_map/ppermute | solution.py:562
  106.3 0.9 collective-permute-start.29
  107.1 2.1 %collective-permute-start.7 = (f32[32,128]{1,0:T(8,128)S(1)}, f32[32,128]{1,0:T(8,128)S(1)}, u32[]{:S(2)}, u32[]{:S(2)}) collective-permute-start(f32[32,128]{1,0:T(8,128)S(1)} %pad_maximum_fusion.near_ref.refs_5_), channel_id=1, source_target_pairs={{0,3},{1,0},{2,1},{3,2},{4,7},{5,4},{6,5},{7,6},{8,11},{9,8},{10,9... | collective-permute-start | bytes 49160 | tf_op jit(solution)/shard_map/ppermute | solution.py:547
  109.2 0.9 collective-permute-done.7.next_ref
  110.0 1.4 %collective-permute-start.9 = (f32[32,128]{1,0:T(8,128)S(1)}, f32[32,128]{1,0:T(8,128)S(1)}, u32[]{:S(2)}, u32[]{:S(2)}) collective-permute-start(f32[32,128]{1,0:T(8,128)S(1)} %pad_maximum_fusion.near_ref.refs_5_), channel_id=1, source_target_pairs={{0,2},{1,3},{2,0},{3,1},{4,6},{5,7},{6,4},{7,5},{8,10},{9,11},{10,... | collective-permute-start | bytes 49160 | tf_op jit(solution)/shard_map/ppermute | solution.py:547
  111.5 1.5 %collective-permute-done.8.last_ref = f32[32,128]{1,0:T(8,128)S(1)} collective-permute-done((f32[32,128]{1,0:T(8,128)S(1)}, f32[32,128]{1,0:T(8,128)S(1)}, u32[]{:S(2)}, u32[]{:S(2)}) %collective-permute-start.8) | collective-permute-done | bytes 16416 | tf_op jit(solution)/shard_map/ppermute | solution.py:547
  113.0 1.2 collective-permute-done.9.far_ref
  114.2 1.1 shard_map.105
  115.3 5.8 %shard_map.112 = (f32[256,1024]{1,0:T(8,128)S(1)}, f32[8,128]{1,0:T(8,128)}) custom-call(s32[32,64]{1,0:T(8,128)S(1)} %get-tuple-element.22.table_ref, bf16[32,256,256]{2,1,0:T(8,128)(2,1)S(1)} %shard_map.107.h_ref, f32[256,1024]{1,0:T(8,128)S(1)} %get-tuple-element.28.refs_0_, f32[16,128]{1,0:T(8,128)S(1)} %get-tuple-element.29.refs_1_, ...), custom_call_target="tpu_custom_call" | custom-call | flops 2147483648 | bytes 16777216 | tf_op jit(solution)/shard_map/pallas_call | solution.py:323
  121.0 4.2 %shard_map.113 = (f32[256,1024]{1,0:T(8,128)}, f32[8,128]{1,0:T(8,128)}) custom-call(s32[32,64]{1,0:T(8,128)S(1)} %get-tuple-element.22.table_ref, bf16[32,256,256]{2,1,0:T(8,128)(2,1)S(1)} %shard_map.107.h_ref, f32[256,1024]{1,0:T(8,128)S(1)} %get-tuple-element.31.refs_0_, bf16[1536,128]{1,0:T(8,128)(2,1)S(1)} %collective-permute-done.28.refs_1_, ...), custom_call_target="tpu_custom_call" | custom-call | flops 1073741824 | bytes 8388608 | tf_op jit(solution)/shard_map/pallas_call | solution.py:323
  (27 shorter events, 0.1 us)
Async XLA Ops:
  3.4 20.2 %collective-permute-start.10 = (bf16[768,128]{1,0:T(8,128)(2,1)}, bf16[768,128]{1,0:T(8,128)(2,1)S(1)}, u32[]{:S(2)}, u32[]{:S(2)}) collective-permute-start(bf16[768,128]{1,0:T(8,128)(2,1)} %get-tuple-element.24), channel_id=1, source_target_pairs={{0,4},{1,5},{2,6},{3,7},{4,0},{5,1},{6,2},{7,3},{8,12},{9,13},{10,... | collective-permute-start | bytes 589832 | tf_op jit(solution)/shard_map/ppermute | solution.py:550
  7.2 9.1 %collective-permute-start.14 = (bf16[768,128]{1,0:T(8,128)(2,1)}, bf16[768,128]{1,0:T(8,128)(2,1)S(1)}, u32[]{:S(2)}, u32[]{:S(2)}) collective-permute-start(bf16[768,128]{1,0:T(8,128)(2,1)} %get-tuple-element.25.refs_2_), channel_id=1, source_target_pairs={{0,128},{8,136},{16,144},{24,152},{32,160},{40,168},{48,176},{56,1... | collective-permute-start | bytes 589832 | tf_op jit(solution)/shard_map/ppermute | solution.py:557
  16.3 9.8 %collective-permute-start.15 = (bf16[1536,128]{1,0:T(8,128)(2,1)S(1)}, bf16[1536,128]{1,0:T(8,128)(2,1)S(1)}, u32[]{:S(2)}, u32[]{:S(2)}) collective-permute-start(bf16[1536,128]{1,0:T(8,128)(2,1)S(1)} %constant_dynamic-update-slice_fusion.2.refs_0_), channel_id=1, source_target_pairs={{0,8},{8,0},{16,24},{24,16},{32,40},{40,32},{48,56},{56,48},{64,72... | collective-permute-start | bytes 1179656 | tf_op jit(solution)/shard_map/ppermute | solution.py:559
  18.0 10.3 %collective-permute-start.16 = (bf16[1536,128]{1,0:T(8,128)(2,1)S(1)}, bf16[1536,128]{1,0:T(8,128)(2,1)}, u32[]{:S(2)}, u32[]{:S(2)}) collective-permute-start(bf16[1536,128]{1,0:T(8,128)(2,1)S(1)} %constant_dynamic-update-slice_fusion.2.refs_0_), channel_id=1, source_target_pairs={{0,16},{8,120},{16,32},{24,8},{32,48},{40,24},{48,64},{56,40},{64,... | collective-permute-start | bytes 1179656 | tf_op jit(solution)/shard_map/ppermute | solution.py:562
  23.6 8.4 %collective-permute-start.11 = (bf16[1536,128]{1,0:T(8,128)(2,1)S(1)}, bf16[1536,128]{1,0:T(8,128)(2,1)S(1)}, u32[]{:S(2)}, u32[]{:S(2)}) collective-permute-start(bf16[1536,128]{1,0:T(8,128)(2,1)S(1)} %constant_dynamic-update-slice_fusion.near_ref), channel_id=1, source_target_pairs={{0,3},{1,0},{2,1},{3,2},{4,7},{5,4},{6,5},{7,6},{8,11},{9,8},{10,9... | collective-permute-start | bytes 1179656 | tf_op jit(solution)/shard_map/ppermute | solution.py:552
  26.1 9.5 %collective-permute-start.12 = (bf16[1536,128]{1,0:T(8,128)(2,1)S(1)}, bf16[1536,128]{1,0:T(8,128)(2,1)S(1)}, u32[]{:S(2)}, u32[]{:S(2)}) collective-permute-start(bf16[1536,128]{1,0:T(8,128)(2,1)S(1)} %constant_dynamic-update-slice_fusion.near_ref), channel_id=1, source_target_pairs={{0,1},{1,2},{2,3},{3,0},{4,5},{5,6},{6,7},{7,4},{8,9},{9,10},{10,1... | collective-permute-start | bytes 1179656 | tf_op jit(solution)/shard_map/ppermute | solution.py:553
  26.1 10.3 %collective-permute-start.17 = (bf16[1536,128]{1,0:T(8,128)(2,1)S(1)}, bf16[1536,128]{1,0:T(8,128)(2,1)}, u32[]{:S(2)}, u32[]{:S(2)}) collective-permute-start(bf16[1536,128]{1,0:T(8,128)(2,1)S(1)} %collective-permute-done.15.refs_1_), channel_id=1, source_target_pairs={{0,16},{8,120},{16,32},{24,8},{32,48},{40,24},{48,64},{56,40},{64,... | collective-permute-start | bytes 1179656 | tf_op jit(solution)/shard_map/ppermute | solution.py:562
  28.3 42.2 %collective-permute-start.20 = (bf16[1536,128]{1,0:T(8,128)(2,1)}, bf16[1536,128]{1,0:T(8,128)(2,1)S(1)}, u32[]{:S(2)}, u32[]{:S(2)}) collective-permute-start(bf16[1536,128]{1,0:T(8,128)(2,1)} %collective-permute-done.16.refs_2_), channel_id=1, source_target_pairs={{0,16},{8,120},{16,32},{24,8},{32,48},{40,24},{48,64},{56,40},{64,... | collective-permute-start | bytes 1179656 | tf_op jit(solution)/shard_map/ppermute | solution.py:562
  36.4 34.2 %collective-permute-start.13 = (bf16[1536,128]{1,0:T(8,128)(2,1)}, bf16[1536,128]{1,0:T(8,128)(2,1)S(1)}, u32[]{:S(2)}, u32[]{:S(2)}) collective-permute-start(bf16[1536,128]{1,0:T(8,128)(2,1)} %broadcast_select_fusion), channel_id=1, source_target_pairs={{0,1},{1,2},{2,3},{3,0},{4,5},{5,6},{6,7},{7,4},{8,11},{9,8},{10,9... | collective-permute-start | bytes 1179656 | tf_op jit(solution)/shard_map/ppermute | solution.py:554
  36.5 37.3 %collective-permute-start.18 = (bf16[1536,128]{1,0:T(8,128)(2,1)}, bf16[1536,128]{1,0:T(8,128)(2,1)}, u32[]{:S(2)}, u32[]{:S(2)}) collective-permute-start(bf16[1536,128]{1,0:T(8,128)(2,1)} %collective-permute-done.16.refs_2_), channel_id=1, source_target_pairs={{0,8},{8,0},{16,24},{24,16},{32,40},{40,32},{48,56},{56,48},{64,72... | collective-permute-start | bytes 1179656 | tf_op jit(solution)/shard_map/ppermute | solution.py:563
  36.5 37.3 %collective-permute-start.19 = (bf16[1536,128]{1,0:T(8,128)(2,1)}, bf16[1536,128]{1,0:T(8,128)(2,1)}, u32[]{:S(2)}, u32[]{:S(2)}) collective-permute-start(bf16[1536,128]{1,0:T(8,128)(2,1)} %collective-permute-done.17.refs_3_), channel_id=1, source_target_pairs={{0,8},{8,0},{16,24},{24,16},{32,40},{40,32},{48,56},{56,48},{64,72... | collective-permute-start | bytes 1179656 | tf_op jit(solution)/shard_map/ppermute | solution.py:563
  37.0 6.6 %collective-permute-start = (f32[24,16]{1,0:T(8,128)}, f32[24,16]{1,0:T(8,128)S(1)}, u32[]{:S(2)}, u32[]{:S(2)}) collective-permute-start(f32[24,16]{1,0:T(8,128)} %get-tuple-element.18._), channel_id=1, source_target_pairs={{0,1},{1,2},{2,3},{3,4},{4,5},{5,6},{6,7},{7,0},{8,9},{9,10},{10,1... | collective-permute-start | bytes 4616 | tf_op jit(solution)/shard_map/ppermute | solution.py:524
  43.5 2.8 %collective-permute-start.1 = (f32[24,16]{1,0:T(8,128)}, f32[24,16]{1,0:T(8,128)S(1)}, u32[]{:S(2)}, u32[]{:S(2)}) collective-permute-start(f32[24,16]{1,0:T(8,128)} %get-tuple-element.18._), channel_id=1, source_target_pairs={{0,7},{1,0},{2,1},{3,2},{4,3},{5,4},{6,5},{7,6},{8,15},{9,8},{10,9... | collective-permute-start | bytes 4616 | tf_op jit(solution)/shard_map/ppermute | solution.py:525
  47.1 4.8 %collective-permute-start.2 = (f32[24,48]{1,0:T(8,128)S(1)}, f32[24,48]{1,0:T(8,128)S(1)}, u32[]{:S(2)}, u32[]{:S(2)}) collective-permute-start(f32[24,48]{1,0:T(8,128)S(1)} %pad_maximum_fusion.1), channel_id=1, source_target_pairs={{0,8},{8,16},{16,24},{24,32},{32,40},{40,48},{48,56},{56,64},{64,7... | collective-permute-start | bytes 13832 | tf_op jit(solution)/shard_map/ppermute | solution.py:524
  51.9 3.7 %collective-permute-start.3 = (f32[24,48]{1,0:T(8,128)S(1)}, f32[24,48]{1,0:T(8,128)S(1)}, u32[]{:S(2)}, u32[]{:S(2)}) collective-permute-start(f32[24,48]{1,0:T(8,128)S(1)} %pad_maximum_fusion.1), channel_id=1, source_target_pairs={{0,248},{8,0},{16,8},{24,16},{32,24},{40,32},{48,40},{56,48},{64,5... | collective-permute-start | bytes 13832 | tf_op jit(solution)/shard_map/ppermute | solution.py:525
  55.6 26.1 %collective-permute-start.21 = (bf16[1536,128]{1,0:T(8,128)(2,1)}, bf16[1536,128]{1,0:T(8,128)(2,1)S(1)}, u32[]{:S(2)}, u32[]{:S(2)}) collective-permute-start(bf16[1536,128]{1,0:T(8,128)(2,1)} %collective-permute-done.17.refs_3_), channel_id=1, source_target_pairs={{0,16},{8,120},{16,32},{24,8},{32,48},{40,24},{48,64},{56,40},{64,... | collective-permute-start | bytes 1179656 | tf_op jit(solution)/shard_map/ppermute | solution.py:571
  61.7 0.8 copy-start
  62.6 0.7 copy-start.2
  64.6 1.0 copy-start.3
  70.5 23.6 %collective-permute-start.22 = (bf16[1536,128]{1,0:T(8,128)(2,1)S(1)}, bf16[1536,128]{1,0:T(8,128)(2,1)S(1)}, u32[]{:S(2)}, u32[]{:S(2)}) collective-permute-start(bf16[1536,128]{1,0:T(8,128)(2,1)S(1)} %collective-permute-done.20.refs_1_), channel_id=1, source_target_pairs={{0,8},{8,0},{16,24},{24,16},{32,40},{40,32},{48,56},{56,48},{64,72... | collective-permute-start | bytes 1179656 | tf_op jit(solution)/shard_map/ppermute | solution.py:563
  81.7 12.4 %collective-permute-start.23 = (bf16[1536,128]{1,0:T(8,128)(2,1)S(1)}, bf16[1536,128]{1,0:T(8,128)(2,1)S(1)}, u32[]{:S(2)}, u32[]{:S(2)}) collective-permute-start(bf16[1536,128]{1,0:T(8,128)(2,1)S(1)} %shard_map.109.refs_2_), channel_id=1, source_target_pairs={{0,8},{8,0},{16,24},{24,16},{32,40},{40,32},{48,56},{56,48},{64,72... | collective-permute-start | bytes 1179656 | tf_op jit(solution)/shard_map/ppermute | solution.py:581
  82.3 1.3 %collective-permute-start.4 = (f32[16,48]{1,0:T(8,128)S(1)}, f32[16,48]{1,0:T(8,128)S(1)}, u32[]{:S(2)}, u32[]{:S(2)}) collective-permute-start(f32[16,48]{1,0:T(8,128)S(1)} %get-tuple-element.33), channel_id=1, source_target_pairs={{0,8},{8,16},{16,24},{24,32},{32,40},{40,48},{48,56},{56,64},{64,7... | collective-permute-start | bytes 9224 | tf_op jit(solution)/shard_map/ppermute | solution.py:524
  82.3 3.2 %collective-permute-start.5 = (f32[16,48]{1,0:T(8,128)S(1)}, f32[16,48]{1,0:T(8,128)S(1)}, u32[]{:S(2)}, u32[]{:S(2)}) collective-permute-start(f32[16,48]{1,0:T(8,128)S(1)} %get-tuple-element.34), channel_id=1, source_target_pairs={{0,248},{8,0},{16,8},{24,16},{32,24},{40,32},{48,40},{56,48},{64,5... | collective-permute-start | bytes 9224 | tf_op jit(solution)/shard_map/ppermute | solution.py:525
  82.8 16.2 %collective-permute-start.24 = (bf16[1536,128]{1,0:T(8,128)(2,1)S(1)}, bf16[1536,128]{1,0:T(8,128)(2,1)S(1)}, u32[]{:S(2)}, u32[]{:S(2)}) collective-permute-start(bf16[1536,128]{1,0:T(8,128)(2,1)S(1)} %collective-permute-done.20.refs_1_), channel_id=1, source_target_pairs={{0,16},{8,120},{16,32},{24,8},{32,48},{40,24},{48,64},{56,40},{64,... | collective-permute-start | bytes 1179656 | tf_op jit(solution)/shard_map/ppermute | solution.py:583
  85.6 4.0 %collective-permute-start.6 = (f32[16,128]{1,0:T(8,128)S(1)}, f32[16,128]{1,0:T(8,128)S(1)}, u32[]{:S(2)}, u32[]{:S(2)}) collective-permute-start(f32[16,128]{1,0:T(8,128)S(1)} %concatenate.21), channel_id=1, source_target_pairs={{0,4},{1,5},{2,6},{3,7},{4,0},{5,1},{6,2},{7,3},{8,12},{9,13},{10,... | collective-permute-start | bytes 24584 | tf_op jit(solution)/shard_map/ppermute | solution.py:545
  89.6 9.8 %collective-permute-start.25 = (bf16[1536,128]{1,0:T(8,128)(2,1)S(1)}, bf16[1536,128]{1,0:T(8,128)(2,1)S(1)}, u32[]{:S(2)}, u32[]{:S(2)}) collective-permute-start(bf16[1536,128]{1,0:T(8,128)(2,1)S(1)} %shard_map.109.refs_2_), channel_id=1, source_target_pairs={{0,16},{8,120},{16,32},{24,8},{32,48},{40,24},{48,64},{56,40},{64,... | collective-permute-start | bytes 1179656 | tf_op jit(solution)/shard_map/ppermute | solution.py:562
  94.1 21.2 %copy-start.1 = (bf16[768,128]{1,0:T(8,128)(2,1)S(1)}, bf16[768,128]{1,0:T(8,128)(2,1)}, u32[]{:S(2)}) copy-start(bf16[768,128]{1,0:T(8,128)(2,1)} %get-tuple-element.25.refs_2_) | copy-start | bytes 589828
  99.0 7.2 %collective-permute-start.28 = (bf16[1536,128]{1,0:T(8,128)(2,1)S(1)}, bf16[1536,128]{1,0:T(8,128)(2,1)S(1)}, u32[]{:S(2)}, u32[]{:S(2)}) collective-permute-start(bf16[1536,128]{1,0:T(8,128)(2,1)S(1)} %shard_map.111.refs_3_), channel_id=1, source_target_pairs={{0,16},{8,120},{16,32},{24,8},{32,48},{40,24},{48,64},{56,40},{64,... | collective-permute-start | bytes 1179656 | tf_op jit(solution)/shard_map/ppermute | solution.py:562
  99.4 15.9 %collective-permute-start.26 = (bf16[1536,128]{1,0:T(8,128)(2,1)S(1)}, bf16[1536,128]{1,0:T(8,128)(2,1)S(1)}, u32[]{:S(2)}, u32[]{:S(2)}) collective-permute-start(bf16[1536,128]{1,0:T(8,128)(2,1)S(1)} %shard_map.111.refs_3_), channel_id=1, source_target_pairs={{0,8},{8,0},{16,24},{24,16},{32,40},{40,32},{48,56},{56,48},{64,72... | collective-permute-start | bytes 1179656 | tf_op jit(solution)/shard_map/ppermute | solution.py:588
  99.5 15.8 %collective-permute-start.27 = (bf16[1536,128]{1,0:T(8,128)(2,1)S(1)}, bf16[1536,128]{1,0:T(8,128)(2,1)S(1)}, u32[]{:S(2)}, u32[]{:S(2)}) collective-permute-start(bf16[1536,128]{1,0:T(8,128)(2,1)S(1)} %collective-permute-done.25.refs_4_), channel_id=1, source_target_pairs={{0,8},{8,0},{16,24},{24,16},{32,40},{40,32},{48,56},{56,48},{64,72... | collective-permute-start | bytes 1179656 | tf_op jit(solution)/shard_map/ppermute | solution.py:563
  106.3 14.8 %collective-permute-start.29 = (bf16[1536,128]{1,0:T(8,128)(2,1)S(1)}, bf16[1536,128]{1,0:T(8,128)(2,1)S(1)}, u32[]{:S(2)}, u32[]{:S(2)}) collective-permute-start(bf16[1536,128]{1,0:T(8,128)(2,1)S(1)} %collective-permute-done.28.refs_1_), channel_id=1, source_target_pairs={{0,8},{8,0},{16,24},{24,16},{32,40},{40,32},{48,56},{56,48},{64,72... | collective-permute-start | bytes 1179656 | tf_op jit(solution)/shard_map/ppermute | solution.py:563
  107.1 2.9 %collective-permute-start.7 = (f32[32,128]{1,0:T(8,128)S(1)}, f32[32,128]{1,0:T(8,128)S(1)}, u32[]{:S(2)}, u32[]{:S(2)}) collective-permute-start(f32[32,128]{1,0:T(8,128)S(1)} %pad_maximum_fusion.near_ref.refs_5_), channel_id=1, source_target_pairs={{0,3},{1,0},{2,1},{3,2},{4,7},{5,4},{6,5},{7,6},{8,11},{9,8},{10,9... | collective-permute-start | bytes 49160 | tf_op jit(solution)/shard_map/ppermute | solution.py:547
  109.2 3.8 %collective-permute-start.8 = (f32[32,128]{1,0:T(8,128)S(1)}, f32[32,128]{1,0:T(8,128)S(1)}, u32[]{:S(2)}, u32[]{:S(2)}) collective-permute-start(f32[32,128]{1,0:T(8,128)S(1)} %pad_maximum_fusion.near_ref.refs_5_), channel_id=1, source_target_pairs={{0,1},{1,2},{2,3},{3,0},{4,5},{5,6},{6,7},{7,4},{8,9},{9,10},{10,1... | collective-permute-start | bytes 49160 | tf_op jit(solution)/shard_map/ppermute | solution.py:547
  110.0 4.1 %collective-permute-start.9 = (f32[32,128]{1,0:T(8,128)S(1)}, f32[32,128]{1,0:T(8,128)S(1)}, u32[]{:S(2)}, u32[]{:S(2)}) collective-permute-start(f32[32,128]{1,0:T(8,128)S(1)} %pad_maximum_fusion.near_ref.refs_5_), channel_id=1, source_target_pairs={{0,2},{1,3},{2,0},{3,1},{4,6},{5,7},{6,4},{7,5},{8,10},{9,11},{10,... | collective-permute-start | bytes 49160 | tf_op jit(solution)/shard_map/ppermute | solution.py:547

commit v3 on v2

--- a/solution.py
+++ b/solution.py
@@ -15,6 +15,7 @@
 BF16 = jnp.bfloat16
 PRECISE = lax.Precision.HIGHEST
 SCALE = 6.0 / CUBE
+FREE = pl.CostEstimate(flops=0, bytes_accessed=0, transcendentals=0)
 
 
 def swap_halves(block):
@@ -74,17 +75,21 @@
     left = lax.broadcasted_iota(jnp.int32, (BS, 2 * BS), 1) < BS
     for copy, source, target in ((copies[1], p_ref, pp_ref), (copies[2], h_ref, hp_ref)):
         copy.wait()
-        for pair in range(SLOTS // 2):
-            halves = []
-            for half in range(2):
-                place = places[2 * pair + half]
-                r, c = place // 16, place % 16
-                block = source[
-                    pl.ds(pl.multiple_of(r * BS, BS), BS),
-                    pl.ds(pl.multiple_of(c // 2 * 128, 128), 128),
-                ]
-                halves.append(jnp.where(c % 2 == half, block, swap_halves(block)))
-            target[pl.ds(pair * BS, BS), :] = jnp.where(left, halves[0], halves[1])
+        for at in range(0, SLOTS // 2, 4):
+            blocks = []
+            for pair in range(at, at + 4):
+                halves = []
+                for half in range(2):
+                    place = places[2 * pair + half]
+                    r, c = place // 16, place % 16
+                    block = source[
+                        pl.ds(pl.multiple_of(r * BS, BS), BS),
+                        pl.ds(pl.multiple_of(c // 2 * 128, 128), 128),
+                    ]
+                    halves.append(jnp.where(c % 2 == half, block, swap_halves(block)))
+                blocks.append(jnp.where(left, halves[0], halves[1]))
+            for k, block in enumerate(blocks):
+                target[pl.ds((at + k) * BS, BS), :] = block
     for copy in copies[3:]:
         copy.wait()
     atom_rows(coef_ref, (x_ref, y_ref, z_ref), info_ref, wide)
@@ -111,7 +116,7 @@
             pltpu.SemaphoreType.DMA((7,)),
         ],
         compiler_params=pltpu.CompilerParams(vmem_limit_bytes=58 * 2**20),
-        cost_estimate=pl.CostEstimate(flops=0, bytes_accessed=6 * 2**20, transcendentals=0),
+        cost_estimate=FREE,
     )(*operands)
 
 
@@ -122,7 +127,7 @@
     return jnp.where(flags > 0, at, 2 * PACK)
 
 
-def table_kernel(pattern_ref, _, p_ref, h_ref, held):
+def table_kernel(pattern_ref, p_ref, h_ref, held):
     row, col = lax.axis_index("row"), lax.axis_index("col")
     r = lax.broadcasted_iota(jnp.int32, (128, 128), 0)
     m = lax.broadcasted_iota(jnp.int32, (128, 128), 1)
@@ -156,7 +161,7 @@
     h_ref[...] = offsets_of(before, four)
 
 
-def tile_tables(pattern, after):
+def tile_tables(pattern):
     vmem = pl.BlockSpec(memory_space=pltpu.VMEM)
     return pl.pallas_call(
         table_kernel,
@@ -164,12 +169,12 @@
             jax.ShapeDtypeStruct((32, 64), jnp.int32),
             jax.ShapeDtypeStruct((8, 128), jnp.int32),
         ),
-        in_specs=[vmem, pl.BlockSpec(memory_space=pl.ANY)],
+        in_specs=[vmem],
         out_specs=(vmem, vmem),
         scratch_shapes=[pltpu.VMEM((128, 128), jnp.int32)],
         compiler_params=pltpu.CompilerParams(vmem_limit_bytes=4 * 2**20),
-        cost_estimate=pl.CostEstimate(flops=0, bytes_accessed=2**21, transcendentals=0),
-    )(pattern, after)
+        cost_estimate=FREE,
+    )(pattern)
 
 
 def spread_tile(packed, offset, both, store):
@@ -177,11 +182,14 @@
     both[PACK : 2 * PACK, :] = swap_halves(packed)
     left = lax.broadcasted_iota(jnp.int32, (BS, 2 * BS), 1) < BS
     for r in range(4):
-        for c in range(8):
-            at0 = pl.multiple_of(offset(r, 2 * c), BS)
-            at1 = pl.multiple_of(offset(r, 2 * c + 1), BS)
-            block = jnp.where(left, both[pl.ds(at0, BS), :], both[pl.ds(at1, BS), :])
-            store(r, c, block)
+        for first in (0, 4):
+            blocks = []
+            for c in range(first, first + 4):
+                at0 = pl.multiple_of(offset(r, 2 * c), BS)
+                at1 = pl.multiple_of(offset(r, 2 * c + 1), BS)
+                blocks.append(jnp.where(left, both[pl.ds(at0, BS), :], both[pl.ds(at1, BS), :]))
+            for k, block in enumerate(blocks):
+                store(r, first + k, block)
 
 
 def spread_kernel(table_ref, near_ref, next_ref, last_ref, far_ref, out_ref, both):
@@ -214,7 +222,7 @@
         out_specs=vmem,
         scratch_shapes=[pltpu.VMEM((2 * PACK + BS, 128), BF16)],
         compiler_params=pltpu.CompilerParams(vmem_limit_bytes=4 * 2**20),
-        cost_estimate=pl.CostEstimate(flops=0, bytes_accessed=8 * 2**20, transcendentals=0),
+        cost_estimate=FREE,
     )(table, *parts)
 
 
@@ -241,18 +249,23 @@
     direction = 1 - 2 * core
     both[2 * PACK :, :] = jnp.zeros((BS, 128), BF16)
     tiles = []
-    for steps, flip in groups:
-        for j in range(2):
-            tiles.append(((y + j) % 2 * 8 + (z + steps * direction + 8) % 8) * 2 + (core + flip) % 2)
+    for count, steps, flip in groups:
+        for j in range(count):
+            tiles.append(
+                ((y + j) % 2 * 8 + (z + steps * direction + 8) % 8) * 2 + (core + flip + j // 2) % 2
+            )
     for at, tile in enumerate(tiles):
         wide[:, at * 256 : at * 256 + 256] = h_ref[tile]
     copy.wait()
-    for g, part in enumerate(parts):
-
-        def one(j, _, part=part, g=g):
-            tile = jnp.where(j == 0, tiles[2 * g], tiles[2 * g + 1])
+    start_at = 0
+    for part, (count, _, _) in zip(parts, groups):
+
+        def one(j, _, part=part, start_at=start_at, count=count):
+            tile = tiles[start_at]
+            for k in range(1, count):
+                tile = jnp.where(j == k, tiles[start_at + k], tile)
             packed = part[pl.ds(pl.multiple_of(j * PACK, PACK), PACK), :]
-            base = pl.multiple_of((2 * g + j) * 256, 256)
+            base = pl.multiple_of((start_at + j) * 256, 256)
 
             def store(r, c, block):
                 dense[pl.ds(base + r * BS, BS), c * 128 : c * 128 + 128] = block
@@ -260,7 +273,8 @@
             spread_tile(packed, lambda r, c: table[tile, r * 16 + c], both, store)
             return 0
 
-        lax.fori_loop(0, 2, one, 0)
+        lax.fori_loop(0, count, one, 0)
+        start_at += count
     if local:
         own, held = refs[7], refs[8]
 
@@ -310,7 +324,7 @@
     if after is not None:
         operands.append(after)
         specs.append(pl.BlockSpec(memory_space=pl.ANY))
-    depth = 512 * len(groups)
+    depth = 256 * sum(g[0] for g in groups)
     scratch = [
         pltpu.VMEM((2 * PACK + BS, 128), BF16),
         pltpu.VMEM((depth, 1024), BF16),
@@ -327,26 +341,27 @@
         out_specs=(vmem, vmem),
         scratch_shapes=scratch,
         compiler_params=pltpu.CompilerParams(vmem_limit_bytes=12 * 2**20),
-        cost_estimate=pl.CostEstimate(
-            flops=4 * 256 * 512 * 1024 * len(groups), bytes_accessed=4 * 2**20 * len(groups), transcendentals=0
-        ),
+        cost_estimate=FREE,
     )(table, *operands)
 
 
-def tie(buffer, token):
+def front(buffer, token):
     anywhere = pl.BlockSpec(memory_space=pl.ANY)
-
-    def kernel(buffer_ref, token_ref, out_ref):
-        pass
+    shape = (2 * PACK, 128)
+
+    def kernel(buffer_ref, token_ref, out_ref, sem):
+        copy = pltpu.make_async_copy(buffer_ref.at[pl.ds(0, 2 * PACK), :], out_ref, sem)
+        copy.start()
+        copy.wait()
 
     return pl.pallas_call(
         kernel,
-        out_shape=jax.ShapeDtypeStruct(buffer.shape, buffer.dtype),
+        out_shape=jax.ShapeDtypeStruct(shape, buffer.dtype),
         in_specs=[anywhere, anywhere],
         out_specs=anywhere,
-        input_output_aliases={0: 0},
+        scratch_shapes=[pltpu.SemaphoreType.DMA],
         compiler_params=pltpu.CompilerParams(vmem_limit_bytes=2**20),
-        cost_estimate=pl.CostEstimate(flops=0, bytes_accessed=0, transcendentals=0),
+        cost_estimate=FREE,
     )(buffer, token)
 
 
@@ -362,6 +377,21 @@
     first = scaled * gaussian
     second = scaled * first
     return gaussian, first, second, scaled * second
+
+
+def split2(value):
+    high = value.astype(BF16)
+    return high, (value - high.astype(F32)).astype(BF16)
+
+
+def three_passes(a, b, dims):
+    high, low = split2(a)
+    terms = ((high, b[1]), (low, b[0]), (high, b[0]))
+    total = None
+    for left, right in terms:
+        part = lax.dot_general(left, right, dims, preferred_element_type=F32)
+        total = part if total is None else total + part
+    return total
 
 
 ROWS = [(a, 2 * bh + bl) for bl in range(2) for a in range(4) for bh in range(2)]
@@ -395,7 +425,7 @@
             total = term if total is None else total + term
         u_ref[b] = total
     s_ref[...] = jnp.zeros_like(s_ref)
-    gz = gz_ref[...]
+    gz = split2(gz_ref[...])
     chunk = 8
     copy.wait()
 
@@ -411,15 +441,11 @@
                 plane = term if plane is None else plane + term
             planes.append(plane)
         spread = jnp.concatenate(planes, axis=0)
-        density = lax.dot_general(
-            spread, gz, (((1,), (1,)), ((), ())), precision=PRECISE, preferred_element_type=F32
-        )
+        density = three_passes(spread, gz, (((1,), (1,)), ((), ())))
         density = density.reshape(chunk, CUBE, 128)
         density_ref[pl.ds(x0, chunk)] = density
         potential = external_ref[pl.ds(x0, chunk)] + jnp.tanh(density)
-        along = jnp.dot(
-            potential.reshape(chunk * CUBE, 128), gz, precision=PRECISE, preferred_element_type=F32
-        )
+        along = three_passes(potential.reshape(chunk * CUBE, 128), gz, (((1,), (0,)), ((), ())))
         for a in range(4):
             total = None
             for x in range(chunk):
@@ -455,9 +481,7 @@
             pltpu.SemaphoreType.DMA,
         ],
         compiler_params=pltpu.CompilerParams(vmem_limit_bytes=12 * 2**20),
-        cost_estimate=pl.CostEstimate(
-            flops=2 * 2 * 6 * 1024 * 256 * 128, bytes_accessed=2 * 2**20, transcendentals=2**18
-        ),
+        cost_estimate=FREE,
     )(info, external)
 
 
@@ -492,7 +516,7 @@
         in_specs=[vmem] * 4,
         out_specs=(vmem, vmem),
         compiler_params=pltpu.CompilerParams(vmem_limit_bytes=2 * 2**20),
-        cost_estimate=pl.CostEstimate(flops=0, bytes_accessed=2**17, transcendentals=0),
+        cost_estimate=FREE,
     )(*parts)
 
 
@@ -520,6 +544,14 @@
     return [(i, (i + step) % size) for i in range(size)]
 
 
+def from_rows(core, last, first):
+    mine = jnp.where(core == 0, last, first)
+    near = lax.ppermute(mine, "row", ACROSS_CORES)
+    mine = jnp.where(core == 0, first, last)
+    far = lax.ppermute(mine, "row", [(i, (i + 2 * (i % 2) - 1) % 32) for i in range(32)])
+    return jnp.where(core == 0, far, near), jnp.where(core == 0, near, far)
+
+
 def from_neighbours(last, first, axis, size):
     before = lax.ppermute(last, axis, ring(axis, size, 1))
     after = lax.ppermute(first, axis, ring(axis, size, -1))
@@ -531,66 +563,60 @@
     hp, pp, info = pack(
         pattern, hamiltonian, density_matrix, coefficients, off_x, off_y, off_z
     )
-    table_p, table_h = tile_tables(pattern, info)
-
+    table_p, table_h = tile_tables(pattern)
+
+    def step(chain):
+        return lax.ppermute(chain, "row", ALONG_Z)
+
+    def swap(chain):
+        return lax.ppermute(chain, "row", ACROSS_CORES)
+
+    together = lax.optimization_barrier
+
+    py = lax.ppermute(pp, "row", ACROSS_Y)
+    hy = lax.ppermute(hp, "col", col_pairs(1, 0))
     before, after = from_neighbours(info, info, "col", 8)
     info = jnp.concatenate([before, info, after], axis=1)
-    before, after = from_neighbours(info, info, "row", 32)
+    pc = swap(pp)
+    h0 = jnp.concatenate([hp, hy], axis=0)
+    py, pc, info = together((py, pc, info))
+    q = jnp.concatenate([pp, py, pc, swap(py)], axis=0)
+    q, info = together((q, info))
+
+    q1 = step(q)
+    before, after = from_rows(core, info, info)
     info = jnp.concatenate([before, info, after, jnp.zeros((24, 112), F32)], axis=1)
-    density, share9 = grid_part(info, external)
-    share = share9
-    before, after = from_neighbours(share[:, 96:144], share[:, 0:48], "row", 32)
+    density, share = grid_part(info, external)
+    q1, share, h0 = together((q1, share, h0))
+
+    q2, x1 = step(q1), swap(q1)
+    h_next = lax.ppermute(h0, "col", col_pairs(0, 3))
+    h_last = lax.ppermute(h0, "col", col_pairs(0, 1))
+    before, after = from_rows(core, share[:, 96:144], share[:, 0:48])
     share = share[:, 48:96] + before + after
     share = jnp.concatenate([share, jnp.zeros((16, 80), F32)], axis=1)
+    q2, share, h_next, h_last = together((q2, share, h_next, h_last))
+
+    q3, x2 = step(q2), swap(q2)
+    h_far = lax.ppermute(jnp.where(core == 0, h_last, h_next), ("row", "col"), ALONG_X)
+    h_dense = spread_hamiltonian(table_h, [h0, h_next, h_last, h_far])
     other = lax.ppermute(share, "col", col_pairs(1, 0))
     share = jnp.concatenate([share, other], axis=0)
+    product, done = accumulate(
+        table_p, h_dense, None, [q, q1, x1], ((4, 0, 0), (4, -1, 0), (4, 1, 1))
+    )
+    q3, share, product = together((q3, share, product))
+
+    q4 = step(front(q3, done))
+    x3 = swap(q3)
     shares = [share] + [lax.ppermute(share, "col", col_pairs(0, d)) for d in (3, 1, 2)]
+    product, _ = accumulate(table_p, h_dense, product, [q2, x2], ((4, -2, 0), (4, 2, 1)))
     atoms, integrals = collect(shares)
-
-    hy = lax.ppermute(hp, "col", col_pairs(1, 0))
-    h0 = jnp.concatenate([hp, hy], axis=0)
-    h_next = lax.ppermute(h0, "col", col_pairs(0, 3))
-    h_last = lax.ppermute(h0, "col", col_pairs(0, 1))
-    h_far = lax.ppermute(jnp.where(core == 0, h_last, h_next), ("row", "col"), ALONG_X)
-    h_dense = spread_hamiltonian(table_h, [h0, h_next, h_last, h_far])
-
-    py = lax.ppermute(pp, "row", ACROSS_Y)
-    m = jnp.concatenate([pp, py], axis=0)
-    mc = lax.ppermute(m, "row", ACROSS_CORES)
-
-    def step(chain):
-        chain = lax.ppermute(chain, "row", ALONG_Z)
-        return chain, lax.ppermute(chain, "row", ACROSS_CORES)
-
-    def groups(s):
-        return ((-s, 0), (-s, 1), (s, 1), (s, 0))
-
-    m1, x1 = step(m)
-    c1, xc1 = step(mc)
-    m2, x2 = step(m1)
-    c2 = lax.ppermute(c1, "row", ALONG_Z)
-    product, done = accumulate(
-        table_p,
-        h_dense,
-        None,
-        [m, mc, m1, c1, x1, xc1],
-        ((0, 0), (0, 1)) + groups(1),
-        after=share9,
+    q4, atoms, product = together((q4, atoms, product))
+    product, _ = accumulate(
+        table_p, h_dense, product, [q3, x3], ((4, -3, 0), (4, 3, 1)), local=(atoms, pp)
     )
-    c2 = tie(c2, done)
-    xc2 = lax.ppermute(c2, "row", ACROSS_CORES)
-    c3, xc3 = step(c2)
-    m3 = lax.ppermute(m2, "row", ALONG_Z)
-    product, done = accumulate(
-        table_p, h_dense, product, [m2, c2, x2, xc2], groups(2), after=share
-    )
-    m3 = tie(m3, done)
-    x3 = lax.ppermute(m3, "row", ACROSS_CORES)
-    m4, x4 = step(m3)
-    product, _ = accumulate(
-        table_p, h_dense, product, [m3, c3, x3, xc3], groups(3), local=(atoms, pp)
-    )
-    product, _ = accumulate(table_p, h_dense, product, [m4, x4], ((4, 0), (4, 1)))
+    product, _ = accumulate(table_p, h_dense, product, [q4, swap(q4)], ((2, 4, 0), (2, 4, 1)))
     return (density, integrals, product)
 
 

time: 127 us -> 92 us (0.72)
  waiting for transfers between devices: 33.7 us -> 20.2 us
  starting transfers between devices: 48.7 us -> 35.7 us
  local copies, waits for them, and re-layouts: 5.39 us -> 0.11 us
  Pallas kernels: 35 us -> 32.5 us
    ppermute x15 -> x14, starting transfers between devices: 27.6 us -> 17.9 us  [the longest x4 11.8 us: step(): return lax.ppermute(chain, 'row', ALONG_Z)]
    ppermute x1, waiting for transfers between devices: 6.84 us -> 0.01 us  [on_device(): py = lax.ppermute(pp, 'row', ACROSS_Y)]
    ppermute x3 -> x1, waiting for transfers between devices: 5.61 us -> 0.01 us  [from_neighbours(): after = lax.ppermute(first, axis, ring(axis, size, -1))]
    ppermute x3 -> x1, waiting for transfers between devices: 5.95 us -> 1.4 us  [from_neighbours(): before = lax.ppermute(last, axis, ring(axis, size, 1))]
    ppermute x3 -> x1, starting transfers between devices: 5.44 us -> 0.95 us  [from_neighbours(): before = lax.ppermute(last, axis, ring(axis, size, 1))]
    unnamed x10 -> x8, local copies, waits for them, and re-layouts: 4.47 us -> 0.02 us
    ppermute x3, waiting for transfers between devices: 3.55 us -> 0.01 us  [on_device(): lax.ppermute(share, 'col', col_pairs(0, d))]
    ppermute x1, waiting for transfers between devices: 0.28 us -> 3.59 us  [on_device(): h_next = lax.ppermute(h0, 'col', col_pairs(0, 3))]
  transfers between devices with their start and end apart: 30 -> 25, of which waited for: 14 -> 8; matrix products, arithmetic and copies ran while one was open for 4% -> 2% of each run, Pallas kernels for 22% -> 28%
where the time goes in v3:
time: 92 us; the launch traced here: 91.6 us
  starting transfers between devices  35.7 us (39%)
  Pallas kernels  32.5 us (35%)
  waiting for transfers between devices  20.2 us (22%)
  other arithmetic  2.07 us (2%)
  between operations  1.03 us (1%)
    pallas_call x4, Pallas kernels, accumulate(): pl.pallas_call(functools.partial(accumulate_kernel, groups, before is Non...  21.6 us
    ppermute x4, starting transfers between devices, step(): return lax.ppermute(chain, 'row', ALONG_Z)  11.8 us
    ppermute x2, waiting for transfers between devices, from_rows(): lax.ppermute(mine, 'row', [(i, (i + 2 * (i % 2) - 1) % 32) for i in range...  6.28 us
    ppermute x6, starting transfers between devices, swap(): return lax.ppermute(chain, 'row', ACROSS_CORES)  5.3 us
    ppermute x1, starting transfers between devices, from_neighbours(): after = lax.ppermute(first, axis, ring(axis, size, -1))  4.14 us
    ppermute x1, starting transfers between devices, on_device(): h_next = lax.ppermute(h0, 'col', col_pairs(0, 3))  3.72 us
    ppermute x1, waiting for transfers between devices, on_device(): h_next = lax.ppermute(h0, 'col', col_pairs(0, 3))  3.59 us
    ppermute x1, waiting for transfers between devices, on_device(): h_last = lax.ppermute(h0, 'col', col_pairs(0, 1))  3.4 us
  transfers between devices with their start and end apart: 25, of which 8 were waited for; matrix products, arithmetic and copies ran while one was open for 2% of the time, Pallas kernels for 28%

profile of v3, /device:TPU:1, one launch (start us, length us, event | category | flops | bytes accessed | tf_op | source)
XLA Modules:
  0.0 91.6 jit_solution(6435147151252424465)
XLA Ops:
  0.6 2.8 %shard_map.103 = (bf16[768,128]{1,0:T(8,128)(2,1)}, bf16[768,128]{1,0:T(8,128)(2,1)}, f32[24,16]{1,0:T(8,128)}) custom-call(s32[128,128]{1,0:T(8,128)} %pattern_ref.1, bf16[256,1024]{1,0:T(8,128)(2,1)} %h_hbm.1, bf16[256,1024]{1,0:T(8,128)(2,1)} %p_hbm.1, f32[4,64]{1,0:T(4,128)} %coef_hbm.1, s32[4]{0:T(128)} %x_hbm.1, s32[4]{0:T(128)} %y_hbm.1, s32[4]{0:T(128)} %z_hbm.1), custom_call_target="tpu_custom_call" | custom-call | tf_op jit(solution)/shard_map/pallas_call | solution.py:101
  3.4 0.0 copy-start.3
  3.4 2.2 %collective-permute-start = (bf16[768,128]{1,0:T(8,128)(2,1)}, bf16[768,128]{1,0:T(8,128)(2,1)S(1)}, u32[]{:S(2)}, u32[]{:S(2)}) collective-permute-start(bf16[768,128]{1,0:T(8,128)(2,1)} %get-tuple-element.35.refs_2_), channel_id=1, source_target_pairs={{0,128},{8,136},{16,144},{24,152},{32,160},{40,168},{48,176},{56,1... | collective-permute-start | bytes 589832 | tf_op jit(solution)/shard_map/ppermute | solution.py:576
  5.7 1.2 %collective-permute-start.1 = (bf16[768,128]{1,0:T(8,128)(2,1)}, bf16[768,128]{1,0:T(8,128)(2,1)S(1)}, u32[]{:S(2)}, u32[]{:S(2)}) collective-permute-start(bf16[768,128]{1,0:T(8,128)(2,1)} %get-tuple-element.35.refs_2_), channel_id=1, source_target_pairs={{0,8},{8,0},{16,24},{24,16},{32,40},{40,32},{48,56},{56,48},{64,72... | collective-permute-start | bytes 589832 | tf_op jit(solution)/shard_map/ppermute | solution.py:572
  6.9 1.0 %collective-permute-start.2 = (f32[24,16]{1,0:T(8,128)}, f32[24,16]{1,0:T(8,128)S(1)}, u32[]{:S(2)}, u32[]{:S(2)}) collective-permute-start(f32[24,16]{1,0:T(8,128)} %get-tuple-element.36), channel_id=1, source_target_pairs={{0,1},{1,2},{2,3},{3,4},{4,5},{5,6},{6,7},{7,0},{8,9},{9,10},{10,1... | collective-permute-start | bytes 4616 | tf_op jit(solution)/shard_map/ppermute | solution.py:556
  7.8 4.1 %collective-permute-start.3 = (f32[24,16]{1,0:T(8,128)}, f32[24,16]{1,0:T(8,128)S(1)}, u32[]{:S(2)}, u32[]{:S(2)}) collective-permute-start(f32[24,16]{1,0:T(8,128)} %get-tuple-element.36), channel_id=1, source_target_pairs={{0,7},{1,0},{2,1},{3,2},{4,3},{5,4},{6,5},{7,6},{8,15},{9,8},{10,9... | collective-permute-start | bytes 4616 | tf_op jit(solution)/shard_map/ppermute | solution.py:557
  12.0 1.4 %collective-permute-done.2 = f32[24,16]{1,0:T(8,128)S(1)} collective-permute-done((f32[24,16]{1,0:T(8,128)}, f32[24,16]{1,0:T(8,128)S(1)}, u32[]{:S(2)}, u32[]{:S(2)}) %collective-permute-start.2) | collective-permute-done | bytes 1568 | tf_op jit(solution)/shard_map/ppermute | solution.py:556
  13.4 0.0 collective-permute-done.3
  13.4 0.8 pad_maximum_fusion.3
  14.2 0.0 collective-permute-done
  14.2 0.0 collective-permute-done.1
  14.2 1.2 %collective-permute-start.4 = (bf16[768,128]{1,0:T(8,128)(2,1)S(1)}, bf16[768,128]{1,0:T(8,128)(2,1)S(1)}, u32[]{:S(2)}, u32[]{:S(2)}) collective-permute-start(bf16[768,128]{1,0:T(8,128)(2,1)S(1)} %collective-permute-done), channel_id=1, source_target_pairs={{0,8},{8,0},{16,24},{24,16},{32,40},{40,32},{48,56},{56,48},{64,72... | collective-permute-start | bytes 589832 | tf_op jit(solution)/shard_map/ppermute | solution.py:572
  15.4 2.3 %collective-permute-start.8 = (bf16[768,128]{1,0:T(8,128)(2,1)}, bf16[768,128]{1,0:T(8,128)(2,1)S(1)}, u32[]{:S(2)}, u32[]{:S(2)}) collective-permute-start(bf16[768,128]{1,0:T(8,128)(2,1)} %get-tuple-element.44), channel_id=1, source_target_pairs={{0,4},{1,5},{2,6},{3,7},{4,0},{5,1},{6,2},{7,3},{8,12},{9,13},{10,... | collective-permute-start | bytes 589832 | tf_op jit(solution)/shard_map/ppermute | solution.py:577
  17.7 0.0 collective-permute-done.4
  17.7 1.0 %pad_maximum_fusion.refs_0_ = bf16[3072,128]{1,0:T(8,128)(2,1)S(1)} fusion(bf16[768,128]{1,0:T(8,128)(2,1)S(1)} %collective-permute-done.4, bf16[768,128]{1,0:T(8,128)(2,1)S(1)} %collective-permute-done.1, bf16[768,128]{1,0:T(8,128)(2,1)S(1)} %collective-permute-done, bf16[768,128]{1,0:T(8,128)(2,1)} %get-tuple-element.35.refs_2_), kind=kLoop, calls=%fused_computation | loop fusion | flops 3145728 | bytes 1572864 | tf_op jit(solution)/shard_map/concatenate | solution.py:583
  18.6 0.0 copy-start.2
  18.7 5.7 %collective-permute-start.7 = (bf16[3072,128]{1,0:T(8,128)(2,1)S(1)}, bf16[3072,128]{1,0:T(8,128)(2,1)S(1)}, u32[]{:S(2)}, u32[]{:S(2)}) collective-permute-start(bf16[3072,128]{1,0:T(8,128)(2,1)S(1)} %pad_maximum_fusion.refs_0_), channel_id=1, source_target_pairs={{0,16},{8,120},{16,32},{24,8},{32,48},{40,24},{48,64},{56,40},{64,... | collective-permute-start | bytes 2359304 | tf_op jit(solution)/shard_map/ppermute | solution.py:569
  24.3 0.1 pad.8.clone
  24.4 0.0 collective-permute-start.5
  24.4 0.7 collective-permute-start.6
  25.1 0.0 collective-permute-done.8
  25.1 2.9 %collective-permute-done.5 = f32[24,48]{1,0:T(8,128)S(1)} collective-permute-done((f32[24,48]{1,0:T(8,128)S(1)}, f32[24,48]{1,0:T(8,128)S(1)}, u32[]{:S(2)}, u32[]{:S(2)}) %collective-permute-start.5) | collective-permute-done | bytes 4640 | tf_op jit(solution)/shard_map/ppermute | solution.py:551
  28.0 0.0 collective-permute-done.6
  28.0 0.1 maximum_maximum_fusion.info_ref
  28.1 3.3 %shard_map.104 = (f32[32,32,128]{2,1,0:T(8,128)}, f32[16,256]{1,0:T(8,128)S(1)}) custom-call(f32[24,256]{1,0:T(8,128)S(1)} %maximum_maximum_fusion.info_ref, f32[32,32,128]{2,1,0:T(8,128)S(1)} %copy-done.1), custom_call_target="tpu_custom_call" | custom-call | tf_op jit(solution)/shard_map/pallas_call | solution.py:466
  31.4 1.9 %collective-permute-done.7.refs_1_ = bf16[3072,128]{1,0:T(8,128)(2,1)S(1)} collective-permute-done((bf16[3072,128]{1,0:T(8,128)(2,1)S(1)}, bf16[3072,128]{1,0:T(8,128)(2,1)S(1)}, u32[]{:S(2)}, u32[]{:S(2)}) %collective-permute-start.7) | collective-permute-done | bytes 786464 | tf_op jit(solution)/shard_map/ppermute | solution.py:569
  33.4 3.1 %collective-permute-start.9 = (bf16[3072,128]{1,0:T(8,128)(2,1)S(1)}, bf16[3072,128]{1,0:T(8,128)(2,1)S(1)}, u32[]{:S(2)}, u32[]{:S(2)}) collective-permute-start(bf16[3072,128]{1,0:T(8,128)(2,1)S(1)} %collective-permute-done.7.refs_1_), channel_id=1, source_target_pairs={{0,16},{8,120},{16,32},{24,8},{32,48},{40,24},{48,64},{56,40},{64,... | collective-permute-start | bytes 2359304 | tf_op jit(solution)/shard_map/ppermute | solution.py:569
  36.5 3.7 %collective-permute-start.12 = (bf16[1536,128]{1,0:T(8,128)(2,1)S(1)}, bf16[1536,128]{1,0:T(8,128)(2,1)S(1)}, u32[]{:S(2)}, u32[]{:S(2)}) collective-permute-start(bf16[1536,128]{1,0:T(8,128)(2,1)S(1)} %pad_maximum_fusion.1.near_ref), channel_id=1, source_target_pairs={{0,3},{1,0},{2,1},{3,2},{4,7},{5,4},{6,5},{7,6},{8,11},{9,8},{10,9... | collective-permute-start | bytes 1179656 | tf_op jit(solution)/shard_map/ppermute | solution.py:593
  40.2 0.0 collective-permute-start.13
  40.2 0.1 slice_select_fusion.1
  40.3 0.0 collective-permute-start.10
  40.3 0.1 collective-permute-start.11
  40.4 3.4 %collective-permute-done.10 = f32[16,48]{1,0:T(8,128)S(1)} collective-permute-done((f32[16,48]{1,0:T(8,128)S(1)}, f32[16,48]{1,0:T(8,128)S(1)}, u32[]{:S(2)}, u32[]{:S(2)}) %collective-permute-start.10) | collective-permute-done | bytes 3104 | tf_op jit(solution)/shard_map/ppermute | solution.py:551
  43.8 0.7 collective-permute-start.17
  44.5 0.0 collective-permute-done.11
  44.5 0.1 select_add_fusion
  44.6 3.6 %collective-permute-done.12.next_ref = bf16[1536,128]{1,0:T(8,128)(2,1)S(1)} collective-permute-done((bf16[1536,128]{1,0:T(8,128)(2,1)S(1)}, bf16[1536,128]{1,0:T(8,128)(2,1)S(1)}, u32[]{:S(2)}, u32[]{:S(2)}) %collective-permute-start.12) | collective-permute-done | bytes 393248 | tf_op jit(solution)/shard_map/ppermute | solution.py:593
  48.2 3.4 %collective-permute-done.13.last_ref = bf16[1536,128]{1,0:T(8,128)(2,1)S(1)} collective-permute-done((bf16[1536,128]{1,0:T(8,128)(2,1)S(1)}, bf16[1536,128]{1,0:T(8,128)(2,1)S(1)}, u32[]{:S(2)}, u32[]{:S(2)}) %collective-permute-start.13) | collective-permute-done | bytes 393248 | tf_op jit(solution)/shard_map/ppermute | solution.py:594
  51.6 0.0 collective-permute-done.9.refs_1_
  51.6 0.0 collective-permute-start.14
  51.6 0.0 collective-permute-start.22
  51.7 1.0 %collective-permute-start.16 = (bf16[1536,128]{1,0:T(8,128)(2,1)S(1)}, bf16[1536,128]{1,0:T(8,128)(2,1)S(1)}, u32[]{:S(2)}, u32[]{:S(2)}) collective-permute-start(bf16[1536,128]{1,0:T(8,128)(2,1)S(1)} %broadcast_select_fusion), channel_id=1, source_target_pairs={{0,1},{1,2},{2,3},{3,0},{4,5},{5,6},{6,7},{7,4},{8,11},{9,8},{10,9... | collective-permute-start | bytes 1179656 | tf_op jit(solution)/shard_map/ppermute | solution.py:601
  52.7 1.9 %collective-permute-start.15 = (f32[16,128]{1,0:T(8,128)S(1)}, f32[16,128]{1,0:T(8,128)S(1)}, u32[]{:S(2)}, u32[]{:S(2)}) collective-permute-start(f32[16,128]{1,0:T(8,128)S(1)} %concatenate.22), channel_id=1, source_target_pairs={{0,4},{1,5},{2,6},{3,7},{4,0},{5,1},{6,2},{7,3},{8,12},{9,13},{10,... | collective-permute-start | bytes 24584 | tf_op jit(solution)/shard_map/ppermute | solution.py:603
  54.6 0.5 shard_map.105
  55.1 1.6 %collective-permute-done.15 = f32[16,128]{1,0:T(8,128)S(1)} collective-permute-done((f32[16,128]{1,0:T(8,128)S(1)}, f32[16,128]{1,0:T(8,128)S(1)}, u32[]{:S(2)}, u32[]{:S(2)}) %collective-permute-start.15) | collective-permute-done | bytes 8224 | tf_op jit(solution)/shard_map/ppermute | solution.py:603
  56.7 2.0 %collective-permute-done.16.far_ref = bf16[1536,128]{1,0:T(8,128)(2,1)S(1)} collective-permute-done((bf16[1536,128]{1,0:T(8,128)(2,1)S(1)}, bf16[1536,128]{1,0:T(8,128)(2,1)S(1)}, u32[]{:S(2)}, u32[]{:S(2)}) %collective-permute-start.16) | collective-permute-done | bytes 393248 | tf_op jit(solution)/shard_map/ppermute | solution.py:601
  58.7 3.1 %shard_map.106.h_ref = bf16[32,256,256]{2,1,0:T(8,128)(2,1)S(1)} custom-call(s32[8,128]{1,0:T(8,128)S(1)} %get-tuple-element.51.table_ref, bf16[1536,128]{1,0:T(8,128)(2,1)S(1)} %pad_maximum_fusion.1.near_ref, bf16[1536,128]{1,0:T(8,128)(2,1)S(1)} %collective-permute-done.12.next_ref, bf16[1536,128]{1,0:T(8,128)(2,1)S(1)} %collective-permute-done.13.last_ref, ...), custom_call_target="tpu_custom_call" | custom-call | tf_op jit(solution)/shard_map/pallas_call | solution.py:218
  61.8 0.0 collective-permute-done.17.refs_2_
  61.8 6.6 %shard_map.107 = (f32[256,1024]{1,0:T(8,128)S(1)}, f32[8,128]{1,0:T(8,128)S(1)}) custom-call(s32[32,64]{1,0:T(8,128)S(1)} %get-tuple-element.50.table_ref, bf16[32,256,256]{2,1,0:T(8,128)(2,1)S(1)} %shard_map.106.h_ref, bf16[3072,128]{1,0:T(8,128)(2,1)S(1)} %pad_maximum_fusion.refs_0_, bf16[3072,128]{1,0:T(8,128)(2,1)S(1)} %collective-permute-done.7.refs_1_, ...), custom_call_target="tpu_custom_call" | custom-call | tf_op jit(solution)/shard_map/pallas_call | solution.py:337
  68.3 0.0 collective-permute-done.14.buffer_ref.refs_3_
  68.4 0.2 shard_map.109
  68.6 0.0 copy-start
  68.6 3.0 %collective-permute-start.21 = (bf16[1536,128]{1,0:T(8,128)(2,1)S(1)}, bf16[1536,128]{1,0:T(8,128)(2,1)S(1)}, u32[]{:S(2)}, u32[]{:S(2)}) collective-permute-start(bf16[1536,128]{1,0:T(8,128)(2,1)S(1)} %shard_map.109), channel_id=1, source_target_pairs={{0,16},{8,120},{16,32},{24,8},{32,48},{40,24},{48,64},{56,40},{64,... | collective-permute-start | bytes 1179656 | tf_op jit(solution)/shard_map/ppermute | solution.py:569
  71.6 1.3 %collective-permute-start.23 = (bf16[3072,128]{1,0:T(8,128)(2,1)S(1)}, bf16[3072,128]{1,0:T(8,128)(2,1)S(1)}, u32[]{:S(2)}, u32[]{:S(2)}) collective-permute-start(bf16[3072,128]{1,0:T(8,128)(2,1)S(1)} %collective-permute-done.14.buffer_ref.refs_3_), channel_id=1, source_target_pairs={{0,8},{8,0},{16,24},{24,16},{32,40},{40,32},{48,56},{56,48},{64,72... | collective-permute-start | bytes 2359304 | tf_op jit(solution)/shard_map/ppermute | solution.py:572
  72.9 0.0 collective-permute-start.18
  73.0 1.4 %collective-permute-start.19 = (f32[32,128]{1,0:T(8,128)S(1)}, f32[32,128]{1,0:T(8,128)S(1)}, u32[]{:S(2)}, u32[]{:S(2)}) collective-permute-start(f32[32,128]{1,0:T(8,128)S(1)} %pad_maximum_fusion.2.near_ref), channel_id=1, source_target_pairs={{0,1},{1,2},{2,3},{3,0},{4,5},{5,6},{6,7},{7,4},{8,9},{9,10},{10,1... | collective-permute-start | bytes 49160 | tf_op jit(solution)/shard_map/ppermute | solution.py:612
  74.4 0.0 collective-permute-done.22.refs_2_
  74.4 5.1 %shard_map.110 = (f32[256,1024]{1,0:T(8,128)S(1)}, f32[8,128]{1,0:T(8,128)}) custom-call(s32[32,64]{1,0:T(8,128)S(1)} %get-tuple-element.50.table_ref, bf16[32,256,256]{2,1,0:T(8,128)(2,1)S(1)} %shard_map.106.h_ref, f32[256,1024]{1,0:T(8,128)S(1)} %get-tuple-element.60.refs_0_, bf16[3072,128]{1,0:T(8,128)(2,1)S(1)} %collective-permute-done.9.refs_1_, ...), custom_call_target="tpu_custom_call" | custom-call | tf_op jit(solution)/shard_map/pallas_call | solution.py:337
  79.5 0.0 collective-permute-done.19.last_ref
  79.5 1.1 %shard_map.108 = (f32[16,128]{1,0:T(8,128)S(1)}, f32[4,64]{1,0:T(4,128)}) custom-call(f32[32,128]{1,0:T(8,128)S(1)} %pad_maximum_fusion.2.near_ref, f32[32,128]{1,0:T(8,128)S(1)} %collective-permute-done.18.next_ref, f32[32,128]{1,0:T(8,128)S(1)} %collective-permute-done.19.last_ref, f32[32,128]{1,0:T(8,128)S(1)} %collective-permute-done.20.far_ref), custom_call_target="tpu_custom_call" | custom-call | tf_op jit(solution)/shard_map/pallas_call | solution.py:513
  80.6 0.8 collective-permute-start.24
  81.4 0.0 collective-permute-done.23.refs_4_
  81.4 5.7 %shard_map.111 = (f32[256,1024]{1,0:T(8,128)S(1)}, f32[8,128]{1,0:T(8,128)}) custom-call(s32[32,64]{1,0:T(8,128)S(1)} %get-tuple-element.50.table_ref, bf16[32,256,256]{2,1,0:T(8,128)(2,1)S(1)} %shard_map.106.h_ref, f32[256,1024]{1,0:T(8,128)S(1)} %get-tuple-element.62.refs_0_, f32[16,128]{1,0:T(8,128)S(1)} %get-tuple-element.63.refs_1_, ...), custom_call_target="tpu_custom_call" | custom-call | tf_op jit(solution)/shard_map/pallas_call | solution.py:337
  87.2 4.2 %shard_map.112 = (f32[256,1024]{1,0:T(8,128)}, f32[8,128]{1,0:T(8,128)}) custom-call(s32[32,64]{1,0:T(8,128)S(1)} %get-tuple-element.50.table_ref, bf16[32,256,256]{2,1,0:T(8,128)(2,1)S(1)} %shard_map.106.h_ref, f32[256,1024]{1,0:T(8,128)S(1)} %get-tuple-element.64.refs_0_, bf16[1536,128]{1,0:T(8,128)(2,1)S(1)} %collective-permute-done.21.refs_1_, ...), custom_call_target="tpu_custom_call" | custom-call | tf_op jit(solution)/shard_map/pallas_call | solution.py:337
  (16 shorter events, 0.1 us)
Async XLA Ops:
  0.6 27.5 %copy-start.1 = (f32[32,32,128]{2,1,0:T(8,128)S(1)}, f32[32,32,128]{2,1,0:T(8,128)}, u32[]{:S(2)}) copy-start(f32[32,32,128]{2,1,0:T(8,128)} %external_hbm.1) | copy-start | bytes 1572868
  3.4 21.7 %copy-start.3 = (bf16[768,128]{1,0:T(8,128)(2,1)S(1)}, bf16[768,128]{1,0:T(8,128)(2,1)}, u32[]{:S(2)}) copy-start(bf16[768,128]{1,0:T(8,128)(2,1)} %get-tuple-element.44) | copy-start | bytes 589828
  3.4 10.7 %collective-permute-start = (bf16[768,128]{1,0:T(8,128)(2,1)}, bf16[768,128]{1,0:T(8,128)(2,1)S(1)}, u32[]{:S(2)}, u32[]{:S(2)}) collective-permute-start(bf16[768,128]{1,0:T(8,128)(2,1)} %get-tuple-element.35.refs_2_), channel_id=1, source_target_pairs={{0,128},{8,136},{16,144},{24,152},{32,160},{40,168},{48,176},{56,1... | collective-permute-start | bytes 589832 | tf_op jit(solution)/shard_map/ppermute | solution.py:576
  5.7 8.5 %collective-permute-start.1 = (bf16[768,128]{1,0:T(8,128)(2,1)}, bf16[768,128]{1,0:T(8,128)(2,1)S(1)}, u32[]{:S(2)}, u32[]{:S(2)}) collective-permute-start(bf16[768,128]{1,0:T(8,128)(2,1)} %get-tuple-element.35.refs_2_), channel_id=1, source_target_pairs={{0,8},{8,0},{16,24},{24,16},{32,40},{40,32},{48,56},{56,48},{64,72... | collective-permute-start | bytes 589832 | tf_op jit(solution)/shard_map/ppermute | solution.py:572
  6.9 6.5 %collective-permute-start.2 = (f32[24,16]{1,0:T(8,128)}, f32[24,16]{1,0:T(8,128)S(1)}, u32[]{:S(2)}, u32[]{:S(2)}) collective-permute-start(f32[24,16]{1,0:T(8,128)} %get-tuple-element.36), channel_id=1, source_target_pairs={{0,1},{1,2},{2,3},{3,4},{4,5},{5,6},{6,7},{7,0},{8,9},{9,10},{10,1... | collective-permute-start | bytes 4616 | tf_op jit(solution)/shard_map/ppermute | solution.py:556
  7.8 5.5 %collective-permute-start.3 = (f32[24,16]{1,0:T(8,128)}, f32[24,16]{1,0:T(8,128)S(1)}, u32[]{:S(2)}, u32[]{:S(2)}) collective-permute-start(f32[24,16]{1,0:T(8,128)} %get-tuple-element.36), channel_id=1, source_target_pairs={{0,7},{1,0},{2,1},{3,2},{4,3},{5,4},{6,5},{7,6},{8,15},{9,8},{10,9... | collective-permute-start | bytes 4616 | tf_op jit(solution)/shard_map/ppermute | solution.py:557
  14.2 3.5 %collective-permute-start.4 = (bf16[768,128]{1,0:T(8,128)(2,1)S(1)}, bf16[768,128]{1,0:T(8,128)(2,1)S(1)}, u32[]{:S(2)}, u32[]{:S(2)}) collective-permute-start(bf16[768,128]{1,0:T(8,128)(2,1)S(1)} %collective-permute-done), channel_id=1, source_target_pairs={{0,8},{8,0},{16,24},{24,16},{32,40},{40,32},{48,56},{56,48},{64,72... | collective-permute-start | bytes 589832 | tf_op jit(solution)/shard_map/ppermute | solution.py:572
  15.4 9.7 %collective-permute-start.8 = (bf16[768,128]{1,0:T(8,128)(2,1)}, bf16[768,128]{1,0:T(8,128)(2,1)S(1)}, u32[]{:S(2)}, u32[]{:S(2)}) collective-permute-start(bf16[768,128]{1,0:T(8,128)(2,1)} %get-tuple-element.44), channel_id=1, source_target_pairs={{0,4},{1,5},{2,6},{3,7},{4,0},{5,1},{6,2},{7,3},{8,12},{9,13},{10,... | collective-permute-start | bytes 589832 | tf_op jit(solution)/shard_map/ppermute | solution.py:577
  18.6 36.0 %copy-start.2 = (s32[128,128]{1,0:T(8,128)S(1)}, s32[128,128]{1,0:T(8,128)}, u32[]{:S(2)}) copy-start(s32[128,128]{1,0:T(8,128)} %pattern_ref.1) | copy-start | bytes 196612
  18.7 14.7 %collective-permute-start.7 = (bf16[3072,128]{1,0:T(8,128)(2,1)S(1)}, bf16[3072,128]{1,0:T(8,128)(2,1)S(1)}, u32[]{:S(2)}, u32[]{:S(2)}) collective-permute-start(bf16[3072,128]{1,0:T(8,128)(2,1)S(1)} %pad_maximum_fusion.refs_0_), channel_id=1, source_target_pairs={{0,16},{8,120},{16,32},{24,8},{32,48},{40,24},{48,64},{56,40},{64,... | collective-permute-start | bytes 2359304 | tf_op jit(solution)/shard_map/ppermute | solution.py:569
  24.4 3.6 %collective-permute-start.5 = (f32[24,48]{1,0:T(8,128)S(1)}, f32[24,48]{1,0:T(8,128)S(1)}, u32[]{:S(2)}, u32[]{:S(2)}) collective-permute-start(f32[24,48]{1,0:T(8,128)S(1)} %pad_maximum_fusion.3), channel_id=1, source_target_pairs={{0,248},{8,16},{16,8},{24,32},{32,24},{40,48},{48,40},{56,64},{64,... | collective-permute-start | bytes 13832 | tf_op jit(solution)/shard_map/ppermute | solution.py:551
  24.4 3.6 %collective-permute-start.6 = (f32[24,48]{1,0:T(8,128)S(1)}, f32[24,48]{1,0:T(8,128)S(1)}, u32[]{:S(2)}, u32[]{:S(2)}) collective-permute-start(f32[24,48]{1,0:T(8,128)S(1)} %pad_maximum_fusion.3), channel_id=1, source_target_pairs={{0,8},{8,0},{16,24},{24,16},{32,40},{40,32},{48,56},{56,48},{64,72... | collective-permute-start | bytes 13832 | tf_op jit(solution)/shard_map/ppermute | solution.py:549
  33.4 18.2 %collective-permute-start.9 = (bf16[3072,128]{1,0:T(8,128)(2,1)S(1)}, bf16[3072,128]{1,0:T(8,128)(2,1)S(1)}, u32[]{:S(2)}, u32[]{:S(2)}) collective-permute-start(bf16[3072,128]{1,0:T(8,128)(2,1)S(1)} %collective-permute-done.7.refs_1_), channel_id=1, source_target_pairs={{0,16},{8,120},{16,32},{24,8},{32,48},{40,24},{48,64},{56,40},{64,... | collective-permute-start | bytes 2359304 | tf_op jit(solution)/shard_map/ppermute | solution.py:569
  36.5 11.7 %collective-permute-start.12 = (bf16[1536,128]{1,0:T(8,128)(2,1)S(1)}, bf16[1536,128]{1,0:T(8,128)(2,1)S(1)}, u32[]{:S(2)}, u32[]{:S(2)}) collective-permute-start(bf16[1536,128]{1,0:T(8,128)(2,1)S(1)} %pad_maximum_fusion.1.near_ref), channel_id=1, source_target_pairs={{0,3},{1,0},{2,1},{3,2},{4,7},{5,4},{6,5},{7,6},{8,11},{9,8},{10,9... | collective-permute-start | bytes 1179656 | tf_op jit(solution)/shard_map/ppermute | solution.py:593
  40.2 11.4 %collective-permute-start.13 = (bf16[1536,128]{1,0:T(8,128)(2,1)S(1)}, bf16[1536,128]{1,0:T(8,128)(2,1)S(1)}, u32[]{:S(2)}, u32[]{:S(2)}) collective-permute-start(bf16[1536,128]{1,0:T(8,128)(2,1)S(1)} %pad_maximum_fusion.1.near_ref), channel_id=1, source_target_pairs={{0,1},{1,2},{2,3},{3,0},{4,5},{5,6},{6,7},{7,4},{8,9},{9,10},{10,1... | collective-permute-start | bytes 1179656 | tf_op jit(solution)/shard_map/ppermute | solution.py:594
  40.3 3.5 %collective-permute-start.10 = (f32[16,48]{1,0:T(8,128)S(1)}, f32[16,48]{1,0:T(8,128)S(1)}, u32[]{:S(2)}, u32[]{:S(2)}) collective-permute-start(f32[16,48]{1,0:T(8,128)S(1)} %get-tuple-element.69), channel_id=1, source_target_pairs={{0,248},{8,16},{16,8},{24,32},{32,24},{40,48},{48,40},{56,64},{64,... | collective-permute-start | bytes 9224 | tf_op jit(solution)/shard_map/ppermute | solution.py:551
  40.3 4.2 %collective-permute-start.11 = (f32[16,48]{1,0:T(8,128)S(1)}, f32[16,48]{1,0:T(8,128)S(1)}, u32[]{:S(2)}, u32[]{:S(2)}) collective-permute-start(f32[16,48]{1,0:T(8,128)S(1)} %get-tuple-element.70), channel_id=1, source_target_pairs={{0,8},{8,0},{16,24},{24,16},{32,40},{40,32},{48,56},{56,48},{64,72... | collective-permute-start | bytes 9224 | tf_op jit(solution)/shard_map/ppermute | solution.py:549
  43.8 17.9 %collective-permute-start.17 = (bf16[3072,128]{1,0:T(8,128)(2,1)S(1)}, bf16[3072,128]{1,0:T(8,128)(2,1)S(1)}, u32[]{:S(2)}, u32[]{:S(2)}) collective-permute-start(bf16[3072,128]{1,0:T(8,128)(2,1)S(1)} %collective-permute-done.7.refs_1_), channel_id=1, source_target_pairs={{0,8},{8,0},{16,24},{24,16},{32,40},{40,32},{48,56},{56,48},{64,72... | collective-permute-start | bytes 2359304 | tf_op jit(solution)/shard_map/ppermute | solution.py:572
  51.6 16.8 %collective-permute-start.14 = (bf16[3072,128]{1,0:T(8,128)(2,1)S(1)}, bf16[3072,128]{1,0:T(8,128)(2,1)S(1)}, u32[]{:S(2)}, u32[]{:S(2)}) collective-permute-start(bf16[3072,128]{1,0:T(8,128)(2,1)S(1)} %collective-permute-done.9.refs_1_), channel_id=1, source_target_pairs={{0,16},{8,120},{16,32},{24,8},{32,48},{40,24},{48,64},{56,40},{64,... | collective-permute-start | bytes 2359304 | tf_op jit(solution)/shard_map/ppermute | solution.py:569
  51.6 22.8 %collective-permute-start.22 = (bf16[3072,128]{1,0:T(8,128)(2,1)S(1)}, bf16[3072,128]{1,0:T(8,128)(2,1)S(1)}, u32[]{:S(2)}, u32[]{:S(2)}) collective-permute-start(bf16[3072,128]{1,0:T(8,128)(2,1)S(1)} %collective-permute-done.9.refs_1_), channel_id=1, source_target_pairs={{0,8},{8,0},{16,24},{24,16},{32,40},{40,32},{48,56},{56,48},{64,72... | collective-permute-start | bytes 2359304 | tf_op jit(solution)/shard_map/ppermute | solution.py:572
  51.7 7.0 %collective-permute-start.16 = (bf16[1536,128]{1,0:T(8,128)(2,1)S(1)}, bf16[1536,128]{1,0:T(8,128)(2,1)S(1)}, u32[]{:S(2)}, u32[]{:S(2)}) collective-permute-start(bf16[1536,128]{1,0:T(8,128)(2,1)S(1)} %broadcast_select_fusion), channel_id=1, source_target_pairs={{0,1},{1,2},{2,3},{3,0},{4,5},{5,6},{6,7},{7,4},{8,11},{9,8},{10,9... | collective-permute-start | bytes 1179656 | tf_op jit(solution)/shard_map/ppermute | solution.py:601
  52.7 4.0 %collective-permute-start.15 = (f32[16,128]{1,0:T(8,128)S(1)}, f32[16,128]{1,0:T(8,128)S(1)}, u32[]{:S(2)}, u32[]{:S(2)}) collective-permute-start(f32[16,128]{1,0:T(8,128)S(1)} %concatenate.22), channel_id=1, source_target_pairs={{0,4},{1,5},{2,6},{3,7},{4,0},{5,1},{6,2},{7,3},{8,12},{9,13},{10,... | collective-permute-start | bytes 24584 | tf_op jit(solution)/shard_map/ppermute | solution.py:603
  68.6 12.9 %copy-start = (bf16[768,128]{1,0:T(8,128)(2,1)S(1)}, bf16[768,128]{1,0:T(8,128)(2,1)}, u32[]{:S(2)}) copy-start(bf16[768,128]{1,0:T(8,128)(2,1)} %get-tuple-element.35.refs_2_) | copy-start | bytes 589828
  68.6 12.0 %collective-permute-start.21 = (bf16[1536,128]{1,0:T(8,128)(2,1)S(1)}, bf16[1536,128]{1,0:T(8,128)(2,1)S(1)}, u32[]{:S(2)}, u32[]{:S(2)}) collective-permute-start(bf16[1536,128]{1,0:T(8,128)(2,1)S(1)} %shard_map.109), channel_id=1, source_target_pairs={{0,16},{8,120},{16,32},{24,8},{32,48},{40,24},{48,64},{56,40},{64,... | collective-permute-start | bytes 1179656 | tf_op jit(solution)/shard_map/ppermute | solution.py:569
  71.6 9.8 %collective-permute-start.23 = (bf16[3072,128]{1,0:T(8,128)(2,1)S(1)}, bf16[3072,128]{1,0:T(8,128)(2,1)S(1)}, u32[]{:S(2)}, u32[]{:S(2)}) collective-permute-start(bf16[3072,128]{1,0:T(8,128)(2,1)S(1)} %collective-permute-done.14.buffer_ref.refs_3_), channel_id=1, source_target_pairs={{0,8},{8,0},{16,24},{24,16},{32,40},{40,32},{48,56},{56,48},{64,72... | collective-permute-start | bytes 2359304 | tf_op jit(solution)/shard_map/ppermute | solution.py:572
  72.9 6.5 %collective-permute-start.18 = (f32[32,128]{1,0:T(8,128)S(1)}, f32[32,128]{1,0:T(8,128)S(1)}, u32[]{:S(2)}, u32[]{:S(2)}) collective-permute-start(f32[32,128]{1,0:T(8,128)S(1)} %pad_maximum_fusion.2.near_ref), channel_id=1, source_target_pairs={{0,3},{1,0},{2,1},{3,2},{4,7},{5,4},{6,5},{7,6},{8,11},{9,8},{10,9... | collective-permute-start | bytes 49160 | tf_op jit(solution)/shard_map/ppermute | solution.py:612
  73.0 6.5 %collective-permute-start.19 = (f32[32,128]{1,0:T(8,128)S(1)}, f32[32,128]{1,0:T(8,128)S(1)}, u32[]{:S(2)}, u32[]{:S(2)}) collective-permute-start(f32[32,128]{1,0:T(8,128)S(1)} %pad_maximum_fusion.2.near_ref), channel_id=1, source_target_pairs={{0,1},{1,2},{2,3},{3,0},{4,5},{5,6},{6,7},{7,4},{8,9},{9,10},{10,1... | collective-permute-start | bytes 49160 | tf_op jit(solution)/shard_map/ppermute | solution.py:612
  74.4 5.1 %collective-permute-start.20 = (f32[32,128]{1,0:T(8,128)S(1)}, f32[32,128]{1,0:T(8,128)S(1)}, u32[]{:S(2)}, u32[]{:S(2)}) collective-permute-start(f32[32,128]{1,0:T(8,128)S(1)} %pad_maximum_fusion.2.near_ref), channel_id=1, source_target_pairs={{0,2},{1,3},{2,0},{3,1},{4,6},{5,7},{6,4},{7,5},{8,10},{9,11},{10,... | collective-permute-start | bytes 49160 | tf_op jit(solution)/shard_map/ppermute | solution.py:612
  80.6 6.6 %collective-permute-start.24 = (bf16[1536,128]{1,0:T(8,128)(2,1)S(1)}, bf16[1536,128]{1,0:T(8,128)(2,1)S(1)}, u32[]{:S(2)}, u32[]{:S(2)}) collective-permute-start(bf16[1536,128]{1,0:T(8,128)(2,1)S(1)} %collective-permute-done.21.refs_1_), channel_id=1, source_target_pairs={{0,8},{8,0},{16,24},{24,16},{32,40},{40,32},{48,56},{56,48},{64,72... | collective-permute-start | bytes 1179656 | tf_op jit(solution)/shard_map/ppermute | solution.py:572

commit v4 on v3

--- a/solution.py
+++ b/solution.py
@@ -177,37 +177,50 @@
     )(pattern)
 
 
-def spread_tile(packed, offset, both, store):
-    both[0:PACK, :] = packed
-    both[PACK : 2 * PACK, :] = swap_halves(packed)
+SPAN = 2 * PACK + BS
+
+
+def prepare(packed, both, base):
+    both[pl.ds(base, PACK), :] = packed
+    both[pl.ds(base + PACK, PACK), :] = swap_halves(packed)
+    both[pl.ds(base + 2 * PACK, BS), :] = jnp.zeros((BS, 128), BF16)
+
+
+def spread_tile(offset, both, base, store):
     left = lax.broadcasted_iota(jnp.int32, (BS, 2 * BS), 1) < BS
     for r in range(4):
         for first in (0, 4):
             blocks = []
             for c in range(first, first + 4):
-                at0 = pl.multiple_of(offset(r, 2 * c), BS)
-                at1 = pl.multiple_of(offset(r, 2 * c + 1), BS)
+                at0 = pl.multiple_of(base + offset(r, 2 * c), BS)
+                at1 = pl.multiple_of(base + offset(r, 2 * c + 1), BS)
                 blocks.append(jnp.where(left, both[pl.ds(at0, BS), :], both[pl.ds(at1, BS), :]))
             for k, block in enumerate(blocks):
                 store(r, first + k, block)
 
 
-def spread_kernel(table_ref, near_ref, next_ref, last_ref, far_ref, out_ref, both):
+def spread_kernel(table_ref, near_ref, next_ref, last_ref, far_ref, out_ref, both, table, sem):
+    copy = pltpu.make_async_copy(table_ref, table, sem)
+    copy.start()
     col = lax.axis_index("col")
     y, x = col // 4, col % 4
-    both[2 * PACK :, :] = jnp.zeros((BS, 128), BF16)
-    for part, dx in ((near_ref, 0), (next_ref, 1), (last_ref, 3), (far_ref, 2)):
-
-        def one(j, _, part=part, dx=dx):
+    parts = ((near_ref, 0), (next_ref, 1), (last_ref, 3), (far_ref, 2))
+    for k, (part, _) in enumerate(parts):
+        for j in range(2):
+            prepare(part[j * PACK : j * PACK + PACK, :], both, (2 * k + j) * SPAN)
+    copy.wait()
+    for k, (_, dx) in enumerate(parts):
+
+        def one(j, _, k=k, dx=dx):
             source = (y + j) % 2 * 4 + (x + dx) % 4
-            packed = part[pl.ds(pl.multiple_of(j * PACK, PACK), PACK), :]
 
             def store(r, c, block):
                 out_ref[
                     source * 4 + c // 2, r * BS : (r + 1) * BS, c % 2 * 128 : c % 2 * 128 + 128
                 ] = block
 
-            spread_tile(packed, lambda r, c: table_ref[r, source * 16 + c], both, store)
+            base = pl.multiple_of((2 * k + j) * SPAN, BS)
+            spread_tile(lambda r, c: table[r, source * 16 + c], both, base, store)
             return 0
 
         lax.fori_loop(0, 2, one, 0)
@@ -218,10 +231,14 @@
     return pl.pallas_call(
         spread_kernel,
         out_shape=jax.ShapeDtypeStruct((32, 256, 256), BF16),
-        in_specs=[pl.BlockSpec(memory_space=pltpu.SMEM)] + [vmem] * len(parts),
+        in_specs=[pl.BlockSpec(memory_space=pl.ANY)] + [vmem] * len(parts),
         out_specs=vmem,
-        scratch_shapes=[pltpu.VMEM((2 * PACK + BS, 128), BF16)],
-        compiler_params=pltpu.CompilerParams(vmem_limit_bytes=4 * 2**20),
+        scratch_shapes=[
+            pltpu.VMEM((8 * SPAN, 128), BF16),
+            pltpu.SMEM((8, 128), jnp.int32),
+            pltpu.SemaphoreType.DMA,
+        ],
+        compiler_params=pltpu.CompilerParams(vmem_limit_bytes=8 * 2**20),
         cost_estimate=FREE,
     )(table, *parts)
 
@@ -233,55 +250,101 @@
     return high, middle, (rest - middle.astype(F32)).astype(BF16)
 
 
-def accumulate_kernel(groups, start, local, after, table_ref, h_ref, *refs):
-    refs = list(refs)
-    before = None if start else refs.pop(0)
-    atoms, mine = (refs.pop(0), refs.pop(0)) if local else (None, None)
-    parts = [refs.pop(0) for _ in groups]
-    if after:
-        refs.pop(0)
-    out_ref, token_ref, both, dense, wide, table, sem = refs[:7]
-    token_ref[...] = jnp.zeros_like(token_ref)
-    copy = pltpu.make_async_copy(table_ref, table, sem)
-    copy.start()
+def tiles_of(groups):
     row = lax.axis_index("row")
     y, z, core = row // 16, row // 2 % 8, row % 2
     direction = 1 - 2 * core
-    both[2 * PACK :, :] = jnp.zeros((BS, 128), BF16)
     tiles = []
     for count, steps, flip in groups:
         for j in range(count):
             tiles.append(
                 ((y + j) % 2 * 8 + (z + steps * direction + 8) % 8) * 2 + (core + flip + j // 2) % 2
             )
-    for at, tile in enumerate(tiles):
+    return tiles
+
+
+def prepare_all(parts, groups, both):
+    at = 0
+    for part, (count, _, _) in zip(parts, groups):
+        for j in range(count):
+            prepare(part[j * PACK : j * PACK + PACK, :], both, at * SPAN)
+            at += 1
+
+
+def spread_all(groups, tiles, table, both, dense, first=0):
+    at = 0
+    for count, _, _ in groups:
+
+        def one(j, _, at=at, count=count):
+            tile = tiles[at]
+            for k in range(1, count):
+                tile = jnp.where(j == k, tiles[at + k], tile)
+            row = pl.multiple_of((first + at + j) * 256, 256)
+
+            def store(r, c, block):
+                dense[pl.ds(row + r * BS, BS), c * 128 : c * 128 + 128] = block
+
+            base = pl.multiple_of((at + j) * SPAN, BS)
+            spread_tile(lambda r, c: table[tile, r * 16 + c], both, base, store)
+            return 0
+
+        lax.fori_loop(0, count, one, 0)
+        at += count
+
+
+def unpack_kernel(groups, table_ref, *refs):
+    parts, (dense, both, table, sem) = refs[: len(groups)], refs[len(groups) :]
+    copy = pltpu.make_async_copy(table_ref, table, sem)
+    copy.start()
+    prepare_all(parts, groups, both)
+    copy.wait()
+    spread_all(groups, tiles_of(groups), table, both, dense)
+
+
+def unpack(table, parts, groups):
+    vmem = pl.BlockSpec(memory_space=pltpu.VMEM)
+    count = sum(g[0] for g in groups)
+    return pl.pallas_call(
+        functools.partial(unpack_kernel, groups),
+        out_shape=jax.ShapeDtypeStruct((256 * count, 1024), BF16),
+        in_specs=[pl.BlockSpec(memory_space=pl.ANY)] + [vmem] * len(parts),
+        out_specs=vmem,
+        scratch_shapes=[
+            pltpu.VMEM((count * SPAN, 128), BF16),
+            pltpu.SMEM((32, 64), jnp.int32),
+            pltpu.SemaphoreType.DMA,
+        ],
+        compiler_params=pltpu.CompilerParams(vmem_limit_bytes=8 * 2**20),
+        cost_estimate=FREE,
+    )(table, *parts)
+
+
+def accumulate_kernel(ready, groups, start, local, last, table_ref, h_ref, *refs):
+    refs = list(refs)
+    before = None if start else refs.pop(0)
+    atoms, mine = (refs.pop(0), refs.pop(0)) if local else (None, None)
+    early = refs.pop(0) if ready else None
+    parts = [refs.pop(0) for _ in groups]
+    out_ref, token_ref, both, dense, wide, table, sem = refs[:7]
+    copy = pltpu.make_async_copy(table_ref, table, sem)
+    copy.start()
+    token_ref[...] = jnp.zeros_like(token_ref)
+    done, tiles = tiles_of(ready), tiles_of(groups)
+    prepare_all(parts, groups, both)
+    if local:
+        prepare(mine[0:PACK, :], both, len(tiles) * SPAN)
+    for at, tile in enumerate(done + tiles):
         wide[:, at * 256 : at * 256 + 256] = h_ref[tile]
     copy.wait()
-    start_at = 0
-    for part, (count, _, _) in zip(parts, groups):
-
-        def one(j, _, part=part, start_at=start_at, count=count):
-            tile = tiles[start_at]
-            for k in range(1, count):
-                tile = jnp.where(j == k, tiles[start_at + k], tile)
-            packed = part[pl.ds(pl.multiple_of(j * PACK, PACK), PACK), :]
-            base = pl.multiple_of((start_at + j) * 256, 256)
-
-            def store(r, c, block):
-                dense[pl.ds(base + r * BS, BS), c * 128 : c * 128 + 128] = block
-
-            spread_tile(packed, lambda r, c: table[tile, r * 16 + c], both, store)
-            return 0
-
-        lax.fori_loop(0, count, one, 0)
-        start_at += count
+    spread_all(groups, tiles, table, both, dense)
     if local:
         own, held = refs[7], refs[8]
+        row = lax.axis_index("row")
 
         def store(r, c, block):
             own[r * BS : r * BS + BS, c * 128 : c * 128 + 128] = block
 
-        spread_tile(mine[0:PACK, :], lambda r, c: table[row, r * 16 + c], both, store)
+        spread_tile(lambda r, c: table[row, r * 16 + c], both, len(tiles) * SPAN, store)
         values = atoms[...]
         lane_atom = lax.broadcasted_iota(jnp.int32, (256, 128), 1) // 4
         row_atom = lax.broadcasted_iota(jnp.int32, (256, 128), 0) // 8
@@ -299,48 +362,64 @@
         chosen = jnp.where(place == m, 1.0, 0.0).astype(BF16)
         for k, t in enumerate(split3(jnp.concatenate(tall, axis=1))):
             held[k] = jnp.dot(t, chosen, preferred_element_type=F32).astype(BF16)
-
-    def column(n, _):
-        lanes = pl.ds(pl.multiple_of(n * 256, 256), 256)
-        total = jnp.dot(wide[...], dense[:, lanes], preferred_element_type=F32)
+    copies = []
+    for n in range(4):
+        lanes = slice(n * 256, n * 256 + 256)
+        total = jnp.dot(
+            wide[:, len(done) * 256 :], dense[:, lanes], preferred_element_type=F32
+        )
+        if ready:
+            total += jnp.dot(
+                wide[:, : len(done) * 256], early[:, lanes], preferred_element_type=F32
+            )
         if local:
             for k in range(3):
                 total += jnp.dot(held[k], own[:, lanes], preferred_element_type=F32)
         if before is not None:
             total += before[:, lanes]
-        out_ref[:, lanes] = total
-        return 0
-
-    lax.fori_loop(0, 4, column, 0)
-
-
-def accumulate(table, h_dense, before, parts, groups, local=(), after=None):
+        if last:
+            result, sems = refs[7], refs[8]
+            result[:, lanes] = total
+            copies.append(
+                pltpu.make_async_copy(result.at[:, lanes], out_ref.at[:, lanes], sems.at[n])
+            )
+            copies[-1].start()
+        else:
+            out_ref[:, lanes] = total
+    for copy in copies:
+        copy.wait()
+
+
+def accumulate(table, h_dense, before, parts, groups, local=(), ready=(), early=None, last=False):
     vmem = pl.BlockSpec(memory_space=pltpu.VMEM)
     operands = [h_dense]
     if before is not None:
         operands.append(before)
-    operands += list(local) + parts
-    specs = [pl.BlockSpec(memory_space=pl.ANY)] + [vmem] * len(operands)
-    if after is not None:
-        operands.append(after)
-        specs.append(pl.BlockSpec(memory_space=pl.ANY))
-    depth = 256 * sum(g[0] for g in groups)
+    operands += list(local)
+    if ready:
+        operands.append(early)
+    operands += parts
+    count = sum(g[0] for g in groups)
     scratch = [
-        pltpu.VMEM((2 * PACK + BS, 128), BF16),
-        pltpu.VMEM((depth, 1024), BF16),
-        pltpu.VMEM((256, depth), BF16),
+        pltpu.VMEM(((count + bool(local)) * SPAN, 128), BF16),
+        pltpu.VMEM((256 * count, 1024), BF16),
+        pltpu.VMEM((256, 256 * (count + sum(g[0] for g in ready))), BF16),
         pltpu.SMEM((32, 64), jnp.int32),
         pltpu.SemaphoreType.DMA,
     ]
     if local:
         scratch += [pltpu.VMEM((256, 1024), BF16), pltpu.VMEM((3, 256, 256), BF16)]
+    if last:
+        scratch += [pltpu.VMEM((256, 1024), F32), pltpu.SemaphoreType.DMA((4,))]
     return pl.pallas_call(
-        functools.partial(accumulate_kernel, groups, before is None, bool(local), after is not None),
+        functools.partial(
+            accumulate_kernel, ready, groups, before is None, bool(local), last
+        ),
         out_shape=(jax.ShapeDtypeStruct((256, 1024), F32), jax.ShapeDtypeStruct((8, 128), F32)),
-        in_specs=specs,
-        out_specs=(vmem, vmem),
+        in_specs=[pl.BlockSpec(memory_space=pl.ANY)] + [vmem] * len(operands),
+        out_specs=(pl.BlockSpec(memory_space=pltpu.HBM) if last else vmem, vmem),
         scratch_shapes=scratch,
-        compiler_params=pltpu.CompilerParams(vmem_limit_bytes=12 * 2**20),
+        compiler_params=pltpu.CompilerParams(vmem_limit_bytes=14 * 2**20),
         cost_estimate=FREE,
     )(table, *operands)
 
@@ -397,13 +476,15 @@
 ROWS = [(a, 2 * bh + bl) for bl in range(2) for a in range(4) for bh in range(2)]
 
 
-def grid_kernel(info_ref, external_hbm, density_ref, share_ref, gx_ref, gy_ref, gz_ref, u_ref, s_ref, external_ref, sem):
+def grid_kernel(info_ref, external_hbm, density_ref, own_ref, near_ref, far_ref, gx_ref, gy_ref, gz_ref, u_ref, s_ref, external_ref, held_ref, sem):
     lanes = 256
     copy = pltpu.make_async_copy(external_hbm, external_ref, sem)
     copy.start()
     cell = lax.broadcasted_iota(jnp.int32, (CUBE, lanes), 0).astype(F32)
     place = lax.broadcasted_iota(jnp.int32, (1, lanes), 1)
-    off_x = info_ref[16:17, :] + CUBE * (place // 48 - 1).astype(F32)
+    turn = 1 - 2 * (lax.axis_index("row") % 2)
+    beside = jnp.where(place < 48, 0, jnp.where(place < 96, turn, -turn))
+    off_x = info_ref[16:17, :] + CUBE * beside.astype(F32)
     off_y = info_ref[17:18, :] + CUBE * (place % 48 // 16 - 1).astype(F32)
     off_z = info_ref[18:19, :]
     for n, value in enumerate(powers(cell - off_x + CUBE // 2)):
@@ -455,10 +536,16 @@
         return 0
 
     lax.fori_loop(0, CUBE // chunk, step, 0)
+    col = lax.axis_index("col")
     for at, (a, b) in enumerate(ROWS):
-        share_ref[at : at + 1, :] = (
+        held_ref[at : at + 1, :] = (
             jnp.sum(s_ref[a] * gy_ref[b], axis=0, keepdims=True) * SCALE**3
         )
+    share = held_ref[...]
+    lane = lax.broadcasted_iota(jnp.int32, (16, 128), 1)
+    for k, ref in enumerate((own_ref, near_ref, far_ref)):
+        part = share if k == 0 else pltpu.roll(share, lanes - 48 * k, 1)
+        ref[...] = pltpu.roll(jnp.where(lane < 48, part[:, :128], 0.0), (col + 7) % 8 * 16, 1)
 
 
 def grid_part(info, external):
@@ -467,10 +554,10 @@
         grid_kernel,
         out_shape=(
             jax.ShapeDtypeStruct(external.shape, F32),
-            jax.ShapeDtypeStruct((16, 256), F32),
+            *[jax.ShapeDtypeStruct((16, 128), F32)] * 3,
         ),
         in_specs=[vmem, pl.BlockSpec(memory_space=pltpu.HBM)],
-        out_specs=(vmem, vmem),
+        out_specs=(vmem,) * 4,
         scratch_shapes=[
             pltpu.VMEM((4, CUBE, 256), F32),
             pltpu.VMEM((4, CUBE, 256), F32),
@@ -478,6 +565,7 @@
             pltpu.VMEM((4, CUBE, 256), F32),
             pltpu.VMEM((4, CUBE, 256), F32),
             pltpu.VMEM(external.shape, F32),
+            pltpu.VMEM((16, 256), F32),
             pltpu.SemaphoreType.DMA,
         ],
         compiler_params=pltpu.CompilerParams(vmem_limit_bytes=12 * 2**20),
@@ -485,39 +573,32 @@
     )(info, external)
 
 
-def collect_kernel(near_ref, next_ref, last_ref, far_ref, atoms_ref, mine_ref):
+def finish_kernel(atoms_ref, mine_ref):
     col = lax.axis_index("col")
-    y, x = col // 4, col % 4
-    total = jnp.zeros((16, 128), F32)
-    for ref, dx in ((near_ref, 0), (next_ref, 1), (last_ref, 3), (far_ref, 2)):
-        for j in range(2):
-            source = (y + j) % 2 * 4 + (x + dx) % 4
-            total += pltpu.roll(ref[16 * j : 16 * j + 16, :], (source + 7) % 8 * 16, 1)
-    atoms_ref[...] = total
-    mine = pltpu.roll(total, (8 - col) % 8 * 16, 1)
+    mine = pltpu.roll(atoms_ref[...], (8 - col) % 8 * 16, 1)
     lane = lax.broadcasted_iota(jnp.int32, (16, 128), 1)
     l = lax.broadcasted_iota(jnp.int32, (128, 64), 0)
     m = lax.broadcasted_iota(jnp.int32, (128, 64), 1)
     move = jnp.where(l % 4 == m % 4, 1.0, 0.0)
     rho = lax.broadcasted_iota(jnp.int32, (16, 64), 0)
     match = lax.broadcasted_iota(jnp.int32, (16, 64), 1) // 4 == rho % 8 // 2 * 4 + rho % 2 * 2 + rho // 8
+    parts = jnp.concatenate([jnp.where(lane // 4 == i, mine, 0.0) for i in range(4)], axis=0)
+    values = jnp.dot(parts, move, precision=PRECISE, preferred_element_type=F32)
     for i in range(4):
-        value = jnp.dot(
-            jnp.where(lane // 4 == i, mine, 0.0), move, precision=PRECISE, preferred_element_type=F32
-        )
-        mine_ref[i : i + 1, :] = jnp.sum(jnp.where(match, value, 0.0), axis=0, keepdims=True)
-
-
-def collect(parts):
+        value = jnp.where(match, values[16 * i : 16 * i + 16, :], 0.0)
+        mine_ref[i : i + 1, :] = jnp.sum(value, axis=0, keepdims=True)
+
+
+def finish(atoms):
     vmem = pl.BlockSpec(memory_space=pltpu.VMEM)
     return pl.pallas_call(
-        collect_kernel,
-        out_shape=(jax.ShapeDtypeStruct((16, 128), F32), jax.ShapeDtypeStruct((4, 64), F32)),
-        in_specs=[vmem] * 4,
-        out_specs=(vmem, vmem),
+        finish_kernel,
+        out_shape=jax.ShapeDtypeStruct((4, 64), F32),
+        in_specs=[vmem],
+        out_specs=vmem,
         compiler_params=pltpu.CompilerParams(vmem_limit_bytes=2 * 2**20),
         cost_estimate=FREE,
-    )(*parts)
+    )(atoms)
 
 
 def row_of(y, z, core):
@@ -544,12 +625,9 @@
     return [(i, (i + step) % size) for i in range(size)]
 
 
-def from_rows(core, last, first):
-    mine = jnp.where(core == 0, last, first)
-    near = lax.ppermute(mine, "row", ACROSS_CORES)
-    mine = jnp.where(core == 0, first, last)
-    far = lax.ppermute(mine, "row", [(i, (i + 2 * (i % 2) - 1) % 32) for i in range(32)])
-    return jnp.where(core == 0, far, near), jnp.where(core == 0, near, far)
+def to_rows(near, far):
+    near = lax.ppermute(near, "row", ACROSS_CORES)
+    return near, lax.ppermute(far, "row", [(i, (i + 2 * (i % 2) - 1) % 32) for i in range(32)])
 
 
 def from_neighbours(last, first, axis, size):
@@ -578,44 +656,45 @@
     before, after = from_neighbours(info, info, "col", 8)
     info = jnp.concatenate([before, info, after], axis=1)
     pc = swap(pp)
-    h0 = jnp.concatenate([hp, hy], axis=0)
-    py, pc, info = together((py, pc, info))
+    near, far = to_rows(info, info)
+    py, pc, info, hy, table_p, table_h = together((py, pc, info, hy, table_p, table_h))
+    info = jnp.concatenate([info, near, far, jnp.zeros((24, 112), F32)], axis=1)
     q = jnp.concatenate([pp, py, pc, swap(py)], axis=0)
     q, info = together((q, info))
+    h0 = jnp.concatenate([hp, hy], axis=0)
 
     q1 = step(q)
-    before, after = from_rows(core, info, info)
-    info = jnp.concatenate([before, info, after, jnp.zeros((24, 112), F32)], axis=1)
-    density, share = grid_part(info, external)
-    q1, share, h0 = together((q1, share, h0))
-
-    q2, x1 = step(q1), swap(q1)
     h_next = lax.ppermute(h0, "col", col_pairs(0, 3))
     h_last = lax.ppermute(h0, "col", col_pairs(0, 1))
-    before, after = from_rows(core, share[:, 96:144], share[:, 0:48])
-    share = share[:, 48:96] + before + after
-    share = jnp.concatenate([share, jnp.zeros((16, 80), F32)], axis=1)
-    q2, share, h_next, h_last = together((q2, share, h_next, h_last))
+    density, share, near, far = grid_part(info, external)
+    near, far = to_rows(near, far)
+    share = share + near + far
+    q1, share, h_next, h_last = together((q1, share, h_next, h_last))
+
+    q2, x1 = step(q1), swap(q1)
+    h_far = lax.ppermute(jnp.where(core == 0, h_last, h_next), ("row", "col"), ALONG_X)
+    share = share + lax.ppermute(share, "col", col_pairs(1, 0))
+    share = share + lax.ppermute(share, "col", [(i, i ^ 1) for i in range(8)])
+    early_groups = ((4, 0, 0), (4, -1, 0))
+    dense = unpack(table_p, [q, q1], early_groups)
+    q2, dense, share, h_far = together((q2, dense, share, h_far))
+    h_dense = spread_hamiltonian(table_h, [h0, h_next, h_last, h_far])
 
     q3, x2 = step(q2), swap(q2)
-    h_far = lax.ppermute(jnp.where(core == 0, h_last, h_next), ("row", "col"), ALONG_X)
-    h_dense = spread_hamiltonian(table_h, [h0, h_next, h_last, h_far])
-    other = lax.ppermute(share, "col", col_pairs(1, 0))
-    share = jnp.concatenate([share, other], axis=0)
+    atoms = share + lax.ppermute(share, "col", [(i, i ^ 2) for i in range(8)])
     product, done = accumulate(
-        table_p, h_dense, None, [q, q1, x1], ((4, 0, 0), (4, -1, 0), (4, 1, 1))
+        table_p, h_dense, None, [x1], ((4, 1, 1),), ready=early_groups, early=dense
     )
-    q3, share, product = together((q3, share, product))
+    q3, atoms, done = together((q3, atoms, done))
 
     q4 = step(front(q3, done))
     x3 = swap(q3)
-    shares = [share] + [lax.ppermute(share, "col", col_pairs(0, d)) for d in (3, 1, 2)]
+    integrals = finish(atoms)
     product, _ = accumulate(table_p, h_dense, product, [q2, x2], ((4, -2, 0), (4, 2, 1)))
-    atoms, integrals = collect(shares)
-    q4, atoms, product = together((q4, atoms, product))
     product, _ = accumulate(
         table_p, h_dense, product, [q3, x3], ((4, -3, 0), (4, 3, 1)), local=(atoms, pp)
     )
+    q4, product = together((q4, product))
     product, _ = accumulate(table_p, h_dense, product, [q4, swap(q4)], ((2, 4, 0), (2, 4, 1)))
     return (density, integrals, product)
 

time: 92 us -> 85.3 us (0.927)
  waiting for transfers between devices: 20.2 us -> 15.5 us
  Pallas kernels: 32.5 us -> 29.1 us
    ppermute x4, starting transfers between devices: 11.8 us -> 4.34 us  [step(): return lax.ppermute(chain, 'row', ALONG_Z)]
    ppermute x8 -> x7, starting transfers between devices: 4.22 us -> 8.86 us  [the longest x1 2.88 us: on_device(): atoms = share + lax.ppermute(share, 'col', [(i, i ^ 2) for i in range(8)])]
    ppermute x6, starting transfers between devices: 5.3 us -> 8.78 us  [swap(): return lax.ppermute(chain, 'row', ACROSS_CORES)]
    ppermute x8 -> x7, waiting for transfers between devices: 7.88 us -> 4.7 us  [the longest x2 3.07 us: to_rows(): lax.ppermute(far, 'row', [(i, (i + 2 * (i % 2) - 1) % 32) for i in range(...]
    ppermute x1, waiting for transfers between devices: 3.59 us -> 0.55 us  [on_device(): h_next = lax.ppermute(h0, 'col', col_pairs(0, 3))]
    pallas_call x5 -> x6, Pallas kernels: 22.6 us -> 19.8 us  [the longest x4 16.3 us: accumulate(): pl.pallas_call(functools.partial(accumulate_kernel, ready, groups, before...]
    ppermute x1, waiting for transfers between devices: 1.98 us -> 0.01 us  [on_device(): lax.ppermute(jnp.where(core == 0, h_last, h_next), ('row', 'col'), ALONG_X)]
    ppermute x6, waiting for transfers between devices: 0.02 us -> 1.87 us  [swap(): return lax.ppermute(chain, 'row', ACROSS_CORES)]
  transfers between devices with their start and end apart: 25 -> 24, of which waited for: 8 -> 10; matrix products, arithmetic and copies ran while one was open for 2% -> 1% of each run, Pallas kernels for 28% -> 27%
where the time goes in v4:
time: 85.3 us; the launch traced here: 85 us
  starting transfers between devices  36.5 us (43%)
  Pallas kernels  29.1 us (34%)
  waiting for transfers between devices  15.5 us (18%)
  other arithmetic  1.9 us (2%)
  between operations  1.01 us (1%)
  local copies, waits for them, and re-layouts  0.97 us (1%)
    pallas_call x4, Pallas kernels, accumulate(): pl.pallas_call(functools.partial(accumulate_kernel, ready, groups, before...  16.3 us
    ppermute x6, starting transfers between devices, swap(): return lax.ppermute(chain, 'row', ACROSS_CORES)  8.78 us
    ppermute x4, starting transfers between devices, step(): return lax.ppermute(chain, 'row', ALONG_Z)  4.34 us
    ppermute x1, starting transfers between devices, from_neighbours(): after = lax.ppermute(first, axis, ring(axis, size, -1))  3.87 us
    ppermute x4, waiting for transfers between devices, step(): return lax.ppermute(chain, 'row', ALONG_Z)  3.59 us
    ppermute x1, waiting for transfers between devices, on_device(): h_last = lax.ppermute(h0, 'col', col_pairs(0, 1))  3.4 us
    pallas_call x1, Pallas kernels, grid_part(): pl.pallas_call(grid_kernel, out_shape=(jax.ShapeDtypeStruct(external.shap...  3.31 us
    ppermute x1, starting transfers between devices, on_device(): h_next = lax.ppermute(h0, 'col', col_pairs(0, 3))  3.09 us
  transfers between devices with their start and end apart: 24, of which 10 were waited for; matrix products, arithmetic and copies ran while one was open for 1% of the time, Pallas kernels for 27%

profile of v4, /device:TPU:1, one launch (start us, length us, event | category | flops | bytes accessed | tf_op | source)
XLA Modules:
  0.0 85.0 jit_solution(17900389946487932377)
XLA Ops:
  0.6 2.8 %shard_map.103 = (bf16[768,128]{1,0:T(8,128)(2,1)}, bf16[768,128]{1,0:T(8,128)(2,1)}, f32[24,16]{1,0:T(8,128)}) custom-call(s32[128,128]{1,0:T(8,128)} %pattern_ref.1, bf16[256,1024]{1,0:T(8,128)(2,1)} %h_hbm.1, bf16[256,1024]{1,0:T(8,128)(2,1)} %p_hbm.1, f32[4,64]{1,0:T(4,128)} %coef_hbm.1, s32[4]{0:T(128)} %x_hbm.1, s32[4]{0:T(128)} %y_hbm.1, s32[4]{0:T(128)} %z_hbm.1), custom_call_target="tpu_custom_call" | custom-call | tf_op jit(solution)/shard_map/pallas_call | solution.py:101
  3.4 2.2 %collective-permute-start = (bf16[768,128]{1,0:T(8,128)(2,1)}, bf16[768,128]{1,0:T(8,128)(2,1)S(1)}, u32[]{:S(2)}, u32[]{:S(2)}) collective-permute-start(bf16[768,128]{1,0:T(8,128)(2,1)} %get-tuple-element.38.refs_2_), channel_id=1, source_target_pairs={{0,128},{8,136},{16,144},{24,152},{32,160},{40,168},{48,176},{56,1... | collective-permute-start | bytes 589832 | tf_op jit(solution)/shard_map/ppermute | solution.py:654
  5.6 1.2 %collective-permute-start.1 = (bf16[768,128]{1,0:T(8,128)(2,1)}, bf16[768,128]{1,0:T(8,128)(2,1)S(1)}, u32[]{:S(2)}, u32[]{:S(2)}) collective-permute-start(bf16[768,128]{1,0:T(8,128)(2,1)} %get-tuple-element.38.refs_2_), channel_id=1, source_target_pairs={{0,8},{8,0},{16,24},{24,16},{32,40},{40,32},{48,56},{56,48},{64,72... | collective-permute-start | bytes 589832 | tf_op jit(solution)/shard_map/ppermute | solution.py:650
  6.9 2.4 %collective-permute-start.4 = (bf16[768,128]{1,0:T(8,128)(2,1)}, bf16[768,128]{1,0:T(8,128)(2,1)S(1)}, u32[]{:S(2)}, u32[]{:S(2)}) collective-permute-start(bf16[768,128]{1,0:T(8,128)(2,1)} %get-tuple-element.40), channel_id=1, source_target_pairs={{0,4},{1,5},{2,6},{3,7},{4,0},{5,1},{6,2},{7,3},{8,12},{9,13},{10,... | collective-permute-start | bytes 589832 | tf_op jit(solution)/shard_map/ppermute | solution.py:655
  9.2 1.2 %collective-permute-start.2 = (f32[24,16]{1,0:T(8,128)}, f32[24,16]{1,0:T(8,128)S(1)}, u32[]{:S(2)}, u32[]{:S(2)}) collective-permute-start(f32[24,16]{1,0:T(8,128)} %get-tuple-element.39), channel_id=1, source_target_pairs={{0,1},{1,2},{2,3},{3,4},{4,5},{5,6},{6,7},{7,0},{8,9},{9,10},{10,1... | collective-permute-start | bytes 4616 | tf_op jit(solution)/shard_map/ppermute | solution.py:634
  10.4 3.9 %collective-permute-start.3 = (f32[24,16]{1,0:T(8,128)}, f32[24,16]{1,0:T(8,128)S(1)}, u32[]{:S(2)}, u32[]{:S(2)}) collective-permute-start(f32[24,16]{1,0:T(8,128)} %get-tuple-element.39), channel_id=1, source_target_pairs={{0,7},{1,0},{2,1},{3,2},{4,3},{5,4},{6,5},{7,6},{8,15},{9,8},{10,9... | collective-permute-start | bytes 4616 | tf_op jit(solution)/shard_map/ppermute | solution.py:635
  14.3 1.4 %collective-permute-done.2 = f32[24,16]{1,0:T(8,128)S(1)} collective-permute-done((f32[24,16]{1,0:T(8,128)}, f32[24,16]{1,0:T(8,128)S(1)}, u32[]{:S(2)}, u32[]{:S(2)}) %collective-permute-start.2) | collective-permute-done | bytes 1568 | tf_op jit(solution)/shard_map/ppermute | solution.py:634
  15.7 0.0 collective-permute-done.3
  15.7 0.8 pad_maximum_fusion.1
  16.5 1.5 %collective-permute-start.6 = (f32[24,48]{1,0:T(8,128)S(1)}, f32[24,48]{1,0:T(8,128)S(1)}, u32[]{:S(2)}, u32[]{:S(2)}) collective-permute-start(f32[24,48]{1,0:T(8,128)S(1)} %pad_maximum_fusion.1), channel_id=1, source_target_pairs={{0,8},{8,0},{16,24},{24,16},{32,40},{40,32},{48,56},{56,48},{64,72... | collective-permute-start | bytes 13832 | tf_op jit(solution)/shard_map/ppermute | solution.py:629
  17.9 1.6 %collective-permute-start.7 = (f32[24,48]{1,0:T(8,128)S(1)}, f32[24,48]{1,0:T(8,128)S(1)}, u32[]{:S(2)}, u32[]{:S(2)}) collective-permute-start(f32[24,48]{1,0:T(8,128)S(1)} %pad_maximum_fusion.1), channel_id=1, source_target_pairs={{0,248},{8,16},{16,8},{24,32},{32,24},{40,48},{48,40},{56,64},{64,... | collective-permute-start | bytes 13832 | tf_op jit(solution)/shard_map/ppermute | solution.py:630
  19.6 0.8 copy-done.2
  20.4 0.5 shard_map.104
  20.9 0.1 pad.3.clone
  21.0 0.0 collective-permute-done
  21.0 0.0 collective-permute-done.1
  21.0 0.0 collective-permute-done.4
  21.0 4.0 %collective-permute-start.5 = (bf16[768,128]{1,0:T(8,128)(2,1)S(1)}, bf16[768,128]{1,0:T(8,128)(2,1)S(1)}, u32[]{:S(2)}, u32[]{:S(2)}) collective-permute-start(bf16[768,128]{1,0:T(8,128)(2,1)S(1)} %collective-permute-done), channel_id=1, source_target_pairs={{0,8},{8,0},{16,24},{24,16},{32,40},{40,32},{48,56},{56,48},{64,72... | collective-permute-start | bytes 589832 | tf_op jit(solution)/shard_map/ppermute | solution.py:650
  25.0 0.0 collective-permute-done.6
  25.0 0.0 collective-permute-done.7
  25.0 0.1 maximum_maximum_fusion.info_ref
  25.1 1.0 %collective-permute-done.5 = bf16[768,128]{1,0:T(8,128)(2,1)S(1)} collective-permute-done((bf16[768,128]{1,0:T(8,128)(2,1)S(1)}, bf16[768,128]{1,0:T(8,128)(2,1)S(1)}, u32[]{:S(2)}, u32[]{:S(2)}) %collective-permute-start.5) | collective-permute-done | bytes 196640 | tf_op jit(solution)/shard_map/ppermute | solution.py:650
  26.1 1.0 %pad_maximum_fusion.refs_0_ = bf16[3072,128]{1,0:T(8,128)(2,1)S(1)} fusion(bf16[768,128]{1,0:T(8,128)(2,1)S(1)} %collective-permute-done.5, bf16[768,128]{1,0:T(8,128)(2,1)S(1)} %collective-permute-done.1, bf16[768,128]{1,0:T(8,128)(2,1)S(1)} %collective-permute-done, bf16[768,128]{1,0:T(8,128)(2,1)} %get-tuple-element.38.refs_2_), kind=kLoop, calls=%fused_computation | loop fusion | flops 3145728 | bytes 1572864 | tf_op jit(solution)/shard_map/concatenate | solution.py:662
  27.1 2.8 %collective-permute-start.8 = (bf16[3072,128]{1,0:T(8,128)(2,1)S(1)}, bf16[3072,128]{1,0:T(8,128)(2,1)S(1)}, u32[]{:S(2)}, u32[]{:S(2)}) collective-permute-start(bf16[3072,128]{1,0:T(8,128)(2,1)S(1)} %pad_maximum_fusion.refs_0_), channel_id=1, source_target_pairs={{0,16},{8,120},{16,32},{24,8},{32,48},{40,24},{48,64},{56,40},{64,... | collective-permute-start | bytes 2359304 | tf_op jit(solution)/shard_map/ppermute | solution.py:647
  29.9 3.1 %collective-permute-start.11 = (bf16[1536,128]{1,0:T(8,128)(2,1)S(1)}, bf16[1536,128]{1,0:T(8,128)(2,1)S(1)}, u32[]{:S(2)}, u32[]{:S(2)}) collective-permute-start(bf16[1536,128]{1,0:T(8,128)(2,1)S(1)} %constant_dynamic-update-slice_fusion.near_ref), channel_id=1, source_target_pairs={{0,3},{1,0},{2,1},{3,2},{4,7},{5,4},{6,5},{7,6},{8,11},{9,8},{10,9... | collective-permute-start | bytes 1179656 | tf_op jit(solution)/shard_map/ppermute | solution.py:667
  33.0 0.0 collective-permute-start.12
  33.0 3.3 %shard_map.105 = (f32[32,32,128]{2,1,0:T(8,128)}, f32[16,128]{1,0:T(8,128)S(1)}, f32[16,128]{1,0:T(8,128)S(1)}, f32[16,128]{1,0:T(8,128)S(1)}) custom-call(f32[24,256]{1,0:T(8,128)S(1)} %maximum_maximum_fusion.info_ref, f32[32,32,128]{2,1,0:T(8,128)S(1)} %copy-done.1), custom_call_target="tpu_custom_call" | custom-call | tf_op jit(solution)/shard_map/pallas_call | solution.py:553
  36.4 0.1 collective-permute-start.10
  36.5 0.3 collective-permute-start.9
  36.8 3.1 %collective-permute-done.10 = f32[16,128]{1,0:T(8,128)S(1)} collective-permute-done((f32[16,128]{1,0:T(8,128)S(1)}, f32[16,128]{1,0:T(8,128)S(1)}, u32[]{:S(2)}, u32[]{:S(2)}) %collective-permute-start.10) | collective-permute-done | bytes 8224 | tf_op jit(solution)/shard_map/ppermute | solution.py:630
  39.8 0.0 collective-permute-done.9
  39.8 0.5 collective-permute-done.11.next_ref
  40.4 3.4 %collective-permute-done.12.last_ref = bf16[1536,128]{1,0:T(8,128)(2,1)S(1)} collective-permute-done((bf16[1536,128]{1,0:T(8,128)(2,1)S(1)}, bf16[1536,128]{1,0:T(8,128)(2,1)S(1)}, u32[]{:S(2)}, u32[]{:S(2)}) %collective-permute-start.12) | collective-permute-done | bytes 393248 | tf_op jit(solution)/shard_map/ppermute | solution.py:668
  43.8 0.0 collective-permute-done.8.refs_1_
  43.8 0.0 collective-permute-start.13
  43.8 1.8 %collective-permute-start.16 = (bf16[1536,128]{1,0:T(8,128)(2,1)S(1)}, bf16[1536,128]{1,0:T(8,128)(2,1)S(1)}, u32[]{:S(2)}, u32[]{:S(2)}) collective-permute-start(bf16[1536,128]{1,0:T(8,128)(2,1)S(1)} %broadcast_select_fusion), channel_id=1, source_target_pairs={{0,1},{1,2},{2,3},{3,0},{4,5},{5,6},{6,7},{7,4},{8,11},{9,8},{10,9... | collective-permute-start | bytes 1179656 | tf_op jit(solution)/shard_map/ppermute | solution.py:675
  45.6 2.5 %collective-permute-start.14 = (f32[16,128]{1,0:T(8,128)S(1)}, f32[16,128]{1,0:T(8,128)S(1)}, u32[]{:S(2)}, u32[]{:S(2)}) collective-permute-start(f32[16,128]{1,0:T(8,128)S(1)} %add_add_fusion), channel_id=1, source_target_pairs={{0,4},{1,5},{2,6},{3,7},{4,0},{5,1},{6,2},{7,3},{8,12},{9,13},{10,... | collective-permute-start | bytes 24584 | tf_op jit(solution)/shard_map/ppermute | solution.py:676
  48.2 1.5 %collective-permute-done.14 = f32[16,128]{1,0:T(8,128)S(1)} collective-permute-done((f32[16,128]{1,0:T(8,128)S(1)}, f32[16,128]{1,0:T(8,128)S(1)}, u32[]{:S(2)}, u32[]{:S(2)}) %collective-permute-start.14) | collective-permute-done | bytes 8224 | tf_op jit(solution)/shard_map/ppermute | solution.py:676
  49.7 0.0 collective-permute-start.15
  49.7 0.0 collective-permute-start.19
  49.7 2.6 %shard_map.106.refs_0_ = bf16[2048,1024]{1,0:T(8,128)(2,1)S(1)} custom-call(s32[32,64]{1,0:T(8,128)S(1)} %get-tuple-element.54.table_ref, bf16[3072,128]{1,0:T(8,128)(2,1)S(1)} %pad_maximum_fusion.refs_0_, bf16[3072,128]{1,0:T(8,128)(2,1)S(1)} %collective-permute-done.8.refs_1_), custom_call_target="tpu_custom_call" | custom-call | tf_op jit(solution)/shard_map/pallas_call | solution.py:307
  52.3 0.1 collective-permute-done.15
  52.5 0.0 collective-permute-done.16.far_ref
  52.5 2.5 %collective-permute-done.13.refs_1_ = bf16[3072,128]{1,0:T(8,128)(2,1)S(1)} collective-permute-done((bf16[3072,128]{1,0:T(8,128)(2,1)S(1)}, bf16[3072,128]{1,0:T(8,128)(2,1)S(1)}, u32[]{:S(2)}, u32[]{:S(2)}) %collective-permute-start.13) | collective-permute-done | bytes 786464 | tf_op jit(solution)/shard_map/ppermute | solution.py:647
  54.9 0.9 %collective-permute-start.17 = (bf16[3072,128]{1,0:T(8,128)(2,1)S(1)}, bf16[3072,128]{1,0:T(8,128)(2,1)S(1)}, u32[]{:S(2)}, u32[]{:S(2)}) collective-permute-start(bf16[3072,128]{1,0:T(8,128)(2,1)S(1)} %collective-permute-done.13.refs_1_), channel_id=1, source_target_pairs={{0,16},{8,120},{16,32},{24,8},{32,48},{40,24},{48,64},{56,40},{64,... | collective-permute-start | bytes 2359304 | tf_op jit(solution)/shard_map/ppermute | solution.py:647
  55.8 2.9 %collective-permute-start.18 = (f32[16,128]{1,0:T(8,128)S(1)}, f32[16,128]{1,0:T(8,128)S(1)}, u32[]{:S(2)}, u32[]{:S(2)}) collective-permute-start(f32[16,128]{1,0:T(8,128)S(1)} %add.22), channel_id=1, source_target_pairs={{0,2},{1,3},{2,0},{3,1},{4,6},{5,7},{6,4},{7,5},{8,10},{9,11},{10,... | collective-permute-start | bytes 24584 | tf_op jit(solution)/shard_map/ppermute | solution.py:684
  58.7 0.0 collective-permute-start.21
  58.7 2.5 %shard_map.107.h_ref = bf16[32,256,256]{2,1,0:T(8,128)(2,1)S(1)} custom-call(s32[8,128]{1,0:T(8,128)S(1)} %get-tuple-element.60.table_ref, bf16[1536,128]{1,0:T(8,128)(2,1)S(1)} %constant_dynamic-update-slice_fusion.near_ref, bf16[1536,128]{1,0:T(8,128)(2,1)S(1)} %collective-permute-done.11.next_ref, bf16[1536,128]{1,0:T(8,128)(2,1)S(1)} %collective-permute-done.12.last_ref, ...), custom_call_target="tpu_custom_call" | custom-call | tf_op jit(solution)/shard_map/pallas_call | solution.py:231
  61.3 0.0 collective-permute-done.19.refs_1_
  61.3 3.6 %shard_map.108 = (f32[256,1024]{1,0:T(8,128)S(1)}, f32[8,128]{1,0:T(8,128)S(1)}) custom-call(s32[32,64]{1,0:T(8,128)S(1)} %get-tuple-element.54.table_ref, bf16[32,256,256]{2,1,0:T(8,128)(2,1)S(1)} %shard_map.107.h_ref, bf16[2048,1024]{1,0:T(8,128)(2,1)S(1)} %shard_map.106.refs_0_, bf16[3072,128]{1,0:T(8,128)(2,1)S(1)} %collective-permute-done.19.refs_1_), custom_call_target="tpu_custom_call" | custom-call | tf_op jit(solution)/shard_map/pallas_call | solution.py:414
  64.9 0.0 collective-permute-done.18
  64.9 1.1 %collective-permute-done.17.buffer_ref.refs_3_ = bf16[3072,128]{1,0:T(8,128)(2,1)S(1)} collective-permute-done((bf16[3072,128]{1,0:T(8,128)(2,1)S(1)}, bf16[3072,128]{1,0:T(8,128)(2,1)S(1)}, u32[]{:S(2)}, u32[]{:S(2)}) %collective-permute-start.17) | collective-permute-done | bytes 786464 | tf_op jit(solution)/shard_map/ppermute | solution.py:647
  66.1 3.5 %collective-permute-start.22 = (bf16[3072,128]{1,0:T(8,128)(2,1)S(1)}, bf16[3072,128]{1,0:T(8,128)(2,1)S(1)}, u32[]{:S(2)}, u32[]{:S(2)}) collective-permute-start(bf16[3072,128]{1,0:T(8,128)(2,1)S(1)} %collective-permute-done.17.buffer_ref.refs_3_), channel_id=1, source_target_pairs={{0,8},{8,0},{16,24},{24,16},{32,40},{40,32},{48,56},{56,48},{64,72... | collective-permute-start | bytes 2359304 | tf_op jit(solution)/shard_map/ppermute | solution.py:650
  69.5 0.2 shard_map.110
  69.7 0.6 collective-permute-start.20
  70.3 0.0 collective-permute-done.21.refs_2_
  70.3 4.2 %shard_map.111 = (f32[256,1024]{1,0:T(8,128)S(1)}, f32[8,128]{1,0:T(8,128)}) custom-call(s32[32,64]{1,0:T(8,128)S(1)} %get-tuple-element.54.table_ref, bf16[32,256,256]{2,1,0:T(8,128)(2,1)S(1)} %shard_map.107.h_ref, f32[256,1024]{1,0:T(8,128)S(1)} %get-tuple-element.67.refs_0_, bf16[3072,128]{1,0:T(8,128)(2,1)S(1)} %collective-permute-done.13.refs_1_, ...), custom_call_target="tpu_custom_call" | custom-call | tf_op jit(solution)/shard_map/pallas_call | solution.py:414
  74.5 0.0 collective-permute-done.22.refs_4_
  74.5 4.9 %shard_map.112 = (f32[256,1024]{1,0:T(8,128)S(1)}, f32[8,128]{1,0:T(8,128)}) custom-call(s32[32,64]{1,0:T(8,128)S(1)} %get-tuple-element.54.table_ref, bf16[32,256,256]{2,1,0:T(8,128)(2,1)S(1)} %shard_map.107.h_ref, f32[256,1024]{1,0:T(8,128)S(1)} %get-tuple-element.68.refs_0_, f32[16,128]{1,0:T(8,128)S(1)} %add.24.atoms_ref.refs_1_, ...), custom_call_target="tpu_custom_call" | custom-call | tf_op jit(solution)/shard_map/pallas_call | solution.py:414
  79.5 0.0 collective-permute-done.20.refs_1_
  79.5 0.1 collective-permute-start.23
  79.6 0.8 shard_map.109
  80.4 0.9 %collective-permute-done.23.refs_2_ = bf16[1536,128]{1,0:T(8,128)(2,1)S(1)} collective-permute-done((bf16[1536,128]{1,0:T(8,128)(2,1)S(1)}, bf16[1536,128]{1,0:T(8,128)(2,1)S(1)}, u32[]{:S(2)}, u32[]{:S(2)}) %collective-permute-start.23) | collective-permute-done | bytes 393248 | tf_op jit(solution)/shard_map/ppermute | solution.py:650
  81.3 3.5 %shard_map.113 = (f32[256,1024]{1,0:T(8,128)}, f32[8,128]{1,0:T(8,128)}) custom-call(s32[32,64]{1,0:T(8,128)S(1)} %get-tuple-element.54.table_ref, bf16[32,256,256]{2,1,0:T(8,128)(2,1)S(1)} %shard_map.107.h_ref, f32[256,1024]{1,0:T(8,128)S(1)} %get-tuple-element.70.refs_0_, bf16[1536,128]{1,0:T(8,128)(2,1)S(1)} %collective-permute-done.20.refs_1_, ...), custom_call_target="tpu_custom_call" | custom-call | tf_op jit(solution)/shard_map/pallas_call | solution.py:414
  (15 shorter events, 0.1 us)
Async XLA Ops:
  0.6 32.4 %copy-start.1 = (f32[32,32,128]{2,1,0:T(8,128)S(1)}, f32[32,32,128]{2,1,0:T(8,128)}, u32[]{:S(2)}) copy-start(f32[32,32,128]{2,1,0:T(8,128)} %external_hbm.1) | copy-start | bytes 1572868
  3.4 17.6 %collective-permute-start = (bf16[768,128]{1,0:T(8,128)(2,1)}, bf16[768,128]{1,0:T(8,128)(2,1)S(1)}, u32[]{:S(2)}, u32[]{:S(2)}) collective-permute-start(bf16[768,128]{1,0:T(8,128)(2,1)} %get-tuple-element.38.refs_2_), channel_id=1, source_target_pairs={{0,128},{8,136},{16,144},{24,152},{32,160},{40,168},{48,176},{56,1... | collective-permute-start | bytes 589832 | tf_op jit(solution)/shard_map/ppermute | solution.py:654
  5.6 15.3 %collective-permute-start.1 = (bf16[768,128]{1,0:T(8,128)(2,1)}, bf16[768,128]{1,0:T(8,128)(2,1)S(1)}, u32[]{:S(2)}, u32[]{:S(2)}) collective-permute-start(bf16[768,128]{1,0:T(8,128)(2,1)} %get-tuple-element.38.refs_2_), channel_id=1, source_target_pairs={{0,8},{8,0},{16,24},{24,16},{32,40},{40,32},{48,56},{56,48},{64,72... | collective-permute-start | bytes 589832 | tf_op jit(solution)/shard_map/ppermute | solution.py:650
  6.9 14.1 %collective-permute-start.4 = (bf16[768,128]{1,0:T(8,128)(2,1)}, bf16[768,128]{1,0:T(8,128)(2,1)S(1)}, u32[]{:S(2)}, u32[]{:S(2)}) collective-permute-start(bf16[768,128]{1,0:T(8,128)(2,1)} %get-tuple-element.40), channel_id=1, source_target_pairs={{0,4},{1,5},{2,6},{3,7},{4,0},{5,1},{6,2},{7,3},{8,12},{9,13},{10,... | collective-permute-start | bytes 589832 | tf_op jit(solution)/shard_map/ppermute | solution.py:655
  9.2 6.5 %collective-permute-start.2 = (f32[24,16]{1,0:T(8,128)}, f32[24,16]{1,0:T(8,128)S(1)}, u32[]{:S(2)}, u32[]{:S(2)}) collective-permute-start(f32[24,16]{1,0:T(8,128)} %get-tuple-element.39), channel_id=1, source_target_pairs={{0,1},{1,2},{2,3},{3,4},{4,5},{5,6},{6,7},{7,0},{8,9},{9,10},{10,1... | collective-permute-start | bytes 4616 | tf_op jit(solution)/shard_map/ppermute | solution.py:634
  10.4 5.3 %collective-permute-start.3 = (f32[24,16]{1,0:T(8,128)}, f32[24,16]{1,0:T(8,128)S(1)}, u32[]{:S(2)}, u32[]{:S(2)}) collective-permute-start(f32[24,16]{1,0:T(8,128)} %get-tuple-element.39), channel_id=1, source_target_pairs={{0,7},{1,0},{2,1},{3,2},{4,3},{5,4},{6,5},{7,6},{8,15},{9,8},{10,9... | collective-permute-start | bytes 4616 | tf_op jit(solution)/shard_map/ppermute | solution.py:635
  16.5 8.5 %collective-permute-start.6 = (f32[24,48]{1,0:T(8,128)S(1)}, f32[24,48]{1,0:T(8,128)S(1)}, u32[]{:S(2)}, u32[]{:S(2)}) collective-permute-start(f32[24,48]{1,0:T(8,128)S(1)} %pad_maximum_fusion.1), channel_id=1, source_target_pairs={{0,8},{8,0},{16,24},{24,16},{32,40},{40,32},{48,56},{56,48},{64,72... | collective-permute-start | bytes 13832 | tf_op jit(solution)/shard_map/ppermute | solution.py:629
  17.9 7.1 %collective-permute-start.7 = (f32[24,48]{1,0:T(8,128)S(1)}, f32[24,48]{1,0:T(8,128)S(1)}, u32[]{:S(2)}, u32[]{:S(2)}) collective-permute-start(f32[24,48]{1,0:T(8,128)S(1)} %pad_maximum_fusion.1), channel_id=1, source_target_pairs={{0,248},{8,16},{16,8},{24,32},{32,24},{40,48},{48,40},{56,64},{64,... | collective-permute-start | bytes 13832 | tf_op jit(solution)/shard_map/ppermute | solution.py:630
  19.6 0.8 copy-start.2
  20.4 9.5 %copy-start.3 = (bf16[768,128]{1,0:T(8,128)(2,1)S(1)}, bf16[768,128]{1,0:T(8,128)(2,1)}, u32[]{:S(2)}) copy-start(bf16[768,128]{1,0:T(8,128)(2,1)} %get-tuple-element.40) | copy-start | bytes 589828
  21.0 5.1 %collective-permute-start.5 = (bf16[768,128]{1,0:T(8,128)(2,1)S(1)}, bf16[768,128]{1,0:T(8,128)(2,1)S(1)}, u32[]{:S(2)}, u32[]{:S(2)}) collective-permute-start(bf16[768,128]{1,0:T(8,128)(2,1)S(1)} %collective-permute-done), channel_id=1, source_target_pairs={{0,8},{8,0},{16,24},{24,16},{32,40},{40,32},{48,56},{56,48},{64,72... | collective-permute-start | bytes 589832 | tf_op jit(solution)/shard_map/ppermute | solution.py:650
  27.1 16.7 %collective-permute-start.8 = (bf16[3072,128]{1,0:T(8,128)(2,1)S(1)}, bf16[3072,128]{1,0:T(8,128)(2,1)S(1)}, u32[]{:S(2)}, u32[]{:S(2)}) collective-permute-start(bf16[3072,128]{1,0:T(8,128)(2,1)S(1)} %pad_maximum_fusion.refs_0_), channel_id=1, source_target_pairs={{0,16},{8,120},{16,32},{24,8},{32,48},{40,24},{48,64},{56,40},{64,... | collective-permute-start | bytes 2359304 | tf_op jit(solution)/shard_map/ppermute | solution.py:647
  29.9 10.4 %collective-permute-start.11 = (bf16[1536,128]{1,0:T(8,128)(2,1)S(1)}, bf16[1536,128]{1,0:T(8,128)(2,1)S(1)}, u32[]{:S(2)}, u32[]{:S(2)}) collective-permute-start(bf16[1536,128]{1,0:T(8,128)(2,1)S(1)} %constant_dynamic-update-slice_fusion.near_ref), channel_id=1, source_target_pairs={{0,3},{1,0},{2,1},{3,2},{4,7},{5,4},{6,5},{7,6},{8,11},{9,8},{10,9... | collective-permute-start | bytes 1179656 | tf_op jit(solution)/shard_map/ppermute | solution.py:667
  33.0 10.7 %collective-permute-start.12 = (bf16[1536,128]{1,0:T(8,128)(2,1)S(1)}, bf16[1536,128]{1,0:T(8,128)(2,1)S(1)}, u32[]{:S(2)}, u32[]{:S(2)}) collective-permute-start(bf16[1536,128]{1,0:T(8,128)(2,1)S(1)} %constant_dynamic-update-slice_fusion.near_ref), channel_id=1, source_target_pairs={{0,1},{1,2},{2,3},{3,0},{4,5},{5,6},{6,7},{7,4},{8,9},{9,10},{10,1... | collective-permute-start | bytes 1179656 | tf_op jit(solution)/shard_map/ppermute | solution.py:668
  36.4 3.5 %collective-permute-start.10 = (f32[16,128]{1,0:T(8,128)S(1)}, f32[16,128]{1,0:T(8,128)S(1)}, u32[]{:S(2)}, u32[]{:S(2)}) collective-permute-start(f32[16,128]{1,0:T(8,128)S(1)} %get-tuple-element.51), channel_id=1, source_target_pairs={{0,248},{8,16},{16,8},{24,32},{32,24},{40,48},{48,40},{56,64},{64,... | collective-permute-start | bytes 24584 | tf_op jit(solution)/shard_map/ppermute | solution.py:630
  36.5 3.4 %collective-permute-start.9 = (f32[16,128]{1,0:T(8,128)S(1)}, f32[16,128]{1,0:T(8,128)S(1)}, u32[]{:S(2)}, u32[]{:S(2)}) collective-permute-start(f32[16,128]{1,0:T(8,128)S(1)} %get-tuple-element.50), channel_id=1, source_target_pairs={{0,8},{8,0},{16,24},{24,16},{32,40},{40,32},{48,56},{56,48},{64,72... | collective-permute-start | bytes 24584 | tf_op jit(solution)/shard_map/ppermute | solution.py:629
  43.8 11.1 %collective-permute-start.13 = (bf16[3072,128]{1,0:T(8,128)(2,1)S(1)}, bf16[3072,128]{1,0:T(8,128)(2,1)S(1)}, u32[]{:S(2)}, u32[]{:S(2)}) collective-permute-start(bf16[3072,128]{1,0:T(8,128)(2,1)S(1)} %collective-permute-done.8.refs_1_), channel_id=1, source_target_pairs={{0,16},{8,120},{16,32},{24,8},{32,48},{40,24},{48,64},{56,40},{64,... | collective-permute-start | bytes 2359304 | tf_op jit(solution)/shard_map/ppermute | solution.py:647
  43.8 8.6 %collective-permute-start.16 = (bf16[1536,128]{1,0:T(8,128)(2,1)S(1)}, bf16[1536,128]{1,0:T(8,128)(2,1)S(1)}, u32[]{:S(2)}, u32[]{:S(2)}) collective-permute-start(bf16[1536,128]{1,0:T(8,128)(2,1)S(1)} %broadcast_select_fusion), channel_id=1, source_target_pairs={{0,1},{1,2},{2,3},{3,0},{4,5},{5,6},{6,7},{7,4},{8,11},{9,8},{10,9... | collective-permute-start | bytes 1179656 | tf_op jit(solution)/shard_map/ppermute | solution.py:675
  45.6 4.0 %collective-permute-start.14 = (f32[16,128]{1,0:T(8,128)S(1)}, f32[16,128]{1,0:T(8,128)S(1)}, u32[]{:S(2)}, u32[]{:S(2)}) collective-permute-start(f32[16,128]{1,0:T(8,128)S(1)} %add_add_fusion), channel_id=1, source_target_pairs={{0,4},{1,5},{2,6},{3,7},{4,0},{5,1},{6,2},{7,3},{8,12},{9,13},{10,... | collective-permute-start | bytes 24584 | tf_op jit(solution)/shard_map/ppermute | solution.py:676
  49.7 2.8 %collective-permute-start.15 = (f32[16,128]{1,0:T(8,128)S(1)}, f32[16,128]{1,0:T(8,128)S(1)}, u32[]{:S(2)}, u32[]{:S(2)}) collective-permute-start(f32[16,128]{1,0:T(8,128)S(1)} %add.21), channel_id=1, source_target_pairs={{0,1},{1,0},{2,3},{3,2},{4,5},{5,4},{6,7},{7,6},{8,9},{9,8},{10,11... | collective-permute-start | bytes 24584 | tf_op jit(solution)/shard_map/ppermute | solution.py:677
  49.7 11.6 %collective-permute-start.19 = (bf16[3072,128]{1,0:T(8,128)(2,1)S(1)}, bf16[3072,128]{1,0:T(8,128)(2,1)S(1)}, u32[]{:S(2)}, u32[]{:S(2)}) collective-permute-start(bf16[3072,128]{1,0:T(8,128)(2,1)S(1)} %collective-permute-done.8.refs_1_), channel_id=1, source_target_pairs={{0,8},{8,0},{16,24},{24,16},{32,40},{40,32},{48,56},{56,48},{64,72... | collective-permute-start | bytes 2359304 | tf_op jit(solution)/shard_map/ppermute | solution.py:650
  54.9 11.1 %collective-permute-start.17 = (bf16[3072,128]{1,0:T(8,128)(2,1)S(1)}, bf16[3072,128]{1,0:T(8,128)(2,1)S(1)}, u32[]{:S(2)}, u32[]{:S(2)}) collective-permute-start(bf16[3072,128]{1,0:T(8,128)(2,1)S(1)} %collective-permute-done.13.refs_1_), channel_id=1, source_target_pairs={{0,16},{8,120},{16,32},{24,8},{32,48},{40,24},{48,64},{56,40},{64,... | collective-permute-start | bytes 2359304 | tf_op jit(solution)/shard_map/ppermute | solution.py:647
  55.8 9.1 %collective-permute-start.18 = (f32[16,128]{1,0:T(8,128)S(1)}, f32[16,128]{1,0:T(8,128)S(1)}, u32[]{:S(2)}, u32[]{:S(2)}) collective-permute-start(f32[16,128]{1,0:T(8,128)S(1)} %add.22), channel_id=1, source_target_pairs={{0,2},{1,3},{2,0},{3,1},{4,6},{5,7},{6,4},{7,5},{8,10},{9,11},{10,... | collective-permute-start | bytes 24584 | tf_op jit(solution)/shard_map/ppermute | solution.py:684
  58.7 11.6 %collective-permute-start.21 = (bf16[3072,128]{1,0:T(8,128)(2,1)S(1)}, bf16[3072,128]{1,0:T(8,128)(2,1)S(1)}, u32[]{:S(2)}, u32[]{:S(2)}) collective-permute-start(bf16[3072,128]{1,0:T(8,128)(2,1)S(1)} %collective-permute-done.13.refs_1_), channel_id=1, source_target_pairs={{0,8},{8,0},{16,24},{24,16},{32,40},{40,32},{48,56},{56,48},{64,72... | collective-permute-start | bytes 2359304 | tf_op jit(solution)/shard_map/ppermute | solution.py:650
  66.1 8.5 %collective-permute-start.22 = (bf16[3072,128]{1,0:T(8,128)(2,1)S(1)}, bf16[3072,128]{1,0:T(8,128)(2,1)S(1)}, u32[]{:S(2)}, u32[]{:S(2)}) collective-permute-start(bf16[3072,128]{1,0:T(8,128)(2,1)S(1)} %collective-permute-done.17.buffer_ref.refs_3_), channel_id=1, source_target_pairs={{0,8},{8,0},{16,24},{24,16},{32,40},{40,32},{48,56},{56,48},{64,72... | collective-permute-start | bytes 2359304 | tf_op jit(solution)/shard_map/ppermute | solution.py:650
  69.7 9.7 %collective-permute-start.20 = (bf16[1536,128]{1,0:T(8,128)(2,1)S(1)}, bf16[1536,128]{1,0:T(8,128)(2,1)S(1)}, u32[]{:S(2)}, u32[]{:S(2)}) collective-permute-start(bf16[1536,128]{1,0:T(8,128)(2,1)S(1)} %shard_map.110), channel_id=1, source_target_pairs={{0,16},{8,120},{16,32},{24,8},{32,48},{40,24},{48,64},{56,40},{64,... | collective-permute-start | bytes 1179656 | tf_op jit(solution)/shard_map/ppermute | solution.py:647
  70.3 4.2 %copy-start = (bf16[768,128]{1,0:T(8,128)(2,1)S(1)}, bf16[768,128]{1,0:T(8,128)(2,1)}, u32[]{:S(2)}) copy-start(bf16[768,128]{1,0:T(8,128)(2,1)} %get-tuple-element.38.refs_2_) | copy-start | bytes 589828
  79.5 1.8 %collective-permute-start.23 = (bf16[1536,128]{1,0:T(8,128)(2,1)S(1)}, bf16[1536,128]{1,0:T(8,128)(2,1)S(1)}, u32[]{:S(2)}, u32[]{:S(2)}) collective-permute-start(bf16[1536,128]{1,0:T(8,128)(2,1)S(1)} %collective-permute-done.20.refs_1_), channel_id=1, source_target_pairs={{0,8},{8,0},{16,24},{24,16},{32,40},{40,32},{48,56},{56,48},{64,72... | collective-permute-start | bytes 1179656 | tf_op jit(solution)/shard_map/ppermute | solution.py:650

commit v5 on v4

--- a/solution.py
+++ b/solution.py
@@ -319,10 +319,10 @@
     )(table, *parts)
 
 
-def accumulate_kernel(ready, groups, start, local, last, table_ref, h_ref, *refs):
+def accumulate_kernel(ready, groups, start, local, table_ref, h_ref, *refs):
     refs = list(refs)
     before = None if start else refs.pop(0)
-    atoms, mine = (refs.pop(0), refs.pop(0)) if local else (None, None)
+    held, own = (refs.pop(0), refs.pop(0)) if local else (None, None)
     early = refs.pop(0) if ready else None
     parts = [refs.pop(0) for _ in groups]
     out_ref, token_ref, both, dense, wide, table, sem = refs[:7]
@@ -331,38 +331,10 @@
     token_ref[...] = jnp.zeros_like(token_ref)
     done, tiles = tiles_of(ready), tiles_of(groups)
     prepare_all(parts, groups, both)
-    if local:
-        prepare(mine[0:PACK, :], both, len(tiles) * SPAN)
     for at, tile in enumerate(done + tiles):
         wide[:, at * 256 : at * 256 + 256] = h_ref[tile]
     copy.wait()
     spread_all(groups, tiles, table, both, dense)
-    if local:
-        own, held = refs[7], refs[8]
-        row = lax.axis_index("row")
-
-        def store(r, c, block):
-            own[r * BS : r * BS + BS, c * 128 : c * 128 + 128] = block
-
-        spread_tile(lambda r, c: table[row, r * 16 + c], both, len(tiles) * SPAN, store)
-        values = atoms[...]
-        lane_atom = lax.broadcasted_iota(jnp.int32, (256, 128), 1) // 4
-        row_atom = lax.broadcasted_iota(jnp.int32, (256, 128), 0) // 8
-        tall = [
-            jnp.where(
-                lane_atom == row_atom,
-                jnp.concatenate([values[8 * b : 8 * b + 8, :]] * 32, axis=0),
-                0.0,
-            )
-            for b in range(2)
-        ]
-        q = lax.broadcasted_iota(jnp.int32, (256, 256), 0)
-        m = lax.broadcasted_iota(jnp.int32, (256, 256), 1)
-        place = q % 128 // 4 * 8 + q // 128 * 4 + q % 4
-        chosen = jnp.where(place == m, 1.0, 0.0).astype(BF16)
-        for k, t in enumerate(split3(jnp.concatenate(tall, axis=1))):
-            held[k] = jnp.dot(t, chosen, preferred_element_type=F32).astype(BF16)
-    copies = []
     for n in range(4):
         lanes = slice(n * 256, n * 256 + 256)
         total = jnp.dot(
@@ -374,23 +346,13 @@
             )
         if local:
             for k in range(3):
-                total += jnp.dot(held[k], own[:, lanes], preferred_element_type=F32)
+                total += jnp.dot(held[k], own[0:256, lanes], preferred_element_type=F32)
         if before is not None:
             total += before[:, lanes]
-        if last:
-            result, sems = refs[7], refs[8]
-            result[:, lanes] = total
-            copies.append(
-                pltpu.make_async_copy(result.at[:, lanes], out_ref.at[:, lanes], sems.at[n])
-            )
-            copies[-1].start()
-        else:
-            out_ref[:, lanes] = total
-    for copy in copies:
-        copy.wait()
-
-
-def accumulate(table, h_dense, before, parts, groups, local=(), ready=(), early=None, last=False):
+        out_ref[:, lanes] = total
+
+
+def accumulate(table, h_dense, before, parts, groups, local=(), ready=(), early=None):
     vmem = pl.BlockSpec(memory_space=pltpu.VMEM)
     operands = [h_dense]
     if before is not None:
@@ -401,23 +363,17 @@
     operands += parts
     count = sum(g[0] for g in groups)
     scratch = [
-        pltpu.VMEM(((count + bool(local)) * SPAN, 128), BF16),
+        pltpu.VMEM((count * SPAN, 128), BF16),
         pltpu.VMEM((256 * count, 1024), BF16),
         pltpu.VMEM((256, 256 * (count + sum(g[0] for g in ready))), BF16),
         pltpu.SMEM((32, 64), jnp.int32),
         pltpu.SemaphoreType.DMA,
     ]
-    if local:
-        scratch += [pltpu.VMEM((256, 1024), BF16), pltpu.VMEM((3, 256, 256), BF16)]
-    if last:
-        scratch += [pltpu.VMEM((256, 1024), F32), pltpu.SemaphoreType.DMA((4,))]
     return pl.pallas_call(
-        functools.partial(
-            accumulate_kernel, ready, groups, before is None, bool(local), last
-        ),
+        functools.partial(accumulate_kernel, ready, groups, before is None, bool(local)),
         out_shape=(jax.ShapeDtypeStruct((256, 1024), F32), jax.ShapeDtypeStruct((8, 128), F32)),
         in_specs=[pl.BlockSpec(memory_space=pl.ANY)] + [vmem] * len(operands),
-        out_specs=(pl.BlockSpec(memory_space=pltpu.HBM) if last else vmem, vmem),
+        out_specs=(vmem, vmem),
         scratch_shapes=scratch,
         compiler_params=pltpu.CompilerParams(vmem_limit_bytes=14 * 2**20),
         cost_estimate=FREE,
@@ -573,7 +529,24 @@
     )(info, external)
 
 
-def finish_kernel(atoms_ref, mine_ref):
+def finish_kernel(atoms_ref, mine_ref, terms_ref):
+    values = atoms_ref[...]
+    lane_atom = lax.broadcasted_iota(jnp.int32, (256, 128), 1) // 4
+    row_atom = lax.broadcasted_iota(jnp.int32, (256, 128), 0) // 8
+    tall = [
+        jnp.where(
+            lane_atom == row_atom,
+            jnp.concatenate([values[8 * b : 8 * b + 8, :]] * 32, axis=0),
+            0.0,
+        )
+        for b in range(2)
+    ]
+    q = lax.broadcasted_iota(jnp.int32, (256, 256), 0)
+    m = lax.broadcasted_iota(jnp.int32, (256, 256), 1)
+    place = q % 128 // 4 * 8 + q // 128 * 4 + q % 4
+    chosen = jnp.where(place == m, 1.0, 0.0).astype(BF16)
+    for k, t in enumerate(split3(jnp.concatenate(tall, axis=1))):
+        terms_ref[k] = jnp.dot(t, chosen, preferred_element_type=F32).astype(BF16)
     col = lax.axis_index("col")
     mine = pltpu.roll(atoms_ref[...], (8 - col) % 8 * 16, 1)
     lane = lax.broadcasted_iota(jnp.int32, (16, 128), 1)
@@ -593,9 +566,12 @@
     vmem = pl.BlockSpec(memory_space=pltpu.VMEM)
     return pl.pallas_call(
         finish_kernel,
-        out_shape=jax.ShapeDtypeStruct((4, 64), F32),
+        out_shape=(
+            jax.ShapeDtypeStruct((4, 64), F32),
+            jax.ShapeDtypeStruct((3, 256, 256), BF16),
+        ),
         in_specs=[vmem],
-        out_specs=vmem,
+        out_specs=(vmem, vmem),
         compiler_params=pltpu.CompilerParams(vmem_limit_bytes=2 * 2**20),
         cost_estimate=FREE,
     )(atoms)
@@ -669,14 +645,16 @@
     density, share, near, far = grid_part(info, external)
     near, far = to_rows(near, far)
     share = share + near + far
-    q1, share, h_next, h_last = together((q1, share, h_next, h_last))
+    q1, share = together((q1, share))
 
     q2, x1 = step(q1), swap(q1)
     h_far = lax.ppermute(jnp.where(core == 0, h_last, h_next), ("row", "col"), ALONG_X)
+    share, h_next, h_last = together((share, h_next, h_last))
     share = share + lax.ppermute(share, "col", col_pairs(1, 0))
-    share = share + lax.ppermute(share, "col", [(i, i ^ 1) for i in range(8)])
     early_groups = ((4, 0, 0), (4, -1, 0))
     dense = unpack(table_p, [q, q1], early_groups)
+    share, dense = together((share, dense))
+    share = share + lax.ppermute(share, "col", [(i, i ^ 1) for i in range(8)])
     q2, dense, share, h_far = together((q2, dense, share, h_far))
     h_dense = spread_hamiltonian(table_h, [h0, h_next, h_last, h_far])
 
@@ -685,17 +663,24 @@
     product, done = accumulate(
         table_p, h_dense, None, [x1], ((4, 1, 1),), ready=early_groups, early=dense
     )
-    q3, atoms, done = together((q3, atoms, done))
+    integrals, terms = finish(atoms)
+    dense2 = unpack(table_p, [q2], ((4, -2, 0),))
+    q3, integrals, terms, dense2, done = together((q3, integrals, terms, dense2, done))
 
     q4 = step(front(q3, done))
     x3 = swap(q3)
-    integrals = finish(atoms)
-    product, _ = accumulate(table_p, h_dense, product, [q2, x2], ((4, -2, 0), (4, 2, 1)))
     product, _ = accumulate(
-        table_p, h_dense, product, [q3, x3], ((4, -3, 0), (4, 3, 1)), local=(atoms, pp)
+        table_p, h_dense, product, [x2], ((4, 2, 1),), ready=((4, -2, 0),), early=dense2
+    )
+    product, _ = accumulate(
+        table_p, h_dense, product, [q3, x3], ((4, -3, 0), (4, 3, 1)), local=(terms, dense)
     )
     q4, product = together((q4, product))
-    product, _ = accumulate(table_p, h_dense, product, [q4, swap(q4)], ((2, 4, 0), (2, 4, 1)))
+    x4 = swap(q4)
+    dense4 = unpack(table_p, [q4], ((2, 4, 0),))
+    product, _ = accumulate(
+        table_p, h_dense, product, [x4], ((2, 4, 1),), ready=((2, 4, 0),), early=dense4
+    )
     return (density, integrals, product)
 
 

time: 85.3 us -> 81.7 us (0.958)
  waiting for transfers between devices: 15.5 us -> 9.58 us
  Pallas kernels: 29.1 us -> 30.5 us
  starting transfers between devices: 36.5 us -> 37.4 us
    ppermute x4, waiting for transfers between devices: 3.59 us -> 0.01 us  [step(): return lax.ppermute(chain, 'row', ALONG_Z)]
    ppermute x4, starting transfers between devices: 4.34 us -> 7.53 us  [step(): return lax.ppermute(chain, 'row', ALONG_Z)]
    pallas_call x1 -> x3, Pallas kernels: 2.64 us -> 5.75 us  [unpack(): pl.pallas_call(functools.partial(unpack_kernel, groups), out_shape=jax.Sh...]
    ppermute x1, waiting for transfers between devices: 0.14 us -> 2.47 us  [on_device(): share = share + lax.ppermute(share, 'col', [(i, i ^ 1) for i in range(8)])]
    ppermute x1, waiting for transfers between devices: 3.4 us -> 1.45 us  [on_device(): h_last = lax.ppermute(h0, 'col', col_pairs(0, 1))]
    pallas_call x4, Pallas kernels: 16.3 us -> 14.5 us  [accumulate(): pl.pallas_call(functools.partial(accumulate_kernel, ready, groups, before...]
    ppermute x1, waiting for transfers between devices: 1.48 us -> 0.01 us  [on_device(): share = share + lax.ppermute(share, 'col', col_pairs(1, 0))]
    ppermute x1, starting transfers between devices: 2.88 us -> 1.51 us  [on_device(): atoms = share + lax.ppermute(share, 'col', [(i, i ^ 2) for i in range(8)])]
  transfers between devices with their start and end apart: 24 -> 24, of which waited for: 10 -> 6; matrix products, arithmetic and copies ran while one was open for 1% -> 1% of each run, Pallas kernels for 27% -> 30%
where the time goes in v5:
time: 81.7 us; the launch traced here: 81.4 us
  starting transfers between devices  37.4 us (46%)
  Pallas kernels  30.5 us (37%)
  waiting for transfers between devices  9.58 us (12%)
  other arithmetic  1.9 us (2%)
  between operations  1.03 us (1%)
  local copies, waits for them, and re-layouts  0.97 us (1%)
    pallas_call x4, Pallas kernels, accumulate(): pl.pallas_call(functools.partial(accumulate_kernel, ready, groups, before...  14.5 us
    ppermute x6, starting transfers between devices, swap(): return lax.ppermute(chain, 'row', ACROSS_CORES)  7.56 us
    ppermute x4, starting transfers between devices, step(): return lax.ppermute(chain, 'row', ALONG_Z)  7.53 us
    pallas_call x3, Pallas kernels, unpack(): pl.pallas_call(functools.partial(unpack_kernel, groups), out_shape=jax.Sh...  5.75 us
    ppermute x1, starting transfers between devices, from_neighbours(): after = lax.ppermute(first, axis, ring(axis, size, -1))  3.87 us
    pallas_call x1, Pallas kernels, grid_part(): pl.pallas_call(grid_kernel, out_shape=(jax.ShapeDtypeStruct(external.shap...  3.31 us
    ppermute x1, starting transfers between devices, on_device(): h_next = lax.ppermute(h0, 'col', col_pairs(0, 3))  3.09 us
    ppermute x2, waiting for transfers between devices, to_rows(): lax.ppermute(far, 'row', [(i, (i + 2 * (i % 2) - 1) % 32) for i in range(...  3.07 us
  transfers between devices with their start and end apart: 24, of which 6 were waited for; matrix products, arithmetic and copies ran while one was open for 1% of the time, Pallas kernels for 30%

profile of v5, /device:TPU:1, one launch (start us, length us, event | category | flops | bytes accessed | tf_op | source)
XLA Modules:
  0.0 81.4 jit_solution(341066004659453490)
XLA Ops:
  0.6 2.8 %shard_map.103 = (bf16[768,128]{1,0:T(8,128)(2,1)}, bf16[768,128]{1,0:T(8,128)(2,1)}, f32[24,16]{1,0:T(8,128)}) custom-call(s32[128,128]{1,0:T(8,128)} %pattern_ref.1, bf16[256,1024]{1,0:T(8,128)(2,1)} %h_hbm.1, bf16[256,1024]{1,0:T(8,128)(2,1)} %p_hbm.1, f32[4,64]{1,0:T(4,128)} %coef_hbm.1, s32[4]{0:T(128)} %x_hbm.1, s32[4]{0:T(128)} %y_hbm.1, s32[4]{0:T(128)} %z_hbm.1), custom_call_target="tpu_custom_call" | custom-call | tf_op jit(solution)/shard_map/pallas_call | solution.py:101
  3.4 2.2 %collective-permute-start = (bf16[768,128]{1,0:T(8,128)(2,1)}, bf16[768,128]{1,0:T(8,128)(2,1)S(1)}, u32[]{:S(2)}, u32[]{:S(2)}) collective-permute-start(bf16[768,128]{1,0:T(8,128)(2,1)} %get-tuple-element.45), channel_id=1, source_target_pairs={{0,128},{8,136},{16,144},{24,152},{32,160},{40,168},{48,176},{56,1... | collective-permute-start | bytes 589832 | tf_op jit(solution)/shard_map/ppermute | solution.py:630
  5.6 1.2 %collective-permute-start.1 = (bf16[768,128]{1,0:T(8,128)(2,1)}, bf16[768,128]{1,0:T(8,128)(2,1)S(1)}, u32[]{:S(2)}, u32[]{:S(2)}) collective-permute-start(bf16[768,128]{1,0:T(8,128)(2,1)} %get-tuple-element.45), channel_id=1, source_target_pairs={{0,8},{8,0},{16,24},{24,16},{32,40},{40,32},{48,56},{56,48},{64,72... | collective-permute-start | bytes 589832 | tf_op jit(solution)/shard_map/ppermute | solution.py:626
  6.9 2.4 %collective-permute-start.4 = (bf16[768,128]{1,0:T(8,128)(2,1)}, bf16[768,128]{1,0:T(8,128)(2,1)S(1)}, u32[]{:S(2)}, u32[]{:S(2)}) collective-permute-start(bf16[768,128]{1,0:T(8,128)(2,1)} %get-tuple-element.47), channel_id=1, source_target_pairs={{0,4},{1,5},{2,6},{3,7},{4,0},{5,1},{6,2},{7,3},{8,12},{9,13},{10,... | collective-permute-start | bytes 589832 | tf_op jit(solution)/shard_map/ppermute | solution.py:631
  9.2 1.2 %collective-permute-start.2 = (f32[24,16]{1,0:T(8,128)}, f32[24,16]{1,0:T(8,128)S(1)}, u32[]{:S(2)}, u32[]{:S(2)}) collective-permute-start(f32[24,16]{1,0:T(8,128)} %get-tuple-element.46), channel_id=1, source_target_pairs={{0,1},{1,2},{2,3},{3,4},{4,5},{5,6},{6,7},{7,0},{8,9},{9,10},{10,1... | collective-permute-start | bytes 4616 | tf_op jit(solution)/shard_map/ppermute | solution.py:610
  10.4 3.9 %collective-permute-start.3 = (f32[24,16]{1,0:T(8,128)}, f32[24,16]{1,0:T(8,128)S(1)}, u32[]{:S(2)}, u32[]{:S(2)}) collective-permute-start(f32[24,16]{1,0:T(8,128)} %get-tuple-element.46), channel_id=1, source_target_pairs={{0,7},{1,0},{2,1},{3,2},{4,3},{5,4},{6,5},{7,6},{8,15},{9,8},{10,9... | collective-permute-start | bytes 4616 | tf_op jit(solution)/shard_map/ppermute | solution.py:611
  14.3 1.4 %collective-permute-done.2 = f32[24,16]{1,0:T(8,128)S(1)} collective-permute-done((f32[24,16]{1,0:T(8,128)}, f32[24,16]{1,0:T(8,128)S(1)}, u32[]{:S(2)}, u32[]{:S(2)}) %collective-permute-start.2) | collective-permute-done | bytes 1568 | tf_op jit(solution)/shard_map/ppermute | solution.py:610
  15.7 0.0 collective-permute-done.3
  15.7 0.8 pad_maximum_fusion.1
  16.5 1.5 %collective-permute-start.6 = (f32[24,48]{1,0:T(8,128)S(1)}, f32[24,48]{1,0:T(8,128)S(1)}, u32[]{:S(2)}, u32[]{:S(2)}) collective-permute-start(f32[24,48]{1,0:T(8,128)S(1)} %pad_maximum_fusion.1), channel_id=1, source_target_pairs={{0,8},{8,0},{16,24},{24,16},{32,40},{40,32},{48,56},{56,48},{64,72... | collective-permute-start | bytes 13832 | tf_op jit(solution)/shard_map/ppermute | solution.py:605
  17.9 1.6 %collective-permute-start.7 = (f32[24,48]{1,0:T(8,128)S(1)}, f32[24,48]{1,0:T(8,128)S(1)}, u32[]{:S(2)}, u32[]{:S(2)}) collective-permute-start(f32[24,48]{1,0:T(8,128)S(1)} %pad_maximum_fusion.1), channel_id=1, source_target_pairs={{0,248},{8,16},{16,8},{24,32},{32,24},{40,48},{48,40},{56,64},{64,... | collective-permute-start | bytes 13832 | tf_op jit(solution)/shard_map/ppermute | solution.py:606
  19.6 0.8 %copy-done.1 = s32[128,128]{1,0:T(8,128)S(1)} copy-done((s32[128,128]{1,0:T(8,128)S(1)}, s32[128,128]{1,0:T(8,128)}, u32[]{:S(2)}) %copy-start.1) | copy-done | bytes 65560
  20.4 0.5 shard_map.104
  20.9 0.1 pad.3.clone
  21.0 0.0 collective-permute-done
  21.0 0.0 collective-permute-done.1
  21.0 0.0 collective-permute-done.4
  21.0 4.0 %collective-permute-start.5 = (bf16[768,128]{1,0:T(8,128)(2,1)S(1)}, bf16[768,128]{1,0:T(8,128)(2,1)S(1)}, u32[]{:S(2)}, u32[]{:S(2)}) collective-permute-start(bf16[768,128]{1,0:T(8,128)(2,1)S(1)} %collective-permute-done), channel_id=1, source_target_pairs={{0,8},{8,0},{16,24},{24,16},{32,40},{40,32},{48,56},{56,48},{64,72... | collective-permute-start | bytes 589832 | tf_op jit(solution)/shard_map/ppermute | solution.py:626
  25.0 0.0 collective-permute-done.6
  25.0 0.0 collective-permute-done.7
  25.0 0.1 maximum_maximum_fusion.info_ref
  25.1 1.0 %collective-permute-done.5 = bf16[768,128]{1,0:T(8,128)(2,1)S(1)} collective-permute-done((bf16[768,128]{1,0:T(8,128)(2,1)S(1)}, bf16[768,128]{1,0:T(8,128)(2,1)S(1)}, u32[]{:S(2)}, u32[]{:S(2)}) %collective-permute-start.5) | collective-permute-done | bytes 196640 | tf_op jit(solution)/shard_map/ppermute | solution.py:626
  26.1 1.0 %pad_maximum_fusion.refs_0_ = bf16[3072,128]{1,0:T(8,128)(2,1)S(1)} fusion(bf16[768,128]{1,0:T(8,128)(2,1)S(1)} %collective-permute-done.5, bf16[768,128]{1,0:T(8,128)(2,1)S(1)} %collective-permute-done.1, bf16[768,128]{1,0:T(8,128)(2,1)S(1)} %collective-permute-done, bf16[768,128]{1,0:T(8,128)(2,1)} %get-tuple-element.45), kind=kLoop, calls=%fused_computation | loop fusion | flops 3145728 | bytes 1572864 | tf_op jit(solution)/shard_map/concatenate | solution.py:638
  27.1 2.8 %collective-permute-start.8 = (bf16[3072,128]{1,0:T(8,128)(2,1)S(1)}, bf16[3072,128]{1,0:T(8,128)(2,1)S(1)}, u32[]{:S(2)}, u32[]{:S(2)}) collective-permute-start(bf16[3072,128]{1,0:T(8,128)(2,1)S(1)} %pad_maximum_fusion.refs_0_), channel_id=1, source_target_pairs={{0,16},{8,120},{16,32},{24,8},{32,48},{40,24},{48,64},{56,40},{64,... | collective-permute-start | bytes 2359304 | tf_op jit(solution)/shard_map/ppermute | solution.py:623
  29.9 3.1 %collective-permute-start.12 = (bf16[1536,128]{1,0:T(8,128)(2,1)S(1)}, bf16[1536,128]{1,0:T(8,128)(2,1)S(1)}, u32[]{:S(2)}, u32[]{:S(2)}) collective-permute-start(bf16[1536,128]{1,0:T(8,128)(2,1)S(1)} %constant_dynamic-update-slice_fusion.near_ref), channel_id=1, source_target_pairs={{0,3},{1,0},{2,1},{3,2},{4,7},{5,4},{6,5},{7,6},{8,11},{9,8},{10,9... | collective-permute-start | bytes 1179656 | tf_op jit(solution)/shard_map/ppermute | solution.py:643
  33.0 0.0 collective-permute-start.13
  33.0 3.3 %shard_map.105 = (f32[32,32,128]{2,1,0:T(8,128)}, f32[16,128]{1,0:T(8,128)S(1)}, f32[16,128]{1,0:T(8,128)S(1)}, f32[16,128]{1,0:T(8,128)S(1)}) custom-call(f32[24,256]{1,0:T(8,128)S(1)} %maximum_maximum_fusion.info_ref, f32[32,32,128]{2,1,0:T(8,128)S(1)} %copy-done), custom_call_target="tpu_custom_call" | custom-call | tf_op jit(solution)/shard_map/pallas_call | solution.py:509
  36.4 0.1 collective-permute-start.10
  36.5 0.3 collective-permute-start.9
  36.8 3.1 %collective-permute-done.10 = f32[16,128]{1,0:T(8,128)S(1)} collective-permute-done((f32[16,128]{1,0:T(8,128)S(1)}, f32[16,128]{1,0:T(8,128)S(1)}, u32[]{:S(2)}, u32[]{:S(2)}) %collective-permute-start.10) | collective-permute-done | bytes 8224 | tf_op jit(solution)/shard_map/ppermute | solution.py:606
  39.8 0.0 collective-permute-done.9
  39.8 0.0 collective-permute-done.8.refs_1_
  39.8 2.5 %collective-permute-start.11 = (bf16[3072,128]{1,0:T(8,128)(2,1)S(1)}, bf16[3072,128]{1,0:T(8,128)(2,1)S(1)}, u32[]{:S(2)}, u32[]{:S(2)}) collective-permute-start(bf16[3072,128]{1,0:T(8,128)(2,1)S(1)} %collective-permute-done.8.refs_1_), channel_id=1, source_target_pairs={{0,16},{8,120},{16,32},{24,8},{32,48},{40,24},{48,64},{56,40},{64,... | collective-permute-start | bytes 2359304 | tf_op jit(solution)/shard_map/ppermute | solution.py:623
  42.3 0.0 collective-permute-done.12.next_ref
  42.3 1.5 %collective-permute-done.13.last_ref = bf16[1536,128]{1,0:T(8,128)(2,1)S(1)} collective-permute-done((bf16[1536,128]{1,0:T(8,128)(2,1)S(1)}, bf16[1536,128]{1,0:T(8,128)(2,1)S(1)}, u32[]{:S(2)}, u32[]{:S(2)}) %collective-permute-start.13) | collective-permute-done | bytes 393248 | tf_op jit(solution)/shard_map/ppermute | solution.py:644
  43.8 1.8 %collective-permute-start.16 = (bf16[1536,128]{1,0:T(8,128)(2,1)S(1)}, bf16[1536,128]{1,0:T(8,128)(2,1)S(1)}, u32[]{:S(2)}, u32[]{:S(2)}) collective-permute-start(bf16[1536,128]{1,0:T(8,128)(2,1)S(1)} %broadcast_select_fusion), channel_id=1, source_target_pairs={{0,1},{1,2},{2,3},{3,0},{4,5},{5,6},{6,7},{7,4},{8,11},{9,8},{10,9... | collective-permute-start | bytes 1179656 | tf_op jit(solution)/shard_map/ppermute | solution.py:651
  45.7 2.5 %collective-permute-start.14 = (f32[16,128]{1,0:T(8,128)S(1)}, f32[16,128]{1,0:T(8,128)S(1)}, u32[]{:S(2)}, u32[]{:S(2)}) collective-permute-start(f32[16,128]{1,0:T(8,128)S(1)} %add_add_fusion), channel_id=1, source_target_pairs={{0,4},{1,5},{2,6},{3,7},{4,0},{5,1},{6,2},{7,3},{8,12},{9,13},{10,... | collective-permute-start | bytes 24584 | tf_op jit(solution)/shard_map/ppermute | solution.py:653
  48.2 2.6 %shard_map.106.refs_0_.refs_2_ = bf16[2048,1024]{1,0:T(8,128)(2,1)S(1)} custom-call(s32[32,64]{1,0:T(8,128)S(1)} %get-tuple-element.63.table_ref, bf16[3072,128]{1,0:T(8,128)(2,1)S(1)} %pad_maximum_fusion.refs_0_, bf16[3072,128]{1,0:T(8,128)(2,1)S(1)} %collective-permute-done.8.refs_1_), custom_call_target="tpu_custom_call" | custom-call | tf_op jit(solution)/shard_map/pallas_call | solution.py:307
  50.8 0.0 collective-permute-done.14
  50.8 0.3 collective-permute-start.15
  51.1 0.0 collective-permute-start.19
  51.1 2.5 %collective-permute-done.15 = f32[16,128]{1,0:T(8,128)S(1)} collective-permute-done((f32[16,128]{1,0:T(8,128)S(1)}, f32[16,128]{1,0:T(8,128)S(1)}, u32[]{:S(2)}, u32[]{:S(2)}) %collective-permute-start.15) | collective-permute-done | bytes 8224 | tf_op jit(solution)/shard_map/ppermute | solution.py:657
  53.6 0.0 collective-permute-done.16.far_ref
  53.6 0.0 collective-permute-done.11.refs_0_
  53.6 1.1 %collective-permute-start.17 = (bf16[3072,128]{1,0:T(8,128)(2,1)S(1)}, bf16[3072,128]{1,0:T(8,128)(2,1)S(1)}, u32[]{:S(2)}, u32[]{:S(2)}) collective-permute-start(bf16[3072,128]{1,0:T(8,128)(2,1)S(1)} %collective-permute-done.11.refs_0_), channel_id=1, source_target_pairs={{0,16},{8,120},{16,32},{24,8},{32,48},{40,24},{48,64},{56,40},{64,... | collective-permute-start | bytes 2359304 | tf_op jit(solution)/shard_map/ppermute | solution.py:623
  54.7 1.5 %collective-permute-start.18 = (f32[16,128]{1,0:T(8,128)S(1)}, f32[16,128]{1,0:T(8,128)S(1)}, u32[]{:S(2)}, u32[]{:S(2)}) collective-permute-start(f32[16,128]{1,0:T(8,128)S(1)} %add.22), channel_id=1, source_target_pairs={{0,2},{1,3},{2,0},{3,1},{4,6},{5,7},{6,4},{7,5},{8,10},{9,11},{10,... | collective-permute-start | bytes 24584 | tf_op jit(solution)/shard_map/ppermute | solution.py:662
  56.2 1.8 %shard_map.108.refs_1_ = bf16[1024,1024]{1,0:T(8,128)(2,1)S(1)} custom-call(s32[32,64]{1,0:T(8,128)S(1)} %get-tuple-element.63.table_ref, bf16[3072,128]{1,0:T(8,128)(2,1)S(1)} %collective-permute-done.11.refs_0_), custom_call_target="tpu_custom_call" | custom-call | tf_op jit(solution)/shard_map/pallas_call | solution.py:307
  58.0 0.1 collective-permute-start.21
  58.1 2.5 %shard_map.109.h_ref = bf16[32,256,256]{2,1,0:T(8,128)(2,1)S(1)} custom-call(s32[8,128]{1,0:T(8,128)S(1)} %get-tuple-element.70.table_ref, bf16[1536,128]{1,0:T(8,128)(2,1)S(1)} %constant_dynamic-update-slice_fusion.near_ref, bf16[1536,128]{1,0:T(8,128)(2,1)S(1)} %collective-permute-done.12.next_ref, bf16[1536,128]{1,0:T(8,128)(2,1)S(1)} %collective-permute-done.13.last_ref, ...), custom_call_target="tpu_custom_call" | custom-call | tf_op jit(solution)/shard_map/pallas_call | solution.py:231
  60.6 3.7 %shard_map.110 = (f32[256,1024]{1,0:T(8,128)S(1)}, f32[8,128]{1,0:T(8,128)S(1)}) custom-call(s32[32,64]{1,0:T(8,128)S(1)} %get-tuple-element.63.table_ref, bf16[32,256,256]{2,1,0:T(8,128)(2,1)S(1)} %shard_map.109.h_ref, bf16[2048,1024]{1,0:T(8,128)(2,1)S(1)} %shard_map.106.refs_0_.refs_2_, bf16[3072,128]{1,0:T(8,128)(2,1)S(1)} %collective-permute-done.19.refs_1_), custom_call_target="tpu_custom_call" | custom-call | tf_op jit(solution)/shard_map/pallas_call | solution.py:372
  64.3 0.9 %shard_map.107 = (f32[4,64]{1,0:T(4,128)}, bf16[3,256,256]{2,1,0:T(8,128)(2,1)S(1)}) custom-call(f32[16,128]{1,0:T(8,128)S(1)} %add.24.atoms_ref), custom_call_target="tpu_custom_call" | custom-call | tf_op jit(solution)/shard_map/pallas_call | solution.py:567
  65.2 0.0 collective-permute-done.17.buffer_ref.refs_3_
  65.2 1.9 %collective-permute-start.22 = (bf16[3072,128]{1,0:T(8,128)(2,1)S(1)}, bf16[3072,128]{1,0:T(8,128)(2,1)S(1)}, u32[]{:S(2)}, u32[]{:S(2)}) collective-permute-start(bf16[3072,128]{1,0:T(8,128)(2,1)S(1)} %collective-permute-done.17.buffer_ref.refs_3_), channel_id=1, source_target_pairs={{0,8},{8,0},{16,24},{24,16},{32,40},{40,32},{48,56},{56,48},{64,72... | collective-permute-start | bytes 2359304 | tf_op jit(solution)/shard_map/ppermute | solution.py:626
  67.2 0.2 shard_map.111
  67.4 1.1 %collective-permute-start.20 = (bf16[1536,128]{1,0:T(8,128)(2,1)S(1)}, bf16[1536,128]{1,0:T(8,128)(2,1)S(1)}, u32[]{:S(2)}, u32[]{:S(2)}) collective-permute-start(bf16[1536,128]{1,0:T(8,128)(2,1)S(1)} %shard_map.111), channel_id=1, source_target_pairs={{0,16},{8,120},{16,32},{24,8},{32,48},{40,24},{48,64},{56,40},{64,... | collective-permute-start | bytes 1179656 | tf_op jit(solution)/shard_map/ppermute | solution.py:623
  68.5 0.0 collective-permute-done.21.refs_2_
  68.5 3.2 %shard_map.112 = (f32[256,1024]{1,0:T(8,128)S(1)}, f32[8,128]{1,0:T(8,128)}) custom-call(s32[32,64]{1,0:T(8,128)S(1)} %get-tuple-element.63.table_ref, bf16[32,256,256]{2,1,0:T(8,128)(2,1)S(1)} %shard_map.109.h_ref, f32[256,1024]{1,0:T(8,128)S(1)} %get-tuple-element.79.refs_0_, bf16[1024,1024]{1,0:T(8,128)(2,1)S(1)} %shard_map.108.refs_1_, ...), custom_call_target="tpu_custom_call" | custom-call | tf_op jit(solution)/shard_map/pallas_call | solution.py:372
  71.7 0.0 collective-permute-done.22.refs_4_
  71.7 4.6 %shard_map.113 = (f32[256,1024]{1,0:T(8,128)S(1)}, f32[8,128]{1,0:T(8,128)}) custom-call(s32[32,64]{1,0:T(8,128)S(1)} %get-tuple-element.63.table_ref, bf16[32,256,256]{2,1,0:T(8,128)(2,1)S(1)} %shard_map.109.h_ref, f32[256,1024]{1,0:T(8,128)S(1)} %get-tuple-element.81.refs_0_, bf16[3,256,256]{2,1,0:T(8,128)(2,1)S(1)} %get-tuple-element.82.refs_1_, ...), custom_call_target="tpu_custom_call" | custom-call | tf_op jit(solution)/shard_map/pallas_call | solution.py:372
  76.4 0.0 collective-permute-done.20.refs_0_
  76.4 0.3 collective-permute-start.23
  76.7 1.3 %shard_map.114.refs_1_ = bf16[512,1024]{1,0:T(8,128)(2,1)S(1)} custom-call(s32[32,64]{1,0:T(8,128)S(1)} %get-tuple-element.63.table_ref, bf16[1536,128]{1,0:T(8,128)(2,1)S(1)} %collective-permute-done.20.refs_0_), custom_call_target="tpu_custom_call" | custom-call | tf_op jit(solution)/shard_map/pallas_call | solution.py:307
  78.0 0.2 collective-permute-done.23.refs_2_
  78.2 3.0 %shard_map.115 = (f32[256,1024]{1,0:T(8,128)}, f32[8,128]{1,0:T(8,128)}) custom-call(s32[32,64]{1,0:T(8,128)S(1)} %get-tuple-element.63.table_ref, bf16[32,256,256]{2,1,0:T(8,128)(2,1)S(1)} %shard_map.109.h_ref, f32[256,1024]{1,0:T(8,128)S(1)} %get-tuple-element.84.refs_0_, bf16[512,1024]{1,0:T(8,128)(2,1)S(1)} %shard_map.114.refs_1_, ...), custom_call_target="tpu_custom_call" | custom-call | tf_op jit(solution)/shard_map/pallas_call | solution.py:372
  (15 shorter events, 0.1 us)
Async XLA Ops:
  0.6 32.4 %copy-start = (f32[32,32,128]{2,1,0:T(8,128)S(1)}, f32[32,32,128]{2,1,0:T(8,128)}, u32[]{:S(2)}) copy-start(f32[32,32,128]{2,1,0:T(8,128)} %external_hbm.1) | copy-start | bytes 1572868
  3.4 17.6 %collective-permute-start = (bf16[768,128]{1,0:T(8,128)(2,1)}, bf16[768,128]{1,0:T(8,128)(2,1)S(1)}, u32[]{:S(2)}, u32[]{:S(2)}) collective-permute-start(bf16[768,128]{1,0:T(8,128)(2,1)} %get-tuple-element.45), channel_id=1, source_target_pairs={{0,128},{8,136},{16,144},{24,152},{32,160},{40,168},{48,176},{56,1... | collective-permute-start | bytes 589832 | tf_op jit(solution)/shard_map/ppermute | solution.py:630
  5.6 15.3 %collective-permute-start.1 = (bf16[768,128]{1,0:T(8,128)(2,1)}, bf16[768,128]{1,0:T(8,128)(2,1)S(1)}, u32[]{:S(2)}, u32[]{:S(2)}) collective-permute-start(bf16[768,128]{1,0:T(8,128)(2,1)} %get-tuple-element.45), channel_id=1, source_target_pairs={{0,8},{8,0},{16,24},{24,16},{32,40},{40,32},{48,56},{56,48},{64,72... | collective-permute-start | bytes 589832 | tf_op jit(solution)/shard_map/ppermute | solution.py:626
  6.9 14.1 %collective-permute-start.4 = (bf16[768,128]{1,0:T(8,128)(2,1)}, bf16[768,128]{1,0:T(8,128)(2,1)S(1)}, u32[]{:S(2)}, u32[]{:S(2)}) collective-permute-start(bf16[768,128]{1,0:T(8,128)(2,1)} %get-tuple-element.47), channel_id=1, source_target_pairs={{0,4},{1,5},{2,6},{3,7},{4,0},{5,1},{6,2},{7,3},{8,12},{9,13},{10,... | collective-permute-start | bytes 589832 | tf_op jit(solution)/shard_map/ppermute | solution.py:631
  9.2 6.5 %collective-permute-start.2 = (f32[24,16]{1,0:T(8,128)}, f32[24,16]{1,0:T(8,128)S(1)}, u32[]{:S(2)}, u32[]{:S(2)}) collective-permute-start(f32[24,16]{1,0:T(8,128)} %get-tuple-element.46), channel_id=1, source_target_pairs={{0,1},{1,2},{2,3},{3,4},{4,5},{5,6},{6,7},{7,0},{8,9},{9,10},{10,1... | collective-permute-start | bytes 4616 | tf_op jit(solution)/shard_map/ppermute | solution.py:610
  10.4 5.3 %collective-permute-start.3 = (f32[24,16]{1,0:T(8,128)}, f32[24,16]{1,0:T(8,128)S(1)}, u32[]{:S(2)}, u32[]{:S(2)}) collective-permute-start(f32[24,16]{1,0:T(8,128)} %get-tuple-element.46), channel_id=1, source_target_pairs={{0,7},{1,0},{2,1},{3,2},{4,3},{5,4},{6,5},{7,6},{8,15},{9,8},{10,9... | collective-permute-start | bytes 4616 | tf_op jit(solution)/shard_map/ppermute | solution.py:611
  16.5 8.5 %collective-permute-start.6 = (f32[24,48]{1,0:T(8,128)S(1)}, f32[24,48]{1,0:T(8,128)S(1)}, u32[]{:S(2)}, u32[]{:S(2)}) collective-permute-start(f32[24,48]{1,0:T(8,128)S(1)} %pad_maximum_fusion.1), channel_id=1, source_target_pairs={{0,8},{8,0},{16,24},{24,16},{32,40},{40,32},{48,56},{56,48},{64,72... | collective-permute-start | bytes 13832 | tf_op jit(solution)/shard_map/ppermute | solution.py:605
  17.9 7.1 %collective-permute-start.7 = (f32[24,48]{1,0:T(8,128)S(1)}, f32[24,48]{1,0:T(8,128)S(1)}, u32[]{:S(2)}, u32[]{:S(2)}) collective-permute-start(f32[24,48]{1,0:T(8,128)S(1)} %pad_maximum_fusion.1), channel_id=1, source_target_pairs={{0,248},{8,16},{16,8},{24,32},{32,24},{40,48},{48,40},{56,64},{64,... | collective-permute-start | bytes 13832 | tf_op jit(solution)/shard_map/ppermute | solution.py:606
  19.6 0.8 %copy-start.1 = (s32[128,128]{1,0:T(8,128)S(1)}, s32[128,128]{1,0:T(8,128)}, u32[]{:S(2)}) copy-start(s32[128,128]{1,0:T(8,128)} %pattern_ref.1) | copy-start | bytes 196612
  20.4 9.5 %copy-start.2 = (bf16[768,128]{1,0:T(8,128)(2,1)S(1)}, bf16[768,128]{1,0:T(8,128)(2,1)}, u32[]{:S(2)}) copy-start(bf16[768,128]{1,0:T(8,128)(2,1)} %get-tuple-element.47) | copy-start | bytes 589828
  21.0 5.1 %collective-permute-start.5 = (bf16[768,128]{1,0:T(8,128)(2,1)S(1)}, bf16[768,128]{1,0:T(8,128)(2,1)S(1)}, u32[]{:S(2)}, u32[]{:S(2)}) collective-permute-start(bf16[768,128]{1,0:T(8,128)(2,1)S(1)} %collective-permute-done), channel_id=1, source_target_pairs={{0,8},{8,0},{16,24},{24,16},{32,40},{40,32},{48,56},{56,48},{64,72... | collective-permute-start | bytes 589832 | tf_op jit(solution)/shard_map/ppermute | solution.py:626
  27.1 12.8 %collective-permute-start.8 = (bf16[3072,128]{1,0:T(8,128)(2,1)S(1)}, bf16[3072,128]{1,0:T(8,128)(2,1)S(1)}, u32[]{:S(2)}, u32[]{:S(2)}) collective-permute-start(bf16[3072,128]{1,0:T(8,128)(2,1)S(1)} %pad_maximum_fusion.refs_0_), channel_id=1, source_target_pairs={{0,16},{8,120},{16,32},{24,8},{32,48},{40,24},{48,64},{56,40},{64,... | collective-permute-start | bytes 2359304 | tf_op jit(solution)/shard_map/ppermute | solution.py:623
  29.9 12.4 %collective-permute-start.12 = (bf16[1536,128]{1,0:T(8,128)(2,1)S(1)}, bf16[1536,128]{1,0:T(8,128)(2,1)S(1)}, u32[]{:S(2)}, u32[]{:S(2)}) collective-permute-start(bf16[1536,128]{1,0:T(8,128)(2,1)S(1)} %constant_dynamic-update-slice_fusion.near_ref), channel_id=1, source_target_pairs={{0,3},{1,0},{2,1},{3,2},{4,7},{5,4},{6,5},{7,6},{8,11},{9,8},{10,9... | collective-permute-start | bytes 1179656 | tf_op jit(solution)/shard_map/ppermute | solution.py:643
  33.0 10.7 %collective-permute-start.13 = (bf16[1536,128]{1,0:T(8,128)(2,1)S(1)}, bf16[1536,128]{1,0:T(8,128)(2,1)S(1)}, u32[]{:S(2)}, u32[]{:S(2)}) collective-permute-start(bf16[1536,128]{1,0:T(8,128)(2,1)S(1)} %constant_dynamic-update-slice_fusion.near_ref), channel_id=1, source_target_pairs={{0,1},{1,2},{2,3},{3,0},{4,5},{5,6},{6,7},{7,4},{8,9},{9,10},{10,1... | collective-permute-start | bytes 1179656 | tf_op jit(solution)/shard_map/ppermute | solution.py:644
  36.4 3.5 %collective-permute-start.10 = (f32[16,128]{1,0:T(8,128)S(1)}, f32[16,128]{1,0:T(8,128)S(1)}, u32[]{:S(2)}, u32[]{:S(2)}) collective-permute-start(f32[16,128]{1,0:T(8,128)S(1)} %get-tuple-element.58), channel_id=1, source_target_pairs={{0,248},{8,16},{16,8},{24,32},{32,24},{40,48},{48,40},{56,64},{64,... | collective-permute-start | bytes 24584 | tf_op jit(solution)/shard_map/ppermute | solution.py:606
  36.5 3.4 %collective-permute-start.9 = (f32[16,128]{1,0:T(8,128)S(1)}, f32[16,128]{1,0:T(8,128)S(1)}, u32[]{:S(2)}, u32[]{:S(2)}) collective-permute-start(f32[16,128]{1,0:T(8,128)S(1)} %get-tuple-element.57), channel_id=1, source_target_pairs={{0,8},{8,0},{16,24},{24,16},{32,40},{40,32},{48,56},{56,48},{64,72... | collective-permute-start | bytes 24584 | tf_op jit(solution)/shard_map/ppermute | solution.py:605
  39.8 13.8 %collective-permute-start.11 = (bf16[3072,128]{1,0:T(8,128)(2,1)S(1)}, bf16[3072,128]{1,0:T(8,128)(2,1)S(1)}, u32[]{:S(2)}, u32[]{:S(2)}) collective-permute-start(bf16[3072,128]{1,0:T(8,128)(2,1)S(1)} %collective-permute-done.8.refs_1_), channel_id=1, source_target_pairs={{0,16},{8,120},{16,32},{24,8},{32,48},{40,24},{48,64},{56,40},{64,... | collective-permute-start | bytes 2359304 | tf_op jit(solution)/shard_map/ppermute | solution.py:623
  43.8 9.8 %collective-permute-start.16 = (bf16[1536,128]{1,0:T(8,128)(2,1)S(1)}, bf16[1536,128]{1,0:T(8,128)(2,1)S(1)}, u32[]{:S(2)}, u32[]{:S(2)}) collective-permute-start(bf16[1536,128]{1,0:T(8,128)(2,1)S(1)} %broadcast_select_fusion), channel_id=1, source_target_pairs={{0,1},{1,2},{2,3},{3,0},{4,5},{5,6},{6,7},{7,4},{8,11},{9,8},{10,9... | collective-permute-start | bytes 1179656 | tf_op jit(solution)/shard_map/ppermute | solution.py:651
  45.7 5.2 %collective-permute-start.14 = (f32[16,128]{1,0:T(8,128)S(1)}, f32[16,128]{1,0:T(8,128)S(1)}, u32[]{:S(2)}, u32[]{:S(2)}) collective-permute-start(f32[16,128]{1,0:T(8,128)S(1)} %add_add_fusion), channel_id=1, source_target_pairs={{0,4},{1,5},{2,6},{3,7},{4,0},{5,1},{6,2},{7,3},{8,12},{9,13},{10,... | collective-permute-start | bytes 24584 | tf_op jit(solution)/shard_map/ppermute | solution.py:653
  50.8 2.7 %collective-permute-start.15 = (f32[16,128]{1,0:T(8,128)S(1)}, f32[16,128]{1,0:T(8,128)S(1)}, u32[]{:S(2)}, u32[]{:S(2)}) collective-permute-start(f32[16,128]{1,0:T(8,128)S(1)} %add.21), channel_id=1, source_target_pairs={{0,1},{1,0},{2,3},{3,2},{4,5},{5,4},{6,7},{7,6},{8,9},{9,8},{10,11... | collective-permute-start | bytes 24584 | tf_op jit(solution)/shard_map/ppermute | solution.py:657
  51.1 9.5 %collective-permute-start.19 = (bf16[3072,128]{1,0:T(8,128)(2,1)S(1)}, bf16[3072,128]{1,0:T(8,128)(2,1)S(1)}, u32[]{:S(2)}, u32[]{:S(2)}) collective-permute-start(bf16[3072,128]{1,0:T(8,128)(2,1)S(1)} %collective-permute-done.8.refs_1_), channel_id=1, source_target_pairs={{0,8},{8,0},{16,24},{24,16},{32,40},{40,32},{48,56},{56,48},{64,72... | collective-permute-start | bytes 2359304 | tf_op jit(solution)/shard_map/ppermute | solution.py:626
  53.6 11.6 %collective-permute-start.17 = (bf16[3072,128]{1,0:T(8,128)(2,1)S(1)}, bf16[3072,128]{1,0:T(8,128)(2,1)S(1)}, u32[]{:S(2)}, u32[]{:S(2)}) collective-permute-start(bf16[3072,128]{1,0:T(8,128)(2,1)S(1)} %collective-permute-done.11.refs_0_), channel_id=1, source_target_pairs={{0,16},{8,120},{16,32},{24,8},{32,48},{40,24},{48,64},{56,40},{64,... | collective-permute-start | bytes 2359304 | tf_op jit(solution)/shard_map/ppermute | solution.py:623
  54.7 9.6 %collective-permute-start.18 = (f32[16,128]{1,0:T(8,128)S(1)}, f32[16,128]{1,0:T(8,128)S(1)}, u32[]{:S(2)}, u32[]{:S(2)}) collective-permute-start(f32[16,128]{1,0:T(8,128)S(1)} %add.22), channel_id=1, source_target_pairs={{0,2},{1,3},{2,0},{3,1},{4,6},{5,7},{6,4},{7,5},{8,10},{9,11},{10,... | collective-permute-start | bytes 24584 | tf_op jit(solution)/shard_map/ppermute | solution.py:662
  58.0 10.6 %collective-permute-start.21 = (bf16[3072,128]{1,0:T(8,128)(2,1)S(1)}, bf16[3072,128]{1,0:T(8,128)(2,1)S(1)}, u32[]{:S(2)}, u32[]{:S(2)}) collective-permute-start(bf16[3072,128]{1,0:T(8,128)(2,1)S(1)} %collective-permute-done.11.refs_0_), channel_id=1, source_target_pairs={{0,8},{8,0},{16,24},{24,16},{32,40},{40,32},{48,56},{56,48},{64,72... | collective-permute-start | bytes 2359304 | tf_op jit(solution)/shard_map/ppermute | solution.py:626
  65.2 6.5 %collective-permute-start.22 = (bf16[3072,128]{1,0:T(8,128)(2,1)S(1)}, bf16[3072,128]{1,0:T(8,128)(2,1)S(1)}, u32[]{:S(2)}, u32[]{:S(2)}) collective-permute-start(bf16[3072,128]{1,0:T(8,128)(2,1)S(1)} %collective-permute-done.17.buffer_ref.refs_3_), channel_id=1, source_target_pairs={{0,8},{8,0},{16,24},{24,16},{32,40},{40,32},{48,56},{56,48},{64,72... | collective-permute-start | bytes 2359304 | tf_op jit(solution)/shard_map/ppermute | solution.py:626
  67.4 9.0 %collective-permute-start.20 = (bf16[1536,128]{1,0:T(8,128)(2,1)S(1)}, bf16[1536,128]{1,0:T(8,128)(2,1)S(1)}, u32[]{:S(2)}, u32[]{:S(2)}) collective-permute-start(bf16[1536,128]{1,0:T(8,128)(2,1)S(1)} %shard_map.111), channel_id=1, source_target_pairs={{0,16},{8,120},{16,32},{24,8},{32,48},{40,24},{48,64},{56,40},{64,... | collective-permute-start | bytes 1179656 | tf_op jit(solution)/shard_map/ppermute | solution.py:623
  76.4 1.8 %collective-permute-start.23 = (bf16[1536,128]{1,0:T(8,128)(2,1)S(1)}, bf16[1536,128]{1,0:T(8,128)(2,1)S(1)}, u32[]{:S(2)}, u32[]{:S(2)}) collective-permute-start(bf16[1536,128]{1,0:T(8,128)(2,1)S(1)} %collective-permute-done.20.refs_0_), channel_id=1, source_target_pairs={{0,8},{8,0},{16,24},{24,16},{32,40},{40,32},{48,56},{56,48},{64,72... | collective-permute-start | bytes 1179656 | tf_op jit(solution)/shard_map/ppermute | solution.py:626

commit v6 on v5

--- a/solution.py
+++ b/solution.py
@@ -633,7 +633,7 @@
     info = jnp.concatenate([before, info, after], axis=1)
     pc = swap(pp)
     near, far = to_rows(info, info)
-    py, pc, info, hy, table_p, table_h = together((py, pc, info, hy, table_p, table_h))
+    py, pc, info, hy = together((py, pc, info, hy))
     info = jnp.concatenate([info, near, far, jnp.zeros((24, 112), F32)], axis=1)
     q = jnp.concatenate([pp, py, pc, swap(py)], axis=0)
     q, info = together((q, info))
@@ -645,7 +645,7 @@
     density, share, near, far = grid_part(info, external)
     near, far = to_rows(near, far)
     share = share + near + far
-    q1, share = together((q1, share))
+    q1, share, table_p, table_h = together((q1, share, table_p, table_h))
 
     q2, x1 = step(q1), swap(q1)
     h_far = lax.ppermute(jnp.where(core == 0, h_last, h_next), ("row", "col"), ALONG_X)

time: 81.7 us -> 81.1 us (level)
  starting transfers between devices: 37.4 us -> 39.5 us
  waiting for transfers between devices: 9.58 us -> 7.83 us
  local copies, waits for them, and re-layouts: 0.97 us -> 0.14 us
    ppermute x4, starting transfers between devices: 7.53 us -> 9.85 us  [step(): return lax.ppermute(chain, 'row', ALONG_Z)]
    ppermute x6, starting transfers between devices: 7.56 us -> 6.1 us  [swap(): return lax.ppermute(chain, 'row', ACROSS_CORES)]
    ppermute x1, waiting for transfers between devices: 1.45 us -> 0.11 us  [on_device(): h_last = lax.ppermute(h0, 'col', col_pairs(0, 1))]
    ppermute x1, starting transfers between devices: 1.83 us -> 3.17 us  [on_device(): lax.ppermute(jnp.where(core == 0, h_last, h_next), ('row', 'col'), ALONG_X)]
    unnamed x7, local copies, waits for them, and re-layouts: 0.86 us -> 0.03 us
  transfers between devices with their start and end apart: 24 -> 24, of which waited for: 6 -> 6; matrix products, arithmetic and copies ran while one was open for 1% -> 1% of each run, Pallas kernels for 30% -> 31%
where the time goes in v6:
time: 81.1 us; the launch traced here: 80.9 us
  starting transfers between devices  39.5 us (49%)
  Pallas kernels  30.5 us (38%)
  waiting for transfers between devices  7.83 us (10%)
  other arithmetic  1.9 us (2%)
  between operations  1.07 us (1%)
    pallas_call x4, Pallas kernels, accumulate(): pl.pallas_call(functools.partial(accumulate_kernel, ready, groups, before...  14.5 us
    ppermute x4, starting transfers between devices, step(): return lax.ppermute(chain, 'row', ALONG_Z)  9.85 us
    ppermute x6, starting transfers between devices, swap(): return lax.ppermute(chain, 'row', ACROSS_CORES)  6.1 us
    pallas_call x3, Pallas kernels, unpack(): pl.pallas_call(functools.partial(unpack_kernel, groups), out_shape=jax.Sh...  5.75 us
    ppermute x1, starting transfers between devices, from_neighbours(): after = lax.ppermute(first, axis, ring(axis, size, -1))  3.87 us
    pallas_call x1, Pallas kernels, grid_part(): pl.pallas_call(grid_kernel, out_shape=(jax.ShapeDtypeStruct(external.shap...  3.31 us
    ppermute x1, starting transfers between devices, on_device(): lax.ppermute(jnp.where(core == 0, h_last, h_next), ('row', 'col'), ALONG_X)  3.17 us
    ppermute x1, starting transfers between devices, on_device(): h_next = lax.ppermute(h0, 'col', col_pairs(0, 3))  3.09 us
  transfers between devices with their start and end apart: 24, of which 6 were waited for; matrix products, arithmetic and copies ran while one was open for 1% of the time, Pallas kernels for 31%

profile of v6, /device:TPU:1, one launch (start us, length us, event | category | flops | bytes accessed | tf_op | source)
XLA Modules:
  0.0 80.9 jit_solution(9813632834940717234)
XLA Ops:
  0.6 2.8 %shard_map.103 = (bf16[768,128]{1,0:T(8,128)(2,1)}, bf16[768,128]{1,0:T(8,128)(2,1)}, f32[24,16]{1,0:T(8,128)}) custom-call(s32[128,128]{1,0:T(8,128)} %pattern_ref.1, bf16[256,1024]{1,0:T(8,128)(2,1)} %h_hbm.1, bf16[256,1024]{1,0:T(8,128)(2,1)} %p_hbm.1, f32[4,64]{1,0:T(4,128)} %coef_hbm.1, s32[4]{0:T(128)} %x_hbm.1, s32[4]{0:T(128)} %y_hbm.1, s32[4]{0:T(128)} %z_hbm.1), custom_call_target="tpu_custom_call" | custom-call | tf_op jit(solution)/shard_map/pallas_call | solution.py:101
  3.4 0.0 copy-start.2
  3.4 0.0 copy-start.1
  3.5 2.2 %collective-permute-start = (bf16[768,128]{1,0:T(8,128)(2,1)}, bf16[768,128]{1,0:T(8,128)(2,1)S(1)}, u32[]{:S(2)}, u32[]{:S(2)}) collective-permute-start(bf16[768,128]{1,0:T(8,128)(2,1)} %get-tuple-element.45), channel_id=1, source_target_pairs={{0,128},{8,136},{16,144},{24,152},{32,160},{40,168},{48,176},{56,1... | collective-permute-start | bytes 589832 | tf_op jit(solution)/shard_map/ppermute | solution.py:630
  5.7 1.2 %collective-permute-start.1 = (bf16[768,128]{1,0:T(8,128)(2,1)}, bf16[768,128]{1,0:T(8,128)(2,1)S(1)}, u32[]{:S(2)}, u32[]{:S(2)}) collective-permute-start(bf16[768,128]{1,0:T(8,128)(2,1)} %get-tuple-element.45), channel_id=1, source_target_pairs={{0,8},{8,0},{16,24},{24,16},{32,40},{40,32},{48,56},{56,48},{64,72... | collective-permute-start | bytes 589832 | tf_op jit(solution)/shard_map/ppermute | solution.py:626
  6.9 2.4 %collective-permute-start.4 = (bf16[768,128]{1,0:T(8,128)(2,1)}, bf16[768,128]{1,0:T(8,128)(2,1)S(1)}, u32[]{:S(2)}, u32[]{:S(2)}) collective-permute-start(bf16[768,128]{1,0:T(8,128)(2,1)} %get-tuple-element.47), channel_id=1, source_target_pairs={{0,4},{1,5},{2,6},{3,7},{4,0},{5,1},{6,2},{7,3},{8,12},{9,13},{10,... | collective-permute-start | bytes 589832 | tf_op jit(solution)/shard_map/ppermute | solution.py:631
  9.2 1.2 %collective-permute-start.2 = (f32[24,16]{1,0:T(8,128)}, f32[24,16]{1,0:T(8,128)S(1)}, u32[]{:S(2)}, u32[]{:S(2)}) collective-permute-start(f32[24,16]{1,0:T(8,128)} %get-tuple-element.46), channel_id=1, source_target_pairs={{0,1},{1,2},{2,3},{3,4},{4,5},{5,6},{6,7},{7,0},{8,9},{9,10},{10,1... | collective-permute-start | bytes 4616 | tf_op jit(solution)/shard_map/ppermute | solution.py:610
  10.5 3.9 %collective-permute-start.3 = (f32[24,16]{1,0:T(8,128)}, f32[24,16]{1,0:T(8,128)S(1)}, u32[]{:S(2)}, u32[]{:S(2)}) collective-permute-start(f32[24,16]{1,0:T(8,128)} %get-tuple-element.46), channel_id=1, source_target_pairs={{0,7},{1,0},{2,1},{3,2},{4,3},{5,4},{6,5},{7,6},{8,15},{9,8},{10,9... | collective-permute-start | bytes 4616 | tf_op jit(solution)/shard_map/ppermute | solution.py:611
  14.3 1.4 %collective-permute-done.2 = f32[24,16]{1,0:T(8,128)S(1)} collective-permute-done((f32[24,16]{1,0:T(8,128)}, f32[24,16]{1,0:T(8,128)S(1)}, u32[]{:S(2)}, u32[]{:S(2)}) %collective-permute-start.2) | collective-permute-done | bytes 1568 | tf_op jit(solution)/shard_map/ppermute | solution.py:610
  15.7 0.0 collective-permute-done.3
  15.7 0.8 pad_maximum_fusion.1
  16.5 1.5 %collective-permute-start.6 = (f32[24,48]{1,0:T(8,128)S(1)}, f32[24,48]{1,0:T(8,128)S(1)}, u32[]{:S(2)}, u32[]{:S(2)}) collective-permute-start(f32[24,48]{1,0:T(8,128)S(1)} %pad_maximum_fusion.1), channel_id=1, source_target_pairs={{0,8},{8,0},{16,24},{24,16},{32,40},{40,32},{48,56},{56,48},{64,72... | collective-permute-start | bytes 13832 | tf_op jit(solution)/shard_map/ppermute | solution.py:605
  18.0 1.6 %collective-permute-start.7 = (f32[24,48]{1,0:T(8,128)S(1)}, f32[24,48]{1,0:T(8,128)S(1)}, u32[]{:S(2)}, u32[]{:S(2)}) collective-permute-start(f32[24,48]{1,0:T(8,128)S(1)} %pad_maximum_fusion.1), channel_id=1, source_target_pairs={{0,248},{8,16},{16,8},{24,32},{32,24},{40,48},{48,40},{56,64},{64,... | collective-permute-start | bytes 13832 | tf_op jit(solution)/shard_map/ppermute | solution.py:606
  19.6 0.1 pad.3.clone
  19.7 0.0 collective-permute-done
  19.7 0.0 collective-permute-done.1
  19.7 0.0 collective-permute-done.4
  19.7 4.0 %collective-permute-start.5 = (bf16[768,128]{1,0:T(8,128)(2,1)S(1)}, bf16[768,128]{1,0:T(8,128)(2,1)S(1)}, u32[]{:S(2)}, u32[]{:S(2)}) collective-permute-start(bf16[768,128]{1,0:T(8,128)(2,1)S(1)} %collective-permute-done), channel_id=1, source_target_pairs={{0,8},{8,0},{16,24},{24,16},{32,40},{40,32},{48,56},{56,48},{64,72... | collective-permute-start | bytes 589832 | tf_op jit(solution)/shard_map/ppermute | solution.py:626
  23.7 0.0 collective-permute-done.6
  23.7 0.0 collective-permute-done.7
  23.7 0.1 maximum_maximum_fusion.info_ref
  23.8 1.0 %collective-permute-done.5 = bf16[768,128]{1,0:T(8,128)(2,1)S(1)} collective-permute-done((bf16[768,128]{1,0:T(8,128)(2,1)S(1)}, bf16[768,128]{1,0:T(8,128)(2,1)S(1)}, u32[]{:S(2)}, u32[]{:S(2)}) %collective-permute-start.5) | collective-permute-done | bytes 196640 | tf_op jit(solution)/shard_map/ppermute | solution.py:626
  24.8 1.0 %pad_maximum_fusion.refs_0_ = bf16[3072,128]{1,0:T(8,128)(2,1)S(1)} fusion(bf16[768,128]{1,0:T(8,128)(2,1)S(1)} %collective-permute-done.5, bf16[768,128]{1,0:T(8,128)(2,1)S(1)} %collective-permute-done.1, bf16[768,128]{1,0:T(8,128)(2,1)S(1)} %collective-permute-done, bf16[768,128]{1,0:T(8,128)(2,1)} %get-tuple-element.45), kind=kLoop, calls=%fused_computation | loop fusion | flops 3145728 | bytes 1572864 | tf_op jit(solution)/shard_map/concatenate | solution.py:638
  25.7 4.2 %collective-permute-start.8 = (bf16[3072,128]{1,0:T(8,128)(2,1)S(1)}, bf16[3072,128]{1,0:T(8,128)(2,1)S(1)}, u32[]{:S(2)}, u32[]{:S(2)}) collective-permute-start(bf16[3072,128]{1,0:T(8,128)(2,1)S(1)} %pad_maximum_fusion.refs_0_), channel_id=1, source_target_pairs={{0,16},{8,120},{16,32},{24,8},{32,48},{40,24},{48,64},{56,40},{64,... | collective-permute-start | bytes 2359304 | tf_op jit(solution)/shard_map/ppermute | solution.py:623
  30.0 3.1 %collective-permute-start.12 = (bf16[1536,128]{1,0:T(8,128)(2,1)S(1)}, bf16[1536,128]{1,0:T(8,128)(2,1)S(1)}, u32[]{:S(2)}, u32[]{:S(2)}) collective-permute-start(bf16[1536,128]{1,0:T(8,128)(2,1)S(1)} %constant_dynamic-update-slice_fusion.near_ref), channel_id=1, source_target_pairs={{0,3},{1,0},{2,1},{3,2},{4,7},{5,4},{6,5},{7,6},{8,11},{9,8},{10,9... | collective-permute-start | bytes 1179656 | tf_op jit(solution)/shard_map/ppermute | solution.py:643
  33.1 3.3 %shard_map.104 = (f32[32,32,128]{2,1,0:T(8,128)}, f32[16,128]{1,0:T(8,128)S(1)}, f32[16,128]{1,0:T(8,128)S(1)}, f32[16,128]{1,0:T(8,128)S(1)}) custom-call(f32[24,256]{1,0:T(8,128)S(1)} %maximum_maximum_fusion.info_ref, f32[32,32,128]{2,1,0:T(8,128)S(1)} %copy-done), custom_call_target="tpu_custom_call" | custom-call | tf_op jit(solution)/shard_map/pallas_call | solution.py:509
  36.4 0.1 collective-permute-start.10
  36.5 0.3 collective-permute-start.9
  36.8 0.5 shard_map.105
  37.3 2.6 %collective-permute-done.10 = f32[16,128]{1,0:T(8,128)S(1)} collective-permute-done((f32[16,128]{1,0:T(8,128)S(1)}, f32[16,128]{1,0:T(8,128)S(1)}, u32[]{:S(2)}, u32[]{:S(2)}) %collective-permute-start.10) | collective-permute-done | bytes 8224 | tf_op jit(solution)/shard_map/ppermute | solution.py:606
  39.9 0.0 collective-permute-done.9
  39.9 0.0 collective-permute-done.8.refs_1_
  39.9 2.5 %collective-permute-start.11 = (bf16[3072,128]{1,0:T(8,128)(2,1)S(1)}, bf16[3072,128]{1,0:T(8,128)(2,1)S(1)}, u32[]{:S(2)}, u32[]{:S(2)}) collective-permute-start(bf16[3072,128]{1,0:T(8,128)(2,1)S(1)} %collective-permute-done.8.refs_1_), channel_id=1, source_target_pairs={{0,16},{8,120},{16,32},{24,8},{32,48},{40,24},{48,64},{56,40},{64,... | collective-permute-start | bytes 2359304 | tf_op jit(solution)/shard_map/ppermute | solution.py:623
  42.4 0.1 collective-permute-done.13.last_ref
  42.5 3.2 %collective-permute-start.16 = (bf16[1536,128]{1,0:T(8,128)(2,1)S(1)}, bf16[1536,128]{1,0:T(8,128)(2,1)S(1)}, u32[]{:S(2)}, u32[]{:S(2)}) collective-permute-start(bf16[1536,128]{1,0:T(8,128)(2,1)S(1)} %broadcast_select_fusion), channel_id=1, source_target_pairs={{0,1},{1,2},{2,3},{3,0},{4,5},{5,6},{6,7},{7,4},{8,11},{9,8},{10,9... | collective-permute-start | bytes 1179656 | tf_op jit(solution)/shard_map/ppermute | solution.py:651
  45.7 2.5 %collective-permute-start.14 = (f32[16,128]{1,0:T(8,128)S(1)}, f32[16,128]{1,0:T(8,128)S(1)}, u32[]{:S(2)}, u32[]{:S(2)}) collective-permute-start(f32[16,128]{1,0:T(8,128)S(1)} %add_add_fusion), channel_id=1, source_target_pairs={{0,4},{1,5},{2,6},{3,7},{4,0},{5,1},{6,2},{7,3},{8,12},{9,13},{10,... | collective-permute-start | bytes 24584 | tf_op jit(solution)/shard_map/ppermute | solution.py:653
  48.2 2.6 %shard_map.106.refs_0_.refs_2_ = bf16[2048,1024]{1,0:T(8,128)(2,1)S(1)} custom-call(s32[32,64]{1,0:T(8,128)S(1)} %get-tuple-element.63.table_ref, bf16[3072,128]{1,0:T(8,128)(2,1)S(1)} %pad_maximum_fusion.refs_0_, bf16[3072,128]{1,0:T(8,128)(2,1)S(1)} %collective-permute-done.8.refs_1_), custom_call_target="tpu_custom_call" | custom-call | tf_op jit(solution)/shard_map/pallas_call | solution.py:307
  50.8 0.0 collective-permute-done.14
  50.9 0.1 collective-permute-start.15
  51.0 0.1 collective-permute-start.19
  51.1 2.4 %collective-permute-done.15 = f32[16,128]{1,0:T(8,128)S(1)} collective-permute-done((f32[16,128]{1,0:T(8,128)S(1)}, f32[16,128]{1,0:T(8,128)S(1)}, u32[]{:S(2)}, u32[]{:S(2)}) %collective-permute-start.15) | collective-permute-done | bytes 8224 | tf_op jit(solution)/shard_map/ppermute | solution.py:657
  53.5 0.0 collective-permute-done.16.far_ref
  53.5 0.0 collective-permute-done.11.refs_0_
  53.5 1.2 %collective-permute-start.17 = (bf16[3072,128]{1,0:T(8,128)(2,1)S(1)}, bf16[3072,128]{1,0:T(8,128)(2,1)S(1)}, u32[]{:S(2)}, u32[]{:S(2)}) collective-permute-start(bf16[3072,128]{1,0:T(8,128)(2,1)S(1)} %collective-permute-done.11.refs_0_), channel_id=1, source_target_pairs={{0,16},{8,120},{16,32},{24,8},{32,48},{40,24},{48,64},{56,40},{64,... | collective-permute-start | bytes 2359304 | tf_op jit(solution)/shard_map/ppermute | solution.py:623
  54.7 1.5 %collective-permute-start.18 = (f32[16,128]{1,0:T(8,128)S(1)}, f32[16,128]{1,0:T(8,128)S(1)}, u32[]{:S(2)}, u32[]{:S(2)}) collective-permute-start(f32[16,128]{1,0:T(8,128)S(1)} %add.22), channel_id=1, source_target_pairs={{0,2},{1,3},{2,0},{3,1},{4,6},{5,7},{6,4},{7,5},{8,10},{9,11},{10,... | collective-permute-start | bytes 24584 | tf_op jit(solution)/shard_map/ppermute | solution.py:662
  56.2 1.8 %shard_map.108.refs_1_ = bf16[1024,1024]{1,0:T(8,128)(2,1)S(1)} custom-call(s32[32,64]{1,0:T(8,128)S(1)} %get-tuple-element.63.table_ref, bf16[3072,128]{1,0:T(8,128)(2,1)S(1)} %collective-permute-done.11.refs_0_), custom_call_target="tpu_custom_call" | custom-call | tf_op jit(solution)/shard_map/pallas_call | solution.py:307
  58.0 0.1 collective-permute-start.21
  58.1 2.5 %shard_map.109.h_ref = bf16[32,256,256]{2,1,0:T(8,128)(2,1)S(1)} custom-call(s32[8,128]{1,0:T(8,128)S(1)} %get-tuple-element.70.table_ref, bf16[1536,128]{1,0:T(8,128)(2,1)S(1)} %constant_dynamic-update-slice_fusion.near_ref, bf16[1536,128]{1,0:T(8,128)(2,1)S(1)} %collective-permute-done.12.next_ref, bf16[1536,128]{1,0:T(8,128)(2,1)S(1)} %collective-permute-done.13.last_ref, ...), custom_call_target="tpu_custom_call" | custom-call | tf_op jit(solution)/shard_map/pallas_call | solution.py:231
  60.6 0.0 collective-permute-done.19.refs_1_
  60.7 3.7 %shard_map.110 = (f32[256,1024]{1,0:T(8,128)S(1)}, f32[8,128]{1,0:T(8,128)S(1)}) custom-call(s32[32,64]{1,0:T(8,128)S(1)} %get-tuple-element.63.table_ref, bf16[32,256,256]{2,1,0:T(8,128)(2,1)S(1)} %shard_map.109.h_ref, bf16[2048,1024]{1,0:T(8,128)(2,1)S(1)} %shard_map.106.refs_0_.refs_2_, bf16[3072,128]{1,0:T(8,128)(2,1)S(1)} %collective-permute-done.19.refs_1_), custom_call_target="tpu_custom_call" | custom-call | tf_op jit(solution)/shard_map/pallas_call | solution.py:372
  64.3 0.0 collective-permute-done.18
  64.3 0.9 %shard_map.107 = (f32[4,64]{1,0:T(4,128)}, bf16[3,256,256]{2,1,0:T(8,128)(2,1)S(1)}) custom-call(f32[16,128]{1,0:T(8,128)S(1)} %add.24.atoms_ref), custom_call_target="tpu_custom_call" | custom-call | tf_op jit(solution)/shard_map/pallas_call | solution.py:567
  65.3 0.0 collective-permute-done.17.buffer_ref.refs_3_
  65.3 0.6 collective-permute-start.22
  65.9 0.2 shard_map.111
  66.1 2.0 %collective-permute-start.20 = (bf16[1536,128]{1,0:T(8,128)(2,1)S(1)}, bf16[1536,128]{1,0:T(8,128)(2,1)S(1)}, u32[]{:S(2)}, u32[]{:S(2)}) collective-permute-start(bf16[1536,128]{1,0:T(8,128)(2,1)S(1)} %shard_map.111), channel_id=1, source_target_pairs={{0,16},{8,120},{16,32},{24,8},{32,48},{40,24},{48,64},{56,40},{64,... | collective-permute-start | bytes 1179656 | tf_op jit(solution)/shard_map/ppermute | solution.py:623
  68.0 3.2 %shard_map.112 = (f32[256,1024]{1,0:T(8,128)S(1)}, f32[8,128]{1,0:T(8,128)}) custom-call(s32[32,64]{1,0:T(8,128)S(1)} %get-tuple-element.63.table_ref, bf16[32,256,256]{2,1,0:T(8,128)(2,1)S(1)} %shard_map.109.h_ref, f32[256,1024]{1,0:T(8,128)S(1)} %get-tuple-element.79.refs_0_, bf16[1024,1024]{1,0:T(8,128)(2,1)S(1)} %shard_map.108.refs_1_, ...), custom_call_target="tpu_custom_call" | custom-call | tf_op jit(solution)/shard_map/pallas_call | solution.py:372
  71.2 0.0 collective-permute-done.22.refs_4_
  71.3 4.6 %shard_map.113 = (f32[256,1024]{1,0:T(8,128)S(1)}, f32[8,128]{1,0:T(8,128)}) custom-call(s32[32,64]{1,0:T(8,128)S(1)} %get-tuple-element.63.table_ref, bf16[32,256,256]{2,1,0:T(8,128)(2,1)S(1)} %shard_map.109.h_ref, f32[256,1024]{1,0:T(8,128)S(1)} %get-tuple-element.81.refs_0_, bf16[3,256,256]{2,1,0:T(8,128)(2,1)S(1)} %get-tuple-element.82.refs_1_, ...), custom_call_target="tpu_custom_call" | custom-call | tf_op jit(solution)/shard_map/pallas_call | solution.py:372
  75.9 0.0 collective-permute-done.20.refs_0_
  75.9 0.1 collective-permute-start.23
  76.0 1.3 %shard_map.114.refs_1_ = bf16[512,1024]{1,0:T(8,128)(2,1)S(1)} custom-call(s32[32,64]{1,0:T(8,128)S(1)} %get-tuple-element.63.table_ref, bf16[1536,128]{1,0:T(8,128)(2,1)S(1)} %collective-permute-done.20.refs_0_), custom_call_target="tpu_custom_call" | custom-call | tf_op jit(solution)/shard_map/pallas_call | solution.py:307
  77.4 0.4 collective-permute-done.23.refs_2_
  77.7 3.0 %shard_map.115 = (f32[256,1024]{1,0:T(8,128)}, f32[8,128]{1,0:T(8,128)}) custom-call(s32[32,64]{1,0:T(8,128)S(1)} %get-tuple-element.63.table_ref, bf16[32,256,256]{2,1,0:T(8,128)(2,1)S(1)} %shard_map.109.h_ref, f32[256,1024]{1,0:T(8,128)S(1)} %get-tuple-element.84.refs_0_, bf16[512,1024]{1,0:T(8,128)(2,1)S(1)} %shard_map.114.refs_1_, ...), custom_call_target="tpu_custom_call" | custom-call | tf_op jit(solution)/shard_map/pallas_call | solution.py:372
  (15 shorter events, 0.1 us)
Async XLA Ops:
  0.6 32.4 %copy-start = (f32[32,32,128]{2,1,0:T(8,128)S(1)}, f32[32,32,128]{2,1,0:T(8,128)}, u32[]{:S(2)}) copy-start(f32[32,32,128]{2,1,0:T(8,128)} %external_hbm.1) | copy-start | bytes 1572868
  3.4 26.5 %copy-start.2 = (bf16[768,128]{1,0:T(8,128)(2,1)S(1)}, bf16[768,128]{1,0:T(8,128)(2,1)}, u32[]{:S(2)}) copy-start(bf16[768,128]{1,0:T(8,128)(2,1)} %get-tuple-element.47) | copy-start | bytes 589828
  3.4 33.3 %copy-start.1 = (s32[128,128]{1,0:T(8,128)S(1)}, s32[128,128]{1,0:T(8,128)}, u32[]{:S(2)}) copy-start(s32[128,128]{1,0:T(8,128)} %pattern_ref.1) | copy-start | bytes 196612
  3.5 16.2 %collective-permute-start = (bf16[768,128]{1,0:T(8,128)(2,1)}, bf16[768,128]{1,0:T(8,128)(2,1)S(1)}, u32[]{:S(2)}, u32[]{:S(2)}) collective-permute-start(bf16[768,128]{1,0:T(8,128)(2,1)} %get-tuple-element.45), channel_id=1, source_target_pairs={{0,128},{8,136},{16,144},{24,152},{32,160},{40,168},{48,176},{56,1... | collective-permute-start | bytes 589832 | tf_op jit(solution)/shard_map/ppermute | solution.py:630
  5.7 14.0 %collective-permute-start.1 = (bf16[768,128]{1,0:T(8,128)(2,1)}, bf16[768,128]{1,0:T(8,128)(2,1)S(1)}, u32[]{:S(2)}, u32[]{:S(2)}) collective-permute-start(bf16[768,128]{1,0:T(8,128)(2,1)} %get-tuple-element.45), channel_id=1, source_target_pairs={{0,8},{8,0},{16,24},{24,16},{32,40},{40,32},{48,56},{56,48},{64,72... | collective-permute-start | bytes 589832 | tf_op jit(solution)/shard_map/ppermute | solution.py:626
  6.9 12.8 %collective-permute-start.4 = (bf16[768,128]{1,0:T(8,128)(2,1)}, bf16[768,128]{1,0:T(8,128)(2,1)S(1)}, u32[]{:S(2)}, u32[]{:S(2)}) collective-permute-start(bf16[768,128]{1,0:T(8,128)(2,1)} %get-tuple-element.47), channel_id=1, source_target_pairs={{0,4},{1,5},{2,6},{3,7},{4,0},{5,1},{6,2},{7,3},{8,12},{9,13},{10,... | collective-permute-start | bytes 589832 | tf_op jit(solution)/shard_map/ppermute | solution.py:631
  9.2 6.5 %collective-permute-start.2 = (f32[24,16]{1,0:T(8,128)}, f32[24,16]{1,0:T(8,128)S(1)}, u32[]{:S(2)}, u32[]{:S(2)}) collective-permute-start(f32[24,16]{1,0:T(8,128)} %get-tuple-element.46), channel_id=1, source_target_pairs={{0,1},{1,2},{2,3},{3,4},{4,5},{5,6},{6,7},{7,0},{8,9},{9,10},{10,1... | collective-permute-start | bytes 4616 | tf_op jit(solution)/shard_map/ppermute | solution.py:610
  10.5 5.3 %collective-permute-start.3 = (f32[24,16]{1,0:T(8,128)}, f32[24,16]{1,0:T(8,128)S(1)}, u32[]{:S(2)}, u32[]{:S(2)}) collective-permute-start(f32[24,16]{1,0:T(8,128)} %get-tuple-element.46), channel_id=1, source_target_pairs={{0,7},{1,0},{2,1},{3,2},{4,3},{5,4},{6,5},{7,6},{8,15},{9,8},{10,9... | collective-permute-start | bytes 4616 | tf_op jit(solution)/shard_map/ppermute | solution.py:611
  16.5 7.2 %collective-permute-start.6 = (f32[24,48]{1,0:T(8,128)S(1)}, f32[24,48]{1,0:T(8,128)S(1)}, u32[]{:S(2)}, u32[]{:S(2)}) collective-permute-start(f32[24,48]{1,0:T(8,128)S(1)} %pad_maximum_fusion.1), channel_id=1, source_target_pairs={{0,8},{8,0},{16,24},{24,16},{32,40},{40,32},{48,56},{56,48},{64,72... | collective-permute-start | bytes 13832 | tf_op jit(solution)/shard_map/ppermute | solution.py:605
  18.0 5.7 %collective-permute-start.7 = (f32[24,48]{1,0:T(8,128)S(1)}, f32[24,48]{1,0:T(8,128)S(1)}, u32[]{:S(2)}, u32[]{:S(2)}) collective-permute-start(f32[24,48]{1,0:T(8,128)S(1)} %pad_maximum_fusion.1), channel_id=1, source_target_pairs={{0,248},{8,16},{16,8},{24,32},{32,24},{40,48},{48,40},{56,64},{64,... | collective-permute-start | bytes 13832 | tf_op jit(solution)/shard_map/ppermute | solution.py:606
  19.7 5.1 %collective-permute-start.5 = (bf16[768,128]{1,0:T(8,128)(2,1)S(1)}, bf16[768,128]{1,0:T(8,128)(2,1)S(1)}, u32[]{:S(2)}, u32[]{:S(2)}) collective-permute-start(bf16[768,128]{1,0:T(8,128)(2,1)S(1)} %collective-permute-done), channel_id=1, source_target_pairs={{0,8},{8,0},{16,24},{24,16},{32,40},{40,32},{48,56},{56,48},{64,72... | collective-permute-start | bytes 589832 | tf_op jit(solution)/shard_map/ppermute | solution.py:626
  25.7 14.1 %collective-permute-start.8 = (bf16[3072,128]{1,0:T(8,128)(2,1)S(1)}, bf16[3072,128]{1,0:T(8,128)(2,1)S(1)}, u32[]{:S(2)}, u32[]{:S(2)}) collective-permute-start(bf16[3072,128]{1,0:T(8,128)(2,1)S(1)} %pad_maximum_fusion.refs_0_), channel_id=1, source_target_pairs={{0,16},{8,120},{16,32},{24,8},{32,48},{40,24},{48,64},{56,40},{64,... | collective-permute-start | bytes 2359304 | tf_op jit(solution)/shard_map/ppermute | solution.py:623
  30.0 12.4 %collective-permute-start.12 = (bf16[1536,128]{1,0:T(8,128)(2,1)S(1)}, bf16[1536,128]{1,0:T(8,128)(2,1)S(1)}, u32[]{:S(2)}, u32[]{:S(2)}) collective-permute-start(bf16[1536,128]{1,0:T(8,128)(2,1)S(1)} %constant_dynamic-update-slice_fusion.near_ref), channel_id=1, source_target_pairs={{0,3},{1,0},{2,1},{3,2},{4,7},{5,4},{6,5},{7,6},{8,11},{9,8},{10,9... | collective-permute-start | bytes 1179656 | tf_op jit(solution)/shard_map/ppermute | solution.py:643
  33.1 9.4 %collective-permute-start.13 = (bf16[1536,128]{1,0:T(8,128)(2,1)S(1)}, bf16[1536,128]{1,0:T(8,128)(2,1)S(1)}, u32[]{:S(2)}, u32[]{:S(2)}) collective-permute-start(bf16[1536,128]{1,0:T(8,128)(2,1)S(1)} %constant_dynamic-update-slice_fusion.near_ref), channel_id=1, source_target_pairs={{0,1},{1,2},{2,3},{3,0},{4,5},{5,6},{6,7},{7,4},{8,9},{9,10},{10,1... | collective-permute-start | bytes 1179656 | tf_op jit(solution)/shard_map/ppermute | solution.py:644
  36.4 3.5 %collective-permute-start.10 = (f32[16,128]{1,0:T(8,128)S(1)}, f32[16,128]{1,0:T(8,128)S(1)}, u32[]{:S(2)}, u32[]{:S(2)}) collective-permute-start(f32[16,128]{1,0:T(8,128)S(1)} %get-tuple-element.56), channel_id=1, source_target_pairs={{0,248},{8,16},{16,8},{24,32},{32,24},{40,48},{48,40},{56,64},{64,... | collective-permute-start | bytes 24584 | tf_op jit(solution)/shard_map/ppermute | solution.py:606
  36.5 3.4 %collective-permute-start.9 = (f32[16,128]{1,0:T(8,128)S(1)}, f32[16,128]{1,0:T(8,128)S(1)}, u32[]{:S(2)}, u32[]{:S(2)}) collective-permute-start(f32[16,128]{1,0:T(8,128)S(1)} %get-tuple-element.55), channel_id=1, source_target_pairs={{0,8},{8,0},{16,24},{24,16},{32,40},{40,32},{48,56},{56,48},{64,72... | collective-permute-start | bytes 24584 | tf_op jit(solution)/shard_map/ppermute | solution.py:605
  39.9 13.6 %collective-permute-start.11 = (bf16[3072,128]{1,0:T(8,128)(2,1)S(1)}, bf16[3072,128]{1,0:T(8,128)(2,1)S(1)}, u32[]{:S(2)}, u32[]{:S(2)}) collective-permute-start(bf16[3072,128]{1,0:T(8,128)(2,1)S(1)} %collective-permute-done.8.refs_1_), channel_id=1, source_target_pairs={{0,16},{8,120},{16,32},{24,8},{32,48},{40,24},{48,64},{56,40},{64,... | collective-permute-start | bytes 2359304 | tf_op jit(solution)/shard_map/ppermute | solution.py:623
  42.5 11.0 %collective-permute-start.16 = (bf16[1536,128]{1,0:T(8,128)(2,1)S(1)}, bf16[1536,128]{1,0:T(8,128)(2,1)S(1)}, u32[]{:S(2)}, u32[]{:S(2)}) collective-permute-start(bf16[1536,128]{1,0:T(8,128)(2,1)S(1)} %broadcast_select_fusion), channel_id=1, source_target_pairs={{0,1},{1,2},{2,3},{3,0},{4,5},{5,6},{6,7},{7,4},{8,11},{9,8},{10,9... | collective-permute-start | bytes 1179656 | tf_op jit(solution)/shard_map/ppermute | solution.py:651
  45.7 5.2 %collective-permute-start.14 = (f32[16,128]{1,0:T(8,128)S(1)}, f32[16,128]{1,0:T(8,128)S(1)}, u32[]{:S(2)}, u32[]{:S(2)}) collective-permute-start(f32[16,128]{1,0:T(8,128)S(1)} %add_add_fusion), channel_id=1, source_target_pairs={{0,4},{1,5},{2,6},{3,7},{4,0},{5,1},{6,2},{7,3},{8,12},{9,13},{10,... | collective-permute-start | bytes 24584 | tf_op jit(solution)/shard_map/ppermute | solution.py:653
  50.9 2.6 %collective-permute-start.15 = (f32[16,128]{1,0:T(8,128)S(1)}, f32[16,128]{1,0:T(8,128)S(1)}, u32[]{:S(2)}, u32[]{:S(2)}) collective-permute-start(f32[16,128]{1,0:T(8,128)S(1)} %add.21), channel_id=1, source_target_pairs={{0,1},{1,0},{2,3},{3,2},{4,5},{5,4},{6,7},{7,6},{8,9},{9,8},{10,11... | collective-permute-start | bytes 24584 | tf_op jit(solution)/shard_map/ppermute | solution.py:657
  51.0 9.7 %collective-permute-start.19 = (bf16[3072,128]{1,0:T(8,128)(2,1)S(1)}, bf16[3072,128]{1,0:T(8,128)(2,1)S(1)}, u32[]{:S(2)}, u32[]{:S(2)}) collective-permute-start(bf16[3072,128]{1,0:T(8,128)(2,1)S(1)} %collective-permute-done.8.refs_1_), channel_id=1, source_target_pairs={{0,8},{8,0},{16,24},{24,16},{32,40},{40,32},{48,56},{56,48},{64,72... | collective-permute-start | bytes 2359304 | tf_op jit(solution)/shard_map/ppermute | solution.py:626
  53.5 11.8 %collective-permute-start.17 = (bf16[3072,128]{1,0:T(8,128)(2,1)S(1)}, bf16[3072,128]{1,0:T(8,128)(2,1)S(1)}, u32[]{:S(2)}, u32[]{:S(2)}) collective-permute-start(bf16[3072,128]{1,0:T(8,128)(2,1)S(1)} %collective-permute-done.11.refs_0_), channel_id=1, source_target_pairs={{0,16},{8,120},{16,32},{24,8},{32,48},{40,24},{48,64},{56,40},{64,... | collective-permute-start | bytes 2359304 | tf_op jit(solution)/shard_map/ppermute | solution.py:623
  54.7 9.6 %collective-permute-start.18 = (f32[16,128]{1,0:T(8,128)S(1)}, f32[16,128]{1,0:T(8,128)S(1)}, u32[]{:S(2)}, u32[]{:S(2)}) collective-permute-start(f32[16,128]{1,0:T(8,128)S(1)} %add.22), channel_id=1, source_target_pairs={{0,2},{1,3},{2,0},{3,1},{4,6},{5,7},{6,4},{7,5},{8,10},{9,11},{10,... | collective-permute-start | bytes 24584 | tf_op jit(solution)/shard_map/ppermute | solution.py:662
  58.0 10.0 %collective-permute-start.21 = (bf16[3072,128]{1,0:T(8,128)(2,1)S(1)}, bf16[3072,128]{1,0:T(8,128)(2,1)S(1)}, u32[]{:S(2)}, u32[]{:S(2)}) collective-permute-start(bf16[3072,128]{1,0:T(8,128)(2,1)S(1)} %collective-permute-done.11.refs_0_), channel_id=1, source_target_pairs={{0,8},{8,0},{16,24},{24,16},{32,40},{40,32},{48,56},{56,48},{64,72... | collective-permute-start | bytes 2359304 | tf_op jit(solution)/shard_map/ppermute | solution.py:626
  65.3 6.0 %collective-permute-start.22 = (bf16[3072,128]{1,0:T(8,128)(2,1)S(1)}, bf16[3072,128]{1,0:T(8,128)(2,1)S(1)}, u32[]{:S(2)}, u32[]{:S(2)}) collective-permute-start(bf16[3072,128]{1,0:T(8,128)(2,1)S(1)} %collective-permute-done.17.buffer_ref.refs_3_), channel_id=1, source_target_pairs={{0,8},{8,0},{16,24},{24,16},{32,40},{40,32},{48,56},{56,48},{64,72... | collective-permute-start | bytes 2359304 | tf_op jit(solution)/shard_map/ppermute | solution.py:626
  66.1 9.8 %collective-permute-start.20 = (bf16[1536,128]{1,0:T(8,128)(2,1)S(1)}, bf16[1536,128]{1,0:T(8,128)(2,1)S(1)}, u32[]{:S(2)}, u32[]{:S(2)}) collective-permute-start(bf16[1536,128]{1,0:T(8,128)(2,1)S(1)} %shard_map.111), channel_id=1, source_target_pairs={{0,16},{8,120},{16,32},{24,8},{32,48},{40,24},{48,64},{56,40},{64,... | collective-permute-start | bytes 1179656 | tf_op jit(solution)/shard_map/ppermute | solution.py:623
  75.9 1.8 %collective-permute-start.23 = (bf16[1536,128]{1,0:T(8,128)(2,1)S(1)}, bf16[1536,128]{1,0:T(8,128)(2,1)S(1)}, u32[]{:S(2)}, u32[]{:S(2)}) collective-permute-start(bf16[1536,128]{1,0:T(8,128)(2,1)S(1)} %collective-permute-done.20.refs_0_), channel_id=1, source_target_pairs={{0,8},{8,0},{16,24},{24,16},{32,40},{40,32},{48,56},{56,48},{64,72... | collective-permute-start | bytes 1179656 | tf_op jit(solution)/shard_map/ppermute | solution.py:626
